TPU v7x, 32 devices: a whole 2x2x4 slice. The times are simulated.
32 devices in a mesh: grp: 2 (over y), src: 4 (over z), tile: 4 (over x, core).
Axes of the slice: x: 2, y: 2, z: 4, core: 2. Of those that a mesh axis runs over, the one named last changes fastest.
Arguments:
- mask: bfloat16 [4096, 2048], P(('grp', 'tile')), parts along dimension 0, may hold values from -1 to 1
- cotangent: bfloat16 [4096, 2048], P(('grp', 'tile')), parts along dimension 0, may hold values from -6 to 6
- pupil_phase: float32 [64, 64], replicated, may hold values from -3.140625 to 3.140625
- source_weight: float32 [12288], replicated, may hold values from 0.2 to 1
- shift_table: int32 [12288, 2], replicated, may hold values from 0 to 64
- source_ids: int32 [8, 8], P(('grp', 'src')), parts along dimension 0, may hold values from 0 to 12287
- source_count: int32 [8], P(('grp', 'src')), parts along dimension 0, may hold values from 1 to 8, as said below
Outputs:
- grad_mask: float32 [8, 512, 2048], P(('grp', 'tile'), 'src'), parts along dimension 0
There are 2 independent parts, one for each index of `grp`. A program takes and returns all parts, laid end to end along the dimension named above; an argument that names none is the same for every part. Nothing has to cross between parts.
Inputs may be any that keep to these rules, and one draw needn't show every extreme that they name: `source_count`: every src index has at least one used slot, and in every draw some src index uses all 8 slots.
All inputs are finite; a program needn't handle non-finite values.
Results may differ from a plain program's by a relative error of at most 0.008.
Values sent between devices are 32-bit elements; how exact they have to be, the bound alone decides.
No kernel may reach another device: no remote copies, remote signals or barrier semaphores. Data moves between devices by JAX's collectives and lax.ppermute only.
A program may use at most 64 MiB of HBM per device.

v0:
```python
import functools
import math

import jax
import jax.numpy as jnp
import ml_dtypes
import numpy as np
from jax import lax
from jax.experimental import pallas as pl
from jax.experimental.pallas import tpu as pltpu
from jax.sharding import PartitionSpec as P

COLS = 2048
TILE_ROWS = 2048
BAND = 128
PUPIL = 64
SLOTS = 8
GRID = 128
CHUNKS = 4
GROUP = 4
OX, OY, WEIGHT, USED = range(4)
LANES = 128
SUMS = 2 * BAND + GRID
GRANT = 53 * 1024 * 1024

VMEM = pl.BlockSpec(memory_space=pltpu.VMEM)
SMEM = pl.BlockSpec(memory_space=pltpu.SMEM)
HBM = pl.BlockSpec(memory_space=pltpu.HBM)


def waves(positions, freqs, length):
    product = np.multiply.outer(positions, freqs) % length
    angle = product.astype(np.float64) * (2.0 * math.pi / length)
    return np.cos(angle), np.sin(angle)


def lowpass(positions, length):
    freqs = np.arange(1, PUPIL)
    step = length // GRID
    apart = np.arange(GRID)[None, :] * step - positions[:, None]
    product = (apart[:, :, None] * freqs) % length
    return (1.0 + 2.0 * np.cos(product * (2.0 * math.pi / length)).sum(2)) / GRID


def low(array):
    return np.ascontiguousarray(array).astype(ml_dtypes.bfloat16)


@functools.cache
def image_tables(columns, height, n_tile, n_src):
    band = np.arange(BAND) - BAND // 2
    cols = np.arange(columns)
    rows = np.arange(TILE_ROWS)
    cos, sin = waves(cols, band, columns)
    col_table = low(np.concatenate([cos, -sin, lowpass(cols, columns)], 1))
    cos, sin = waves(rows, band, TILE_ROWS)
    row_table = np.concatenate([cos, sin, lowpass(rows, TILE_ROWS)], 1)
    row_table = low(row_table.reshape(n_tile, height, 2 * BAND + GRID).transpose(0, 2, 1))
    portion = height // n_src
    out_table = np.concatenate([cos, -sin], 1).astype(np.float32)
    return col_table, row_table, out_table.reshape(n_tile * n_src, portion, 2 * BAND)


COLS_IN, COLS_OUT = slice(0, 2 * BAND), slice(2 * BAND, 2 * BAND + 2 * GRID)
ROWS_IN = slice(COLS_OUT.stop, COLS_OUT.stop + GRID)
ROWS_OUT = slice(ROWS_IN.stop, ROWS_IN.stop + 2 * PUPIL)
GRID_ROWS = ROWS_OUT.stop


@functools.cache
def grid_tables(columns):
    points = np.arange(GRID)
    band = np.arange(BAND) - BAND // 2
    cos, sin = waves(points, band, GRID)
    cols_in = np.block([[cos.T, sin.T], [-sin.T, cos.T]])
    cols_out = np.block([[cos, -sin], [sin, cos]])
    cos, sin = waves(points, np.arange(PUPIL) - PUPIL // 2, GRID)
    rows_in = np.block([[cos, -sin, sin, cos]])
    rows_out = np.block([[cos.T, sin.T], [-sin.T, cos.T]])
    cos, sin = waves(np.arange(columns), band, columns)
    return low(np.concatenate([cols_in, cols_out, rows_in, rows_out, np.block([cos, -sin])], 0))


def dot(left, right):
    return jnp.dot(left, right, preferred_element_type=jnp.float32)


def forward_kernel(
    mask, cotangent, col_table, row_table,
    partial,
    mask_v, cot_v, col_v, row_v, sems,
):
    height, columns = mask.shape
    width = columns // CHUNKS
    tile = lax.axis_index("tile")
    chunk_copies = []
    for step in range(CHUNKS):
        part = pl.ds(step * width, width)
        copies = [
            pltpu.make_async_copy(col_table.at[part, :], col_v.at[part, :], sems.at[step, 0]),
            pltpu.make_async_copy(mask.at[:, part], mask_v.at[step], sems.at[step, 1]),
            pltpu.make_async_copy(cotangent.at[:, part], cot_v.at[step], sems.at[step, 2]),
        ]
        for copy in copies:
            copy.start()
        chunk_copies.append(copies)
    row_copy = pltpu.make_async_copy(row_table.at[tile], row_v, sems.at[CHUNKS, 0])
    row_copy.start()

    for step in range(CHUNKS):
        for copy in chunk_copies[step]:
            copy.wait()
        part = pl.ds(step * width, width)
        mask_add = dot(mask_v[step], col_v[part, : 2 * BAND])
        cot_add = dot(cot_v[step], col_v[part, 2 * BAND :])
        mask_part = mask_add if step == 0 else mask_part + mask_add
        cot_part = cot_add if step == 0 else cot_part + cot_add

    row_copy.wait()
    blocks = dot(row_v[: 2 * BAND, :], mask_part.astype(jnp.bfloat16))
    partial[:BAND, :] = blocks[:BAND, :BAND] + blocks[BAND:, BAND:]
    partial[BAND : 2 * BAND, :] = blocks[:BAND, BAND:] - blocks[BAND:, :BAND]
    partial[2 * BAND :, :] = dot(row_v[2 * BAND :, :], cot_part.astype(jnp.bfloat16))


def forward(mask, cotangent, col_table, row_table):
    height, columns = mask.shape
    width = columns // CHUNKS
    return pl.pallas_call(
        forward_kernel,
        out_shape=jax.ShapeDtypeStruct((SUMS, BAND), jnp.float32),
        in_specs=[HBM] * 4,
        out_specs=VMEM,
        scratch_shapes=[
            pltpu.VMEM((CHUNKS, height, width), jnp.bfloat16),
            pltpu.VMEM((CHUNKS, height, width), jnp.bfloat16),
            pltpu.VMEM(col_table.shape, jnp.bfloat16),
            pltpu.VMEM(row_table.shape[1:], jnp.bfloat16),
            pltpu.SemaphoreType.DMA((CHUNKS + 1, 3)),
        ],
        compiler_params=pltpu.CompilerParams(vmem_limit_bytes=GRANT),
        cost_estimate=pl.CostEstimate(
            flops=2 * height * columns * SUMS, bytes_accessed=6 * 1024 * 1024, transcendentals=0
        ),
        name="forward",
    )(mask, cotangent, col_table, row_table)


def list_kernel(ids, shift, weight, lines):
    lane = lax.broadcasted_iota(jnp.int32, (SLOTS, LANES), 1)
    place = lax.broadcasted_iota(jnp.int32, (SLOTS, LANES), 0)

    def one(row, carry):
        blocks, weights, there = [], [], jnp.zeros_like(lane)
        for slot in range(SLOTS):
            source = jnp.maximum(ids[row, slot], 0)
            start = pl.multiple_of(source // LANES * LANES, LANES)
            blocks.append(shift[:, pl.ds(start, LANES)])
            weights.append(weight[pl.ds(source // LANES, 1), :])
            there = jnp.where(place == slot, source % LANES, there)
        here = lane == there
        line = jnp.zeros((SLOTS, LANES), jnp.float32)
        for dim, into in ((0, OX), (1, OY)):
            values = jnp.concatenate([block[dim : dim + 1, :] for block in blocks], 0)
            found = jnp.sum(jnp.where(here, values.astype(jnp.float32), 0.0), 1, keepdims=True)
            line = jnp.where(lane == into, found, line)
        found = jnp.sum(jnp.where(here, jnp.concatenate(weights, 0), 0.0), 1, keepdims=True)
        line = jnp.where(lane == WEIGHT, found, line)
        for slot in range(SLOTS):
            used = jnp.where(ids[row, slot] >= 0, 1.0, 0.0)
            line = jnp.where((lane == USED) & (place == slot), used, line)
        lines[pl.ds(pl.multiple_of(row * SLOTS, SLOTS), SLOTS), :] = line
        return carry

    lax.fori_loop(0, ids.shape[0], one, jnp.int32(0), unroll=ids.shape[0] <= 4)


def slot_lines(ids, shift, weight):
    count = ids.size
    return pl.pallas_call(
        list_kernel,
        out_shape=jax.ShapeDtypeStruct((count, LANES), jnp.float32),
        in_specs=[SMEM, VMEM, VMEM],
        out_specs=VMEM,
        name="slot_lines",
    )(ids, shift, weight)


def adjoint_kernel(
    n_src, own, other, lines, pupil, table, out_table,
    result,
    spec, image, band, table_v, out_v, lines_s, list_x, list_y, list_w, sems,
):
    place = lax.axis_index("tile") * n_src + lax.axis_index("src")
    lines_copy = pltpu.make_async_copy(lines, lines_s, sems.at[0])
    small, columns = GRID_ROWS, table.shape[0] - GRID_ROWS
    grid_part, col_part = pl.ds(0, small), pl.ds(small, columns)
    grid_copy = pltpu.make_async_copy(table.at[grid_part, :], table_v.at[grid_part, :], sems.at[1])
    col_copy = pltpu.make_async_copy(table.at[col_part, :], table_v.at[col_part, :], sems.at[2])
    out_copy = pltpu.make_async_copy(out_table.at[place], out_v, sems.at[3])
    for copy in (lines_copy, grid_copy, col_copy, out_copy):
        copy.start()

    scale = 1.0 / math.sqrt(TILE_ROWS * COLS)
    whole = own[...] + other[...]
    spec[...] = (whole[: 2 * BAND] * scale).astype(jnp.bfloat16).astype(jnp.float32)
    image[:GRID, :] = whole[2 * BAND :]
    image[GRID:, :] = whole[2 * BAND :]
    band[...] = jnp.zeros_like(band)

    lines_copy.wait()

    def add(line, total):
        list_x[total] = lines_s[line, OX].astype(jnp.int32)
        list_y[total] = lines_s[line, OY].astype(jnp.int32)
        list_w[total] = lines_s[line, WEIGHT] * (2.0 / SLOTS / PUPIL / PUPIL)
        return total + lines_s[line, USED].astype(jnp.int32)

    count = lines.shape[0]
    total = lax.fori_loop(0, count, add, jnp.int32(0), unroll=count <= 32)
    for slot in range(GROUP):
        list_x[total + slot] = jnp.int32(0)
        list_y[total + slot] = jnp.int32(0)
        list_w[total + slot] = jnp.float32(0.0)
    grid_copy.wait()

    def group(step, carry):
        starts, pupils, amplitudes = [], [], []
        for slot in range(GROUP):
            index = step * GROUP + slot
            offset_x, offset_y = list_x[index], list_y[index]
            real = pltpu.roll(pupil[:PUPIL, :], offset_x, 1)
            imag = pltpu.roll(pupil[PUPIL:, :], offset_x, 1)
            spec_real = spec[pl.ds(offset_y, PUPIL), :]
            spec_imag = spec[pl.ds(BAND + offset_y, PUPIL), :]
            amp_real = real * spec_real - imag * spec_imag
            amp_imag = real * spec_imag + imag * spec_real
            starts.append(offset_y)
            pupils.append((real, imag, list_w[index]))
            amplitudes.append(jnp.concatenate([amp_real, amp_imag], 1).astype(jnp.bfloat16))
        halfway = dot(jnp.concatenate(amplitudes, 0), table_v[COLS_IN, :]).astype(jnp.bfloat16)
        halfway = jnp.concatenate(
            [
                jnp.concatenate(
                    [
                        halfway[slot * PUPIL : (slot + 1) * PUPIL, :GRID],
                        halfway[slot * PUPIL : (slot + 1) * PUPIL, GRID:],
                    ],
                    0,
                )
                for slot in range(GROUP)
            ],
            1,
        )
        rows_in = table_v[ROWS_IN, :]
        rows_in = jnp.concatenate([rows_in[:, : 2 * PUPIL], rows_in[:, 2 * PUPIL :]], 0)
        field = dot(rows_in, halfway)
        field_grad = jnp.concatenate(
            [
                (field[:, slot * GRID : (slot + 1) * GRID] * image[...]).astype(jnp.bfloat16)
                for slot in range(GROUP)
            ],
            1,
        )
        back = dot(table_v[ROWS_OUT, :], field_grad).astype(jnp.bfloat16)
        back = jnp.concatenate(
            [
                jnp.concatenate(
                    [
                        back[:PUPIL, slot * GRID : (slot + 1) * GRID],
                        back[PUPIL:, slot * GRID : (slot + 1) * GRID],
                    ],
                    1,
                )
                for slot in range(GROUP)
            ],
            0,
        )
        grad = dot(back, table_v[COLS_OUT, :])
        for slot in range(GROUP):
            real, imag, factor = pupils[slot]
            grad_real = grad[slot * PUPIL : (slot + 1) * PUPIL, :BAND] * factor
            grad_imag = grad[slot * PUPIL : (slot + 1) * PUPIL, BAND:] * factor
            rows = pl.ds(starts[slot], PUPIL)
            band[rows, :] = band[rows, :] + (real * grad_real + imag * grad_imag)
            rows = pl.ds(BAND + starts[slot], PUPIL)
            band[rows, :] = band[rows, :] + (real * grad_imag - imag * grad_real)
        return carry

    lax.fori_loop(0, (total + GROUP - 1) // GROUP, group, jnp.int32(0))

    col_copy.wait()
    out_copy.wait()
    real = band[:BAND, :] * scale
    imag = band[BAND:, :] * scale
    left = jnp.concatenate(
        [jnp.concatenate([real, imag], 1), jnp.concatenate([imag, -real], 1)], 0
    ).astype(jnp.bfloat16)
    mixed = dot(out_v[...].astype(jnp.bfloat16), left).astype(jnp.bfloat16)
    result[0] = lax.dot_general(
        mixed, table_v[col_part, :], (((1,), (1,)), ((), ())), preferred_element_type=jnp.float32
    )


def adjoint(own, other, lines, pupil, table, out_table, n_src):
    portion = out_table.shape[1]
    columns = table.shape[0] - GRID_ROWS
    places = lines.shape[0] + GROUP
    return pl.pallas_call(
        functools.partial(adjoint_kernel, n_src),
        out_shape=jax.ShapeDtypeStruct((1, portion, columns), jnp.float32),
        in_specs=[VMEM] * 4 + [HBM, HBM],
        out_specs=VMEM,
        scratch_shapes=[
            pltpu.VMEM((2 * BAND, BAND), jnp.float32),
            pltpu.VMEM((2 * GRID, GRID), jnp.float32),
            pltpu.VMEM((2 * BAND, BAND), jnp.float32),
            pltpu.VMEM(table.shape, jnp.bfloat16),
            pltpu.VMEM(out_table.shape[1:], jnp.float32),
            pltpu.SMEM(lines.shape, jnp.float32),
            pltpu.SMEM((places,), jnp.int32),
            pltpu.SMEM((places,), jnp.int32),
            pltpu.SMEM((places,), jnp.float32),
            pltpu.SemaphoreType.DMA((4,)),
        ],
        compiler_params=pltpu.CompilerParams(vmem_limit_bytes=GRANT),
        cost_estimate=pl.CostEstimate(
            flops=2 * 128 * 4096 * 256, bytes_accessed=4 * 1024 * 1024, transcendentals=0
        ),
        name="adjoint",
    )(own, other, lines, pupil, table, out_table)


def pupil_rows(phase):
    grid = jnp.arange(PUPIL, dtype=jnp.int32)
    radius = (2 * grid[:, None] - PUPIL + 1) ** 2 + (2 * grid[None, :] - PUPIL + 1) ** 2
    inside = radius <= PUPIL * PUPIL
    both = jnp.concatenate(
        [jnp.where(inside, jnp.cos(phase), 0.0), jnp.where(inside, jnp.sin(phase), 0.0)], 0
    )
    return jnp.pad(both, ((0, 0), (0, BAND - PUPIL)))


def swapped(array, sizes, steps):
    axes = tuple(sizes)
    places = np.arange(math.prod(sizes.values())).reshape(tuple(sizes.values()))
    there = places
    for dim, axis in enumerate(axes):
        there = np.take(there, np.arange(sizes[axis]) ^ steps.get(axis, 0), dim)
    turn = [(int(a), int(b)) for a, b in zip(places.ravel(), there.ravel())]
    return lax.ppermute(array, axes, turn)


def body(mask, cotangent, pupil_phase, source_weight, shift_table, source_ids, source_count):
    height, columns = mask.shape
    n_tile, n_src = lax.axis_size("tile"), lax.axis_size("src")
    col_table, row_table, out_table = image_tables(columns, height, n_tile, n_src)
    sizes = {"src": n_src, "tile": n_tile}
    used = jnp.arange(SLOTS, dtype=jnp.int32)[None, :] < source_count[0]
    ids = jnp.where(used, source_ids, -1)
    step = 1
    while step < n_src:
        ids = jnp.concatenate([ids, swapped(ids, sizes, {"src": step})], 0)
        step *= 2
    lines = slot_lines(ids, shift_table.T, source_weight.reshape(-1, LANES))
    own = forward(mask, cotangent, col_table, row_table)
    step = 1
    while step < n_tile // 2:
        own = own + swapped(own, sizes, {"tile": step})
        step *= 2
    other = swapped(own, sizes, {"tile": step})
    return adjoint(
        own, other, lines, pupil_rows(pupil_phase), grid_tables(columns), out_table, n_src
    )


def solution(mesh):
    placed = (
        P(("grp", "tile"), None),
        P(("grp", "tile"), None),
        P(),
        P(),
        P(),
        P(("grp", "src"), None),
        P(("grp", "src")),
    )
    return jax.shard_map(
        body, mesh=mesh, in_specs=placed, out_specs=P(("grp", "tile"), "src", None), check_vma=False
    )
```

profile of v0, /device:TPU:0, one launch (start us, length us, event | category | flops | bytes accessed | tf_op | source)
XLA Modules:
  0.0 24.4 jit_solution(16384129801854106701)
XLA Ops:
  0.7 0.7 %compare_select_fusion = s32[1,8]{1,0:T(1,128)S(1)} fusion(s32[1,8]{1,0:T(1,128)} %param.16, s32[]{:T(128)} %bitcast.3), kind=kLoop, calls=%fused_computation.6 | loop fusion | flops 16 | bytes 68 | tf_op jit(solution)/shard_map/jit(_where)/select_n | solution.py:360
  1.3 0.0 copy-start.1
  1.3 3.0 %collective-permute-start.2 = (s32[1,8]{1,0:T(1,128)S(1)}, s32[1,8]{1,0:T(1,128)S(1)}, u32[]{:S(2)}, u32[]{:S(2)}) collective-permute-start(s32[1,8]{1,0:T(1,128)S(1)} %compare_select_fusion), channel_id=1, source_target_pairs={{0,4},{1,5},{2,6},{3,7},{4,0},{5,1},{6,2},{7,3},{8,12},{9,13},{10,... | collective-permute-start | bytes 104 | tf_op jit(solution)/shard_map/ppermute | solution.py:351
  4.3 3.6 %forward.1 = f32[384,128]{1,0:T(8,128)S(1)} custom-call(bf16[512,2048]{1,0:T(8,128)(2,1)} %mask.1, bf16[512,2048]{1,0:T(8,128)(2,1)} %cotangent.1, bf16[2048,384]{1,0:T(8,128)(2,1)} %constant.28.clone.col_table, bf16[4,384,512]{2,1,0:T(8,128)(2,1)} %constant.29.clone.row_table), custom_call_target="tpu_custom_call" | custom-call | flops 805306368 | bytes 6291456 | tf_op jit(solution)/shard_map/forward/pallas_call | solution.py:129
  7.9 0.1 collective-permute-start
  8.0 0.0 copy-done.1
  8.0 0.1 cosine_select_fusion
  8.2 0.0 collective-permute-done.2
  8.2 2.7 %collective-permute-start.3 = (s32[2,8]{1,0:T(2,128)S(1)}, s32[2,8]{1,0:T(2,128)S(1)}, u32[]{:S(2)}, u32[]{:S(2)}) collective-permute-start(s32[2,8]{1,0:T(2,128)S(1)} %pad_add_fusion.1), channel_id=1, source_target_pairs={{0,8},{1,9},{2,10},{3,11},{4,12},{5,13},{6,14},{7,15},{8,0},{9,1},... | collective-permute-start | bytes 200 | tf_op jit(solution)/shard_map/ppermute | solution.py:351
  10.9 0.0 collective-permute-done
  10.9 1.6 %collective-permute-start.1 = (f32[384,128]{1,0:T(8,128)S(1)}, f32[384,128]{1,0:T(8,128)S(1)}, u32[]{:S(2)}, u32[]{:S(2)}) collective-permute-start(f32[384,128]{1,0:T(8,128)S(1)} %add.54.own), channel_id=1, source_target_pairs={{0,2},{1,3},{2,0},{3,1},{4,6},{5,7},{6,4},{7,5},{8,10},{9,11},{10,... | collective-permute-start | bytes 589832 | tf_op jit(solution)/shard_map/ppermute | solution.py:351
  12.5 0.3 %collective-permute-done.3 = s32[2,8]{1,0:T(2,128)S(1)} collective-permute-done((s32[2,8]{1,0:T(2,128)S(1)}, s32[2,8]{1,0:T(2,128)S(1)}, u32[]{:S(2)}, u32[]{:S(2)}) %collective-permute-start.3) | collective-permute-done | bytes 96 | tf_op jit(solution)/shard_map/ppermute | solution.py:351
  12.7 0.6 %pad_add_fusion.ids = s32[4,8]{1,0:T(4,128)} fusion(s32[2,8]{1,0:T(2,128)S(1)} %collective-permute-done.3, s32[1,8]{1,0:T(1,128)S(1)} %collective-permute-done.2, s32[1,8]{1,0:T(1,128)S(1)} %compare_select_fusion), kind=kLoop, calls=%fused_computation.5 | loop fusion | flops 64 | bytes 256 | tf_op jit(solution)/shard_map/concatenate | solution.py:363
  13.3 1.7 %slot_lines.1.lines = f32[32,128]{1,0:T(8,128)} custom-call(s32[4,8]{1,0:T(4,128)} %pad_add_fusion.ids, s32[2,12288]{1,0:T(2,128)} %bitcast.4, f32[96,128]{1,0:T(8,128)} %bitcast.5), custom_call_target="tpu_custom_call" | custom-call | tf_op jit(solution)/shard_map/slot_lines/pallas_call | solution.py:180
  15.1 2.9 %collective-permute-done.1.other = f32[384,128]{1,0:T(8,128)S(1)} collective-permute-done((f32[384,128]{1,0:T(8,128)S(1)}, f32[384,128]{1,0:T(8,128)S(1)}, u32[]{:S(2)}, u32[]{:S(2)}) %collective-permute-start.1) | collective-permute-done | bytes 196640 | tf_op jit(solution)/shard_map/ppermute | solution.py:351
  18.0 0.0 copy-start
  18.0 0.7 %copy-done = f32[32,128]{1,0:T(8,128)S(1)} copy-done((f32[32,128]{1,0:T(8,128)S(1)}, f32[32,128]{1,0:T(8,128)}, u32[]{:S(2)}) %copy-start) | copy-done | bytes 16408
  18.7 5.7 %adjoint.1 = f32[1,128,2048]{2,1,0:T(8,128)} custom-call(f32[384,128]{1,0:T(8,128)S(1)} %add.54.own, f32[384,128]{1,0:T(8,128)S(1)} %collective-permute-done.1.other, f32[32,128]{1,0:T(8,128)S(1)} %copy-done, f32[128,128]{1,0:T(8,128)S(1)} %select_maximum_fusion.pupil, bf16[2816,256]{1,0:T(8,128)(2,1)} %constant.30.clone.table, ...), custom_call_target="tpu_custom_call" | custom-call | flops 268435456 | bytes 4194304 | tf_op jit(solution)/shard_map/adjoint/pallas_call | solution.py:309
  (4 shorter events, 0.0 us)
Async XLA Ops:
  1.3 6.7 %copy-start.1 = (f32[64,64]{1,0:T(8,128)S(1)}, f32[64,64]{1,0:T(8,128)}, u32[]{:S(2)}) copy-start(f32[64,64]{1,0:T(8,128)} %param.13) | copy-start | bytes 49156
  1.3 6.9 %collective-permute-start.2 = (s32[1,8]{1,0:T(1,128)S(1)}, s32[1,8]{1,0:T(1,128)S(1)}, u32[]{:S(2)}, u32[]{:S(2)}) collective-permute-start(s32[1,8]{1,0:T(1,128)S(1)} %compare_select_fusion), channel_id=1, source_target_pairs={{0,4},{1,5},{2,6},{3,7},{4,0},{5,1},{6,2},{7,3},{8,12},{9,13},{10,... | collective-permute-start | bytes 104 | tf_op jit(solution)/shard_map/ppermute | solution.py:351
  7.9 2.9 %collective-permute-start = (f32[384,128]{1,0:T(8,128)S(1)}, f32[384,128]{1,0:T(8,128)S(1)}, u32[]{:S(2)}, u32[]{:S(2)}) collective-permute-start(f32[384,128]{1,0:T(8,128)S(1)} %forward.1), channel_id=1, source_target_pairs={{0,1},{1,0},{2,3},{3,2},{4,5},{5,4},{6,7},{7,6},{8,9},{9,8},{10,11... | collective-permute-start | bytes 589832 | tf_op jit(solution)/shard_map/ppermute | solution.py:351
  8.2 4.5 %collective-permute-start.3 = (s32[2,8]{1,0:T(2,128)S(1)}, s32[2,8]{1,0:T(2,128)S(1)}, u32[]{:S(2)}, u32[]{:S(2)}) collective-permute-start(s32[2,8]{1,0:T(2,128)S(1)} %pad_add_fusion.1), channel_id=1, source_target_pairs={{0,8},{1,9},{2,10},{3,11},{4,12},{5,13},{6,14},{7,15},{8,0},{9,1},... | collective-permute-start | bytes 200 | tf_op jit(solution)/shard_map/ppermute | solution.py:351
  10.9 7.1 %collective-permute-start.1 = (f32[384,128]{1,0:T(8,128)S(1)}, f32[384,128]{1,0:T(8,128)S(1)}, u32[]{:S(2)}, u32[]{:S(2)}) collective-permute-start(f32[384,128]{1,0:T(8,128)S(1)} %add.54.own), channel_id=1, source_target_pairs={{0,2},{1,3},{2,0},{3,1},{4,6},{5,7},{6,4},{7,5},{8,10},{9,11},{10,... | collective-permute-start | bytes 589832 | tf_op jit(solution)/shard_map/ppermute | solution.py:351
  18.0 0.7 %copy-start = (f32[32,128]{1,0:T(8,128)S(1)}, f32[32,128]{1,0:T(8,128)}, u32[]{:S(2)}) copy-start(f32[32,128]{1,0:T(8,128)} %slot_lines.1.lines) | copy-start | bytes 49156
where the time goes:
time: 24.7 us; the launch traced here: 24.4 us
  Pallas kernels  11.1 us (45%)
  starting transfers between devices  7.31 us (30%)
  waiting for transfers between devices  3.15 us (13%)
  other arithmetic  1.44 us (6%)
  local copies, waits for them, and re-layouts  0.72 us (3%)
  between operations  0.72 us (3%)
    ppermute x4, starting transfers between devices, swapped(): return lax.ppermute(array, axes, turn)  7.31 us
    pallas_call x1, Pallas kernels, adjoint(): pl.pallas_call(functools.partial(adjoint_kernel, n_src), out_shape=jax.Sh...  5.73 us
    pallas_call x1, Pallas kernels, forward(): pl.pallas_call(forward_kernel, out_shape=jax.ShapeDtypeStruct((SUMS, BAND...  3.6 us
    ppermute x4, waiting for transfers between devices, swapped(): return lax.ppermute(array, axes, turn)  3.15 us
    pallas_call x1, Pallas kernels, slot_lines(): pl.pallas_call(list_kernel, out_shape=jax.ShapeDtypeStruct((count, LANES)...  1.75 us
    unnamed x4, local copies, waits for them, and re-layouts  0.72 us
    select_n x1, other arithmetic, body(): ids = jnp.where(used, source_ids, -1)  0.66 us
    concatenate x2, other arithmetic, body(): ids = jnp.concatenate([ids, swapped(ids, sizes, {'src': step})], 0)  0.61 us
  transfers between devices with their start and end apart: 4, of which 2 were waited for; matrix products, arithmetic and copies ran while one was open for 3% of the time, Pallas kernels for 22%

commit v1 on v0

--- a/solution.py
+++ b/solution.py
@@ -17,7 +17,7 @@
 SLOTS = 8
 GRID = 128
 CHUNKS = 4
-GROUP = 4
+GROUP = 8
 OX, OY, WEIGHT, USED = range(4)
 LANES = 128
 SUMS = 2 * BAND + GRID
@@ -87,7 +87,7 @@
 
 def forward_kernel(
     mask, cotangent, col_table, row_table,
-    partial,
+    partial, zeros,
     mask_v, cot_v, col_v, row_v, sems,
 ):
     height, columns = mask.shape
@@ -121,6 +121,7 @@
     partial[:BAND, :] = blocks[:BAND, :BAND] + blocks[BAND:, BAND:]
     partial[BAND : 2 * BAND, :] = blocks[:BAND, BAND:] - blocks[BAND:, :BAND]
     partial[2 * BAND :, :] = dot(row_v[2 * BAND :, :], cot_part.astype(jnp.bfloat16))
+    zeros[...] = jnp.zeros_like(zeros)
 
 
 def forward(mask, cotangent, col_table, row_table):
@@ -128,9 +129,12 @@
     width = columns // CHUNKS
     return pl.pallas_call(
         forward_kernel,
-        out_shape=jax.ShapeDtypeStruct((SUMS, BAND), jnp.float32),
+        out_shape=(
+            jax.ShapeDtypeStruct((SUMS, BAND), jnp.float32),
+            jax.ShapeDtypeStruct((1, SLOTS), jnp.int32),
+        ),
         in_specs=[HBM] * 4,
-        out_specs=VMEM,
+        out_specs=(VMEM, VMEM),
         scratch_shapes=[
             pltpu.VMEM((CHUNKS, height, width), jnp.bfloat16),
             pltpu.VMEM((CHUNKS, height, width), jnp.bfloat16),
@@ -182,6 +186,8 @@
         out_shape=jax.ShapeDtypeStruct((count, LANES), jnp.float32),
         in_specs=[SMEM, VMEM, VMEM],
         out_specs=VMEM,
+        compiler_params=pltpu.CompilerParams(vmem_limit_bytes=2 * 1024 * 1024),
+        cost_estimate=pl.CostEstimate(flops=1, bytes_accessed=1, transcendentals=0),
         name="slot_lines",
     )(ids, shift, weight)
 
@@ -356,14 +362,14 @@
     n_tile, n_src = lax.axis_size("tile"), lax.axis_size("src")
     col_table, row_table, out_table = image_tables(columns, height, n_tile, n_src)
     sizes = {"src": n_src, "tile": n_tile}
+    own, zeros = forward(mask, cotangent, col_table, row_table)
     used = jnp.arange(SLOTS, dtype=jnp.int32)[None, :] < source_count[0]
-    ids = jnp.where(used, source_ids, -1)
+    ids = jnp.where(used, source_ids, -1) + zeros
     step = 1
     while step < n_src:
         ids = jnp.concatenate([ids, swapped(ids, sizes, {"src": step})], 0)
         step *= 2
     lines = slot_lines(ids, shift_table.T, source_weight.reshape(-1, LANES))
-    own = forward(mask, cotangent, col_table, row_table)
     step = 1
     while step < n_tile // 2:
         own = own + swapped(own, sizes, {"tile": step})

time: 24.7 us -> 23.3 us (0.943)
  waiting for transfers between devices: 3.15 us -> 4.67 us
  Pallas kernels: 11.1 us -> 9.73 us
  other arithmetic: 1.44 us -> 0.2 us
  local copies, waits for them, and re-layouts: 0.72 us -> 0.02 us
  starting transfers between devices: 7.31 us -> 7.74 us
    ppermute x4, waiting for transfers between devices: 3.15 us -> 4.67 us  [swapped(): return lax.ppermute(array, axes, turn)]
    pallas_call x1, Pallas kernels: 1.75 us -> 0.81 us  [slot_lines(): pl.pallas_call(list_kernel, out_shape=jax.ShapeDtypeStruct((count, LANES)...]
    unnamed x4 -> x8, local copies, waits for them, and re-layouts: 0.72 us -> 0.02 us
    select_n x1 -> x0, other arithmetic: 0.66 us -> none  [body(): ids = jnp.where(used, source_ids, -1)]
    concatenate x2, other arithmetic: 0.61 us -> 0.02 us  [body(): ids = jnp.concatenate([ids, swapped(ids, sizes, {'src': step})], 0)]
    pallas_call x1, Pallas kernels: 5.73 us -> 5.28 us  [adjoint(): pl.pallas_call(functools.partial(adjoint_kernel, n_src), out_shape=jax.Sh...]
    ppermute x4, starting transfers between devices: 7.31 us -> 7.74 us  [swapped(): return lax.ppermute(array, axes, turn)]
  transfers between devices with their start and end apart: 4 -> 4, of which waited for: 2 -> 2; matrix products, arithmetic and copies ran while one was open for 3% -> 1% of each run, Pallas kernels for 22% -> 4%
where the time goes in v1:
time: 23.3 us; the launch traced here: 23.1 us
  Pallas kernels  9.73 us (42%)
  starting transfers between devices  7.74 us (33%)
  waiting for transfers between devices  4.67 us (20%)
  between operations  0.76 us (3%)
    ppermute x4, starting transfers between devices, swapped(): return lax.ppermute(array, axes, turn)  7.74 us
    pallas_call x1, Pallas kernels, adjoint(): pl.pallas_call(functools.partial(adjoint_kernel, n_src), out_shape=jax.Sh...  5.28 us
    ppermute x4, waiting for transfers between devices, swapped(): return lax.ppermute(array, axes, turn)  4.67 us
    pallas_call x1, Pallas kernels, forward(): pl.pallas_call(forward_kernel, out_shape=(jax.ShapeDtypeStruct((SUMS, BAN...  3.63 us
    pallas_call x1, Pallas kernels, slot_lines(): pl.pallas_call(list_kernel, out_shape=jax.ShapeDtypeStruct((count, LANES)...  0.81 us
  transfers between devices with their start and end apart: 4, of which 2 were waited for; matrix products, arithmetic and copies ran while one was open for 1% of the time, Pallas kernels for 4%

profile of v1, /device:TPU:0, one launch (start us, length us, event | category | flops | bytes accessed | tf_op | source)
XLA Modules:
  0.0 23.1 jit_solution(8329661135992233192)
XLA Ops:
  0.7 0.0 copy-start.3
  0.7 0.0 copy-start.2
  0.7 0.0 copy-start
  0.7 0.0 copy-start.1
  0.7 3.6 %forward.1 = (f32[384,128]{1,0:T(8,128)S(1)}, s32[1,8]{1,0:T(1,128)S(1)}) custom-call(bf16[512,2048]{1,0:T(8,128)(2,1)} %mask.1, bf16[512,2048]{1,0:T(8,128)(2,1)} %cotangent.1, bf16[2048,384]{1,0:T(8,128)(2,1)} %constant.28.clone.col_table, bf16[4,384,512]{2,1,0:T(8,128)(2,1)} %constant.29.clone.row_table), custom_call_target="tpu_custom_call" | custom-call | flops 805306368 | bytes 6291456 | tf_op jit(solution)/shard_map/forward/pallas_call | solution.py:130
  4.3 0.0 copy-done.3
  4.4 3.1 %collective-permute-start.2 = (s32[1,8]{1,0:T(1,128)S(1)}, s32[1,8]{1,0:T(1,128)S(1)}, u32[]{:S(2)}, u32[]{:S(2)}) collective-permute-start(s32[1,8]{1,0:T(1,128)S(1)} %fusion), channel_id=1, source_target_pairs={{0,4},{1,5},{2,6},{3,7},{4,0},{5,1},{6,2},{7,3},{8,12},{9,13},{10,... | collective-permute-start | bytes 104 | tf_op jit(solution)/shard_map/ppermute | solution.py:357
  7.4 0.0 collective-permute-start
  7.5 0.0 copy-done.2
  7.5 0.1 cosine_select_fusion
  7.6 1.4 %collective-permute-done.2 = s32[1,8]{1,0:T(1,128)S(1)} collective-permute-done((s32[1,8]{1,0:T(1,128)S(1)}, s32[1,8]{1,0:T(1,128)S(1)}, u32[]{:S(2)}, u32[]{:S(2)}) %collective-permute-start.2) | collective-permute-done | bytes 64 | tf_op jit(solution)/shard_map/ppermute | solution.py:357
  9.0 3.1 %collective-permute-start.3 = (s32[2,8]{1,0:T(2,128)S(1)}, s32[2,8]{1,0:T(2,128)S(1)}, u32[]{:S(2)}, u32[]{:S(2)}) collective-permute-start(s32[2,8]{1,0:T(2,128)S(1)} %pad_add_fusion.1), channel_id=1, source_target_pairs={{0,8},{1,9},{2,10},{3,11},{4,12},{5,13},{6,14},{7,15},{8,0},{9,1},... | collective-permute-start | bytes 200 | tf_op jit(solution)/shard_map/ppermute | solution.py:357
  12.1 0.0 collective-permute-done
  12.1 1.6 %collective-permute-start.1 = (f32[384,128]{1,0:T(8,128)S(1)}, f32[384,128]{1,0:T(8,128)S(1)}, u32[]{:S(2)}, u32[]{:S(2)}) collective-permute-start(f32[384,128]{1,0:T(8,128)S(1)} %add.57.own), channel_id=1, source_target_pairs={{0,2},{1,3},{2,0},{3,1},{4,6},{5,7},{6,4},{7,5},{8,10},{9,11},{10,... | collective-permute-start | bytes 589832 | tf_op jit(solution)/shard_map/ppermute | solution.py:357
  13.7 0.0 collective-permute-done.3
  13.7 0.0 copy-done
  13.7 0.0 copy-done.1
  13.7 0.8 %slot_lines.1.lines = f32[32,128]{1,0:T(8,128)S(1)} custom-call(s32[4,8]{1,0:T(4,128)S(1)} %pad_add_fusion.ids, s32[2,12288]{1,0:T(2,128)S(1)} %bitcast.4, f32[96,128]{1,0:T(8,128)S(1)} %bitcast.5), custom_call_target="tpu_custom_call" | custom-call | flops 1 | bytes 1 | tf_op jit(solution)/shard_map/slot_lines/pallas_call | solution.py:184
  14.5 3.3 %collective-permute-done.1.other = f32[384,128]{1,0:T(8,128)S(1)} collective-permute-done((f32[384,128]{1,0:T(8,128)S(1)}, f32[384,128]{1,0:T(8,128)S(1)}, u32[]{:S(2)}, u32[]{:S(2)}) %collective-permute-start.1) | collective-permute-done | bytes 196640 | tf_op jit(solution)/shard_map/ppermute | solution.py:357
  17.8 5.3 %adjoint.1 = f32[1,128,2048]{2,1,0:T(8,128)} custom-call(f32[384,128]{1,0:T(8,128)S(1)} %add.57.own, f32[384,128]{1,0:T(8,128)S(1)} %collective-permute-done.1.other, f32[32,128]{1,0:T(8,128)S(1)} %slot_lines.1.lines, f32[128,128]{1,0:T(8,128)S(1)} %select_maximum_fusion.pupil, bf16[2816,256]{1,0:T(8,128)(2,1)} %constant.30.clone.table, ...), custom_call_target="tpu_custom_call" | custom-call | flops 268435456 | bytes 4194304 | tf_op jit(solution)/shard_map/adjoint/pallas_call | solution.py:315
  (6 shorter events, 0.1 us)
Async XLA Ops:
  0.7 3.7 %copy-start.3 = (s32[1,8]{1,0:T(1,128)S(1)}, s32[1,8]{1,0:T(1,128)}, u32[]{:S(2)}) copy-start(s32[1,8]{1,0:T(1,128)} %param.16) | copy-start | bytes 100
  0.7 6.8 %copy-start.2 = (f32[64,64]{1,0:T(8,128)S(1)}, f32[64,64]{1,0:T(8,128)}, u32[]{:S(2)}) copy-start(f32[64,64]{1,0:T(8,128)} %param.13) | copy-start | bytes 49156
  0.7 13.0 %copy-start = (s32[12288,2]{0,1:T(2,128)S(1)}, s32[12288,2]{0,1:T(2,128)}, u32[]{:S(2)}) copy-start(s32[12288,2]{0,1:T(2,128)} %param.15) | copy-start | bytes 294916
  0.7 13.0 %copy-start.1 = (f32[12288]{0:T(1024)S(1)}, f32[12288]{0:T(1024)}, u32[]{:S(2)}) copy-start(f32[12288]{0:T(1024)} %param.14) | copy-start | bytes 147460
  4.4 4.6 %collective-permute-start.2 = (s32[1,8]{1,0:T(1,128)S(1)}, s32[1,8]{1,0:T(1,128)S(1)}, u32[]{:S(2)}, u32[]{:S(2)}) collective-permute-start(s32[1,8]{1,0:T(1,128)S(1)} %fusion), channel_id=1, source_target_pairs={{0,4},{1,5},{2,6},{3,7},{4,0},{5,1},{6,2},{7,3},{8,12},{9,13},{10,... | collective-permute-start | bytes 104 | tf_op jit(solution)/shard_map/ppermute | solution.py:357
  7.4 4.6 %collective-permute-start = (f32[384,128]{1,0:T(8,128)S(1)}, f32[384,128]{1,0:T(8,128)S(1)}, u32[]{:S(2)}, u32[]{:S(2)}) collective-permute-start(f32[384,128]{1,0:T(8,128)S(1)} %get-tuple-element.7), channel_id=1, source_target_pairs={{0,1},{1,0},{2,3},{3,2},{4,5},{5,4},{6,7},{7,6},{8,9},{9,8},{10,11... | collective-permute-start | bytes 589832 | tf_op jit(solution)/shard_map/ppermute | solution.py:357
  9.0 4.7 %collective-permute-start.3 = (s32[2,8]{1,0:T(2,128)S(1)}, s32[2,8]{1,0:T(2,128)S(1)}, u32[]{:S(2)}, u32[]{:S(2)}) collective-permute-start(s32[2,8]{1,0:T(2,128)S(1)} %pad_add_fusion.1), channel_id=1, source_target_pairs={{0,8},{1,9},{2,10},{3,11},{4,12},{5,13},{6,14},{7,15},{8,0},{9,1},... | collective-permute-start | bytes 200 | tf_op jit(solution)/shard_map/ppermute | solution.py:357
  12.1 5.7 %collective-permute-start.1 = (f32[384,128]{1,0:T(8,128)S(1)}, f32[384,128]{1,0:T(8,128)S(1)}, u32[]{:S(2)}, u32[]{:S(2)}) collective-permute-start(f32[384,128]{1,0:T(8,128)S(1)} %add.57.own), channel_id=1, source_target_pairs={{0,2},{1,3},{2,0},{3,1},{4,6},{5,7},{6,4},{7,5},{8,10},{9,11},{10,... | collective-permute-start | bytes 589832 | tf_op jit(solution)/shard_map/ppermute | solution.py:357

commit v2 on v1

--- a/solution.py
+++ b/solution.py
@@ -17,8 +17,10 @@
 SLOTS = 8
 GRID = 128
 CHUNKS = 4
-GROUP = 8
+GROUP = 24
 OX, OY, WEIGHT, USED = range(4)
+TOTAL = 2
+PARTS = 4
 LANES = 128
 SUMS = 2 * BAND + GRID
 GRANT = 53 * 1024 * 1024
@@ -58,17 +60,18 @@
     row_table = low(row_table.reshape(n_tile, height, 2 * BAND + GRID).transpose(0, 2, 1))
     portion = height // n_src
     out_table = np.concatenate([cos, -sin], 1).astype(np.float32)
-    return col_table, row_table, out_table.reshape(n_tile * n_src, portion, 2 * BAND)
+    out_table = out_table.reshape(n_tile * n_src, portion, 2 * BAND)
+    cos, sin = waves(cols, band, columns)
+    return col_table, row_table, out_table, low(np.concatenate([cos, -sin], 1).T)
 
 
 COLS_IN, COLS_OUT = slice(0, 2 * BAND), slice(2 * BAND, 2 * BAND + 2 * GRID)
 ROWS_IN = slice(COLS_OUT.stop, COLS_OUT.stop + GRID)
 ROWS_OUT = slice(ROWS_IN.stop, ROWS_IN.stop + 2 * PUPIL)
-GRID_ROWS = ROWS_OUT.stop
 
 
 @functools.cache
-def grid_tables(columns):
+def grid_tables():
     points = np.arange(GRID)
     band = np.arange(BAND) - BAND // 2
     cos, sin = waves(points, band, GRID)
@@ -77,8 +80,7 @@
     cos, sin = waves(points, np.arange(PUPIL) - PUPIL // 2, GRID)
     rows_in = np.block([[cos, -sin, sin, cos]])
     rows_out = np.block([[cos.T, sin.T], [-sin.T, cos.T]])
-    cos, sin = waves(np.arange(columns), band, columns)
-    return low(np.concatenate([cols_in, cols_out, rows_in, rows_out, np.block([cos, -sin])], 0))
+    return low(np.concatenate([cols_in, cols_out, rows_in, rows_out], 0))
 
 
 def dot(left, right):
@@ -150,11 +152,12 @@
     )(mask, cotangent, col_table, row_table)
 
 
-def list_kernel(ids, shift, weight, lines):
+def list_kernel(*refs):
+    *id_parts, shift, weight, offsets, factors, lines, lines_s, sem = refs
     lane = lax.broadcasted_iota(jnp.int32, (SLOTS, LANES), 1)
     place = lax.broadcasted_iota(jnp.int32, (SLOTS, LANES), 0)
 
-    def one(row, carry):
+    def line_block(ids, row):
         blocks, weights, there = [], [], jnp.zeros_like(lane)
         for slot in range(SLOTS):
             source = jnp.maximum(ids[row, slot], 0)
@@ -173,76 +176,97 @@
         for slot in range(SLOTS):
             used = jnp.where(ids[row, slot] >= 0, 1.0, 0.0)
             line = jnp.where((lane == USED) & (place == slot), used, line)
-        lines[pl.ds(pl.multiple_of(row * SLOTS, SLOTS), SLOTS), :] = line
-        return carry
-
-    lax.fori_loop(0, ids.shape[0], one, jnp.int32(0), unroll=ids.shape[0] <= 4)
-
-
-def slot_lines(ids, shift, weight):
-    count = ids.size
+        return line
+
+    first = 0
+    for ids in id_parts:
+        rows = ids.shape[0]
+
+        def one(row, carry, ids=ids, first=first):
+            start = pl.multiple_of((first + row) * SLOTS, SLOTS)
+            lines[pl.ds(start, SLOTS), :] = line_block(ids, row)
+            return carry
+
+        lax.fori_loop(0, rows, one, jnp.int32(0), unroll=rows <= 4)
+        first += rows
+
+    copy = pltpu.make_async_copy(lines, lines_s, sem)
+    copy.start()
+    copy.wait()
+
+    def add(line, total):
+        offsets[OX, total] = lines_s[line, OX].astype(jnp.int32)
+        offsets[OY, total] = lines_s[line, OY].astype(jnp.int32)
+        factors[total] = lines_s[line, WEIGHT] * (2.0 / SLOTS / PUPIL / PUPIL)
+        return total + lines_s[line, USED].astype(jnp.int32)
+
+    count = lines.shape[0]
+    total = lax.fori_loop(0, count, add, jnp.int32(0), unroll=count <= 32)
+    offsets[TOTAL, 0] = total
+    for slot in range(GROUP):
+        offsets[OX, total + slot] = jnp.int32(0)
+        offsets[OY, total + slot] = jnp.int32(0)
+        factors[total + slot] = jnp.float32(0.0)
+
+
+def used_slots(id_parts, shift, weight):
+    count = sum(ids.size for ids in id_parts)
+    places = count + GROUP
     return pl.pallas_call(
         list_kernel,
-        out_shape=jax.ShapeDtypeStruct((count, LANES), jnp.float32),
-        in_specs=[SMEM, VMEM, VMEM],
-        out_specs=VMEM,
+        out_shape=(
+            jax.ShapeDtypeStruct((3, places), jnp.int32),
+            jax.ShapeDtypeStruct((places,), jnp.float32),
+        ),
+        in_specs=[SMEM] * len(id_parts) + [VMEM, VMEM],
+        out_specs=(SMEM, SMEM),
+        scratch_shapes=[
+            pltpu.VMEM((count, LANES), jnp.float32),
+            pltpu.SMEM((count, LANES), jnp.float32),
+            pltpu.SemaphoreType.DMA,
+        ],
         compiler_params=pltpu.CompilerParams(vmem_limit_bytes=2 * 1024 * 1024),
         cost_estimate=pl.CostEstimate(flops=1, bytes_accessed=1, transcendentals=0),
-        name="slot_lines",
-    )(ids, shift, weight)
+        name="used_slots",
+    )(*id_parts, shift, weight)
 
 
 def adjoint_kernel(
-    n_src, own, other, lines, pupil, table, out_table,
+    n_src, own, other, offsets, factors, pupil, table, col_table, out_table,
     result,
-    spec, image, band, table_v, out_v, lines_s, list_x, list_y, list_w, sems,
+    spec_real, spec_imag, image, table_v, col_v, out_v, result_v, sems, out_sems, *bands,
 ):
     place = lax.axis_index("tile") * n_src + lax.axis_index("src")
-    lines_copy = pltpu.make_async_copy(lines, lines_s, sems.at[0])
-    small, columns = GRID_ROWS, table.shape[0] - GRID_ROWS
-    grid_part, col_part = pl.ds(0, small), pl.ds(small, columns)
-    grid_copy = pltpu.make_async_copy(table.at[grid_part, :], table_v.at[grid_part, :], sems.at[1])
-    col_copy = pltpu.make_async_copy(table.at[col_part, :], table_v.at[col_part, :], sems.at[2])
-    out_copy = pltpu.make_async_copy(out_table.at[place], out_v, sems.at[3])
-    for copy in (lines_copy, grid_copy, col_copy, out_copy):
+    grid_copy = pltpu.make_async_copy(table, table_v, sems.at[0])
+    out_copy = pltpu.make_async_copy(out_table.at[place], out_v, sems.at[1])
+    col_copy = pltpu.make_async_copy(col_table, col_v, sems.at[2])
+    for copy in (grid_copy, out_copy, col_copy):
         copy.start()
 
     scale = 1.0 / math.sqrt(TILE_ROWS * COLS)
     whole = own[...] + other[...]
-    spec[...] = (whole[: 2 * BAND] * scale).astype(jnp.bfloat16).astype(jnp.float32)
+    spec = (whole[: 2 * BAND] * scale).astype(jnp.bfloat16).astype(jnp.float32)
+    spec_real[...] = spec[:BAND]
+    spec_imag[...] = spec[BAND:]
     image[:GRID, :] = whole[2 * BAND :]
     image[GRID:, :] = whole[2 * BAND :]
-    band[...] = jnp.zeros_like(band)
-
-    lines_copy.wait()
-
-    def add(line, total):
-        list_x[total] = lines_s[line, OX].astype(jnp.int32)
-        list_y[total] = lines_s[line, OY].astype(jnp.int32)
-        list_w[total] = lines_s[line, WEIGHT] * (2.0 / SLOTS / PUPIL / PUPIL)
-        return total + lines_s[line, USED].astype(jnp.int32)
-
-    count = lines.shape[0]
-    total = lax.fori_loop(0, count, add, jnp.int32(0), unroll=count <= 32)
-    for slot in range(GROUP):
-        list_x[total + slot] = jnp.int32(0)
-        list_y[total + slot] = jnp.int32(0)
-        list_w[total + slot] = jnp.float32(0.0)
+    for band in bands:
+        band[...] = jnp.zeros_like(band)
+    total = offsets[TOTAL, 0]
     grid_copy.wait()
 
     def group(step, carry):
         starts, pupils, amplitudes = [], [], []
         for slot in range(GROUP):
             index = step * GROUP + slot
-            offset_x, offset_y = list_x[index], list_y[index]
+            offset_x, offset_y = offsets[OX, index], offsets[OY, index]
             real = pltpu.roll(pupil[:PUPIL, :], offset_x, 1)
             imag = pltpu.roll(pupil[PUPIL:, :], offset_x, 1)
-            spec_real = spec[pl.ds(offset_y, PUPIL), :]
-            spec_imag = spec[pl.ds(BAND + offset_y, PUPIL), :]
-            amp_real = real * spec_real - imag * spec_imag
-            amp_imag = real * spec_imag + imag * spec_real
+            rows = pl.ds(offset_y, PUPIL)
+            amp_real = real * spec_real[rows, :] - imag * spec_imag[rows, :]
+            amp_imag = real * spec_imag[rows, :] + imag * spec_real[rows, :]
             starts.append(offset_y)
-            pupils.append((real, imag, list_w[index]))
+            pupils.append((real, imag, factors[index]))
             amplitudes.append(jnp.concatenate([amp_real, amp_imag], 1).astype(jnp.bfloat16))
         halfway = dot(jnp.concatenate(amplitudes, 0), table_v[COLS_IN, :]).astype(jnp.bfloat16)
         halfway = jnp.concatenate(
@@ -288,53 +312,65 @@
             grad_real = grad[slot * PUPIL : (slot + 1) * PUPIL, :BAND] * factor
             grad_imag = grad[slot * PUPIL : (slot + 1) * PUPIL, BAND:] * factor
             rows = pl.ds(starts[slot], PUPIL)
-            band[rows, :] = band[rows, :] + (real * grad_real + imag * grad_imag)
-            rows = pl.ds(BAND + starts[slot], PUPIL)
-            band[rows, :] = band[rows, :] + (real * grad_imag - imag * grad_real)
+            band_real, band_imag = bands[slot % 2], bands[2 + slot % 2]
+            band_real[rows, :] = band_real[rows, :] + (real * grad_real + imag * grad_imag)
+            band_imag[rows, :] = band_imag[rows, :] + (real * grad_imag - imag * grad_real)
         return carry
 
     lax.fori_loop(0, (total + GROUP - 1) // GROUP, group, jnp.int32(0))
 
-    col_copy.wait()
-    out_copy.wait()
-    real = band[:BAND, :] * scale
-    imag = band[BAND:, :] * scale
+    real = (bands[0][...] + bands[1][...]) * scale
+    imag = (bands[2][...] + bands[3][...]) * scale
     left = jnp.concatenate(
         [jnp.concatenate([real, imag], 1), jnp.concatenate([imag, -real], 1)], 0
     ).astype(jnp.bfloat16)
+    out_copy.wait()
     mixed = dot(out_v[...].astype(jnp.bfloat16), left).astype(jnp.bfloat16)
-    result[0] = lax.dot_general(
-        mixed, table_v[col_part, :], (((1,), (1,)), ((), ())), preferred_element_type=jnp.float32
-    )
-
-
-def adjoint(own, other, lines, pupil, table, out_table, n_src):
+    col_copy.wait()
+    width = result.shape[2] // PARTS
+    copies = []
+    for step in range(PARTS):
+        part = pl.ds(step * width, width)
+        result_v[:, part] = dot(mixed, col_v[:, part])
+        copy = pltpu.make_async_copy(
+            result_v.at[:, part], result.at[0, :, part], out_sems.at[step]
+        )
+        copy.start()
+        copies.append(copy)
+    for copy in copies:
+        copy.wait()
+
+
+def adjoint(own, other, offsets, factors, pupil, table, col_table, out_table, n_src):
     portion = out_table.shape[1]
-    columns = table.shape[0] - GRID_ROWS
-    places = lines.shape[0] + GROUP
+    columns = col_table.shape[1]
+    band = pltpu.VMEM((BAND, BAND), jnp.float32)
     return pl.pallas_call(
         functools.partial(adjoint_kernel, n_src),
         out_shape=jax.ShapeDtypeStruct((1, portion, columns), jnp.float32),
-        in_specs=[VMEM] * 4 + [HBM, HBM],
-        out_specs=VMEM,
+        in_specs=[VMEM, VMEM, SMEM, SMEM, VMEM, HBM, HBM, HBM],
+        out_specs=HBM,
         scratch_shapes=[
-            pltpu.VMEM((2 * BAND, BAND), jnp.float32),
+            band,
+            band,
             pltpu.VMEM((2 * GRID, GRID), jnp.float32),
-            pltpu.VMEM((2 * BAND, BAND), jnp.float32),
             pltpu.VMEM(table.shape, jnp.bfloat16),
+            pltpu.VMEM(col_table.shape, jnp.bfloat16),
             pltpu.VMEM(out_table.shape[1:], jnp.float32),
-            pltpu.SMEM(lines.shape, jnp.float32),
-            pltpu.SMEM((places,), jnp.int32),
-            pltpu.SMEM((places,), jnp.int32),
-            pltpu.SMEM((places,), jnp.float32),
-            pltpu.SemaphoreType.DMA((4,)),
+            pltpu.VMEM((portion, columns), jnp.float32),
+            pltpu.SemaphoreType.DMA((3,)),
+            pltpu.SemaphoreType.DMA((PARTS,)),
+            band,
+            band,
+            band,
+            band,
         ],
         compiler_params=pltpu.CompilerParams(vmem_limit_bytes=GRANT),
         cost_estimate=pl.CostEstimate(
             flops=2 * 128 * 4096 * 256, bytes_accessed=4 * 1024 * 1024, transcendentals=0
         ),
         name="adjoint",
-    )(own, other, lines, pupil, table, out_table)
+    )(own, other, offsets, factors, pupil, table, col_table, out_table)
 
 
 def pupil_rows(phase):
@@ -360,24 +396,27 @@
 def body(mask, cotangent, pupil_phase, source_weight, shift_table, source_ids, source_count):
     height, columns = mask.shape
     n_tile, n_src = lax.axis_size("tile"), lax.axis_size("src")
-    col_table, row_table, out_table = image_tables(columns, height, n_tile, n_src)
+    col_table, row_table, out_table, out_cols = image_tables(columns, height, n_tile, n_src)
     sizes = {"src": n_src, "tile": n_tile}
     own, zeros = forward(mask, cotangent, col_table, row_table)
     used = jnp.arange(SLOTS, dtype=jnp.int32)[None, :] < source_count[0]
     ids = jnp.where(used, source_ids, -1) + zeros
+    id_parts = (ids,)
     step = 1
     while step < n_src:
-        ids = jnp.concatenate([ids, swapped(ids, sizes, {"src": step})], 0)
+        ids = jnp.concatenate(id_parts, 0) if len(id_parts) > 1 else ids
+        id_parts = (ids, swapped(ids, sizes, {"src": step}))
         step *= 2
-    lines = slot_lines(ids, shift_table.T, source_weight.reshape(-1, LANES))
+    offsets, factors = used_slots(
+        id_parts, shift_table.T, source_weight.reshape(-1, LANES)
+    )
     step = 1
     while step < n_tile // 2:
         own = own + swapped(own, sizes, {"tile": step})
         step *= 2
     other = swapped(own, sizes, {"tile": step})
-    return adjoint(
-        own, other, lines, pupil_rows(pupil_phase), grid_tables(columns), out_table, n_src
-    )
+    pupil = pupil_rows(pupil_phase)
+    return adjoint(own, other, offsets, factors, pupil, grid_tables(), out_cols, out_table, n_src)
 
 
 def solution(mesh):

time: 23.3 us -> 21.6 us (0.927)
  waiting for transfers between devices: 4.67 us -> 3.16 us
  starting transfers between devices: 7.74 us -> 7.3 us
  Pallas kernels: 9.73 us -> 9.97 us
    pallas_call x1, Pallas kernels: 0.81 us -> 2.58 us  [used_slots(): pl.pallas_call(list_kernel, out_shape=(jax.ShapeDtypeStruct((3, places),...]
    pallas_call x1, Pallas kernels: 5.28 us -> 3.75 us  [adjoint(): pl.pallas_call(functools.partial(adjoint_kernel, n_src), out_shape=jax.Sh...]
    ppermute x4, waiting for transfers between devices: 4.67 us -> 3.16 us  [swapped(): return lax.ppermute(array, axes, turn)]
    ppermute x4, starting transfers between devices: 7.74 us -> 7.3 us  [swapped(): return lax.ppermute(array, axes, turn)]
  transfers between devices with their start and end apart: 4 -> 4, of which waited for: 2 -> 2; matrix products, arithmetic and copies ran while one was open for 1% -> 1% of each run, Pallas kernels for 4% -> 12%
where the time goes in v2:
time: 21.6 us; the launch traced here: 21.4 us
  Pallas kernels  9.97 us (46%)
  starting transfers between devices  7.3 us (34%)
  waiting for transfers between devices  3.16 us (15%)
  between operations  0.76 us (4%)
    ppermute x4, starting transfers between devices, swapped(): return lax.ppermute(array, axes, turn)  7.3 us
    pallas_call x1, Pallas kernels, adjoint(): pl.pallas_call(functools.partial(adjoint_kernel, n_src), out_shape=jax.Sh...  3.75 us
    pallas_call x1, Pallas kernels, forward(): pl.pallas_call(forward_kernel, out_shape=(jax.ShapeDtypeStruct((SUMS, BAN...  3.64 us
    ppermute x4, waiting for transfers between devices, swapped(): return lax.ppermute(array, axes, turn)  3.16 us
    pallas_call x1, Pallas kernels, used_slots(): pl.pallas_call(list_kernel, out_shape=(jax.ShapeDtypeStruct((3, places),...  2.58 us
  transfers between devices with their start and end apart: 4, of which 2 were waited for; matrix products, arithmetic and copies ran while one was open for 1% of the time, Pallas kernels for 12%

profile of v2, /device:TPU:0, one launch (start us, length us, event | category | flops | bytes accessed | tf_op | source)
XLA Modules:
  0.0 21.4 jit_solution(14990570387231897327)
XLA Ops:
  0.7 0.0 copy-start.4
  0.7 0.0 copy-start.3
  0.7 0.0 copy-start.1
  0.7 0.0 copy-start.2
  0.7 0.0 copy-start
  0.7 3.6 %forward.1 = (f32[384,128]{1,0:T(8,128)S(1)}, s32[1,8]{1,0:T(1,128)S(1)}) custom-call(bf16[512,2048]{1,0:T(8,128)(2,1)} %mask.1, bf16[512,2048]{1,0:T(8,128)(2,1)} %cotangent.1, bf16[2048,384]{1,0:T(8,128)(2,1)} %constant.30.clone.col_table, bf16[4,384,512]{2,1,0:T(8,128)(2,1)} %constant.31.clone.row_table), custom_call_target="tpu_custom_call" | custom-call | flops 805306368 | bytes 6291456 | tf_op jit(solution)/shard_map/forward/pallas_call | solution.py:132
  4.4 0.0 copy-done.4
  4.4 3.1 %collective-permute-start.2 = (s32[1,8]{1,0:T(1,128)S(1)}, s32[1,8]{1,0:T(1,128)S(1)}, u32[]{:S(2)}, u32[]{:S(2)}) collective-permute-start(s32[1,8]{1,0:T(1,128)S(1)} %fusion), channel_id=1, source_target_pairs={{0,4},{1,5},{2,6},{3,7},{4,0},{5,1},{6,2},{7,3},{8,12},{9,13},{10,... | collective-permute-start | bytes 104 | tf_op jit(solution)/shard_map/ppermute | solution.py:393
  7.5 0.0 collective-permute-start
  7.5 0.0 copy-done.3
  7.5 0.1 cosine_select_fusion
  7.6 1.3 %collective-permute-done = f32[384,128]{1,0:T(8,128)S(1)} collective-permute-done((f32[384,128]{1,0:T(8,128)S(1)}, f32[384,128]{1,0:T(8,128)S(1)}, u32[]{:S(2)}, u32[]{:S(2)}) %collective-permute-start) | collective-permute-done | bytes 196640 | tf_op jit(solution)/shard_map/ppermute | solution.py:393
  8.9 1.6 %collective-permute-start.1 = (f32[384,128]{1,0:T(8,128)S(1)}, f32[384,128]{1,0:T(8,128)S(1)}, u32[]{:S(2)}, u32[]{:S(2)}) collective-permute-start(f32[384,128]{1,0:T(8,128)S(1)} %add.57.own), channel_id=1, source_target_pairs={{0,2},{1,3},{2,0},{3,1},{4,6},{5,7},{6,4},{7,5},{8,10},{9,11},{10,... | collective-permute-start | bytes 589832 | tf_op jit(solution)/shard_map/ppermute | solution.py:393
  10.5 0.0 collective-permute-done.2
  10.5 2.7 %collective-permute-start.3 = (s32[2,8]{1,0:T(2,128)S(1)}, s32[2,8]{1,0:T(2,128)S(1)}, u32[]{:S(2)}, u32[]{:S(2)}) collective-permute-start(s32[2,8]{1,0:T(2,128)S(1)} %pad_add_fusion.refs_0_), channel_id=1, source_target_pairs={{0,8},{1,9},{2,10},{3,11},{4,12},{5,13},{6,14},{7,15},{8,0},{9,1},... | collective-permute-start | bytes 200 | tf_op jit(solution)/shard_map/ppermute | solution.py:393
  13.2 1.9 %collective-permute-done.3.refs_1_ = s32[2,8]{1,0:T(2,128)S(1)} collective-permute-done((s32[2,8]{1,0:T(2,128)S(1)}, s32[2,8]{1,0:T(2,128)S(1)}, u32[]{:S(2)}, u32[]{:S(2)}) %collective-permute-start.3) | collective-permute-done | bytes 96 | tf_op jit(solution)/shard_map/ppermute | solution.py:393
  15.0 0.0 copy-done.1
  15.0 0.0 copy-done.2
  15.1 2.6 %used_slots.1 = (s32[3,56]{1,0:T(4,128)S(1)}, f32[56]{0:T(128)S(1)}) custom-call(s32[2,8]{1,0:T(2,128)S(1)} %pad_add_fusion.refs_0_, s32[2,8]{1,0:T(2,128)S(1)} %collective-permute-done.3.refs_1_, s32[2,12288]{1,0:T(2,128)S(1)} %bitcast.4, f32[96,128]{1,0:T(8,128)S(1)} %bitcast.5), custom_call_target="tpu_custom_call" | custom-call | flops 1 | bytes 1 | tf_op jit(solution)/shard_map/used_slots/pallas_call | solution.py:215
  17.6 0.0 collective-permute-done.1.other
  17.6 0.0 copy-done
  17.7 3.8 %adjoint.1 = f32[1,128,2048]{2,1,0:T(8,128)} custom-call(f32[384,128]{1,0:T(8,128)S(1)} %add.57.own, f32[384,128]{1,0:T(8,128)S(1)} %collective-permute-done.1.other, s32[3,56]{1,0:T(4,128)S(1)} %get-tuple-element.11.offsets, f32[56]{0:T(128)S(1)} %get-tuple-element.12.factors, f32[128,128]{1,0:T(8,128)S(1)} %select_maximum_fusion.pupil, ...), custom_call_target="tpu_custom_call" | custom-call | flops 268435456 | bytes 4194304 | tf_op jit(solution)/shard_map/adjoint/pallas_call | solution.py:348
  (5 shorter events, 0.1 us)
Async XLA Ops:
  0.7 3.7 %copy-start.4 = (s32[1,8]{1,0:T(1,128)S(1)}, s32[1,8]{1,0:T(1,128)}, u32[]{:S(2)}) copy-start(s32[1,8]{1,0:T(1,128)} %param.17) | copy-start | bytes 100
  0.7 6.8 %copy-start.3 = (f32[64,64]{1,0:T(8,128)S(1)}, f32[64,64]{1,0:T(8,128)}, u32[]{:S(2)}) copy-start(f32[64,64]{1,0:T(8,128)} %param.14) | copy-start | bytes 49156
  0.7 14.4 %copy-start.1 = (s32[12288,2]{0,1:T(2,128)S(1)}, s32[12288,2]{0,1:T(2,128)}, u32[]{:S(2)}) copy-start(s32[12288,2]{0,1:T(2,128)} %param.16) | copy-start | bytes 294916
  0.7 14.4 %copy-start.2 = (f32[12288]{0:T(1024)S(1)}, f32[12288]{0:T(1024)}, u32[]{:S(2)}) copy-start(f32[12288]{0:T(1024)} %param.15) | copy-start | bytes 147460
  0.7 17.0 %copy-start = (bf16[768,256]{1,0:T(8,128)(2,1)S(1)}, bf16[768,256]{1,0:T(8,128)(2,1)}, u32[]{:S(2)}) copy-start(bf16[768,256]{1,0:T(8,128)(2,1)} %constant.32.clone.table) | copy-start | bytes 1179652
  4.4 6.1 %collective-permute-start.2 = (s32[1,8]{1,0:T(1,128)S(1)}, s32[1,8]{1,0:T(1,128)S(1)}, u32[]{:S(2)}, u32[]{:S(2)}) collective-permute-start(s32[1,8]{1,0:T(1,128)S(1)} %fusion), channel_id=1, source_target_pairs={{0,4},{1,5},{2,6},{3,7},{4,0},{5,1},{6,2},{7,3},{8,12},{9,13},{10,... | collective-permute-start | bytes 104 | tf_op jit(solution)/shard_map/ppermute | solution.py:393
  7.5 1.4 %collective-permute-start = (f32[384,128]{1,0:T(8,128)S(1)}, f32[384,128]{1,0:T(8,128)S(1)}, u32[]{:S(2)}, u32[]{:S(2)}) collective-permute-start(f32[384,128]{1,0:T(8,128)S(1)} %get-tuple-element.9), channel_id=1, source_target_pairs={{0,1},{1,0},{2,3},{3,2},{4,5},{5,4},{6,7},{7,6},{8,9},{9,8},{10,11... | collective-permute-start | bytes 589832 | tf_op jit(solution)/shard_map/ppermute | solution.py:393
  8.9 8.7 %collective-permute-start.1 = (f32[384,128]{1,0:T(8,128)S(1)}, f32[384,128]{1,0:T(8,128)S(1)}, u32[]{:S(2)}, u32[]{:S(2)}) collective-permute-start(f32[384,128]{1,0:T(8,128)S(1)} %add.57.own), channel_id=1, source_target_pairs={{0,2},{1,3},{2,0},{3,1},{4,6},{5,7},{6,4},{7,5},{8,10},{9,11},{10,... | collective-permute-start | bytes 589832 | tf_op jit(solution)/shard_map/ppermute | solution.py:393
  10.5 4.5 %collective-permute-start.3 = (s32[2,8]{1,0:T(2,128)S(1)}, s32[2,8]{1,0:T(2,128)S(1)}, u32[]{:S(2)}, u32[]{:S(2)}) collective-permute-start(s32[2,8]{1,0:T(2,128)S(1)} %pad_add_fusion.refs_0_), channel_id=1, source_target_pairs={{0,8},{1,9},{2,10},{3,11},{4,12},{5,13},{6,14},{7,15},{8,0},{9,1},... | collective-permute-start | bytes 200 | tf_op jit(solution)/shard_map/ppermute | solution.py:393

commit v3 on v2

--- a/solution.py
+++ b/solution.py
@@ -17,9 +17,8 @@
 SLOTS = 8
 GRID = 128
 CHUNKS = 4
-GROUP = 24
-OX, OY, WEIGHT, USED = range(4)
-TOTAL = 2
+GROUP = 32
+OX, OY, FACTOR = range(3)
 PARTS = 4
 LANES = 128
 SUMS = 2 * BAND + GRID
@@ -152,19 +151,19 @@
     )(mask, cotangent, col_table, row_table)
 
 
-def list_kernel(*refs):
-    *id_parts, shift, weight, offsets, factors, lines, lines_s, sem = refs
+def lines_kernel(ids, shift, weight, lines):
     lane = lax.broadcasted_iota(jnp.int32, (SLOTS, LANES), 1)
     place = lax.broadcasted_iota(jnp.int32, (SLOTS, LANES), 0)
 
-    def line_block(ids, row):
-        blocks, weights, there = [], [], jnp.zeros_like(lane)
+    def one(row, carry):
+        blocks, weights, there = [], [], jnp.full_like(lane, -1)
         for slot in range(SLOTS):
             source = jnp.maximum(ids[row, slot], 0)
             start = pl.multiple_of(source // LANES * LANES, LANES)
             blocks.append(shift[:, pl.ds(start, LANES)])
             weights.append(weight[pl.ds(source // LANES, 1), :])
-            there = jnp.where(place == slot, source % LANES, there)
+            found = jnp.where(ids[row, slot] >= 0, source % LANES, -1)
+            there = jnp.where(place == slot, found, there)
         here = lane == there
         line = jnp.zeros((SLOTS, LANES), jnp.float32)
         for dim, into in ((0, OX), (1, OY)):
@@ -172,75 +171,38 @@
             found = jnp.sum(jnp.where(here, values.astype(jnp.float32), 0.0), 1, keepdims=True)
             line = jnp.where(lane == into, found, line)
         found = jnp.sum(jnp.where(here, jnp.concatenate(weights, 0), 0.0), 1, keepdims=True)
-        line = jnp.where(lane == WEIGHT, found, line)
-        for slot in range(SLOTS):
-            used = jnp.where(ids[row, slot] >= 0, 1.0, 0.0)
-            line = jnp.where((lane == USED) & (place == slot), used, line)
-        return line
-
-    first = 0
-    for ids in id_parts:
-        rows = ids.shape[0]
-
-        def one(row, carry, ids=ids, first=first):
-            start = pl.multiple_of((first + row) * SLOTS, SLOTS)
-            lines[pl.ds(start, SLOTS), :] = line_block(ids, row)
-            return carry
-
-        lax.fori_loop(0, rows, one, jnp.int32(0), unroll=rows <= 4)
-        first += rows
-
-    copy = pltpu.make_async_copy(lines, lines_s, sem)
-    copy.start()
-    copy.wait()
-
-    def add(line, total):
-        offsets[OX, total] = lines_s[line, OX].astype(jnp.int32)
-        offsets[OY, total] = lines_s[line, OY].astype(jnp.int32)
-        factors[total] = lines_s[line, WEIGHT] * (2.0 / SLOTS / PUPIL / PUPIL)
-        return total + lines_s[line, USED].astype(jnp.int32)
-
-    count = lines.shape[0]
-    total = lax.fori_loop(0, count, add, jnp.int32(0), unroll=count <= 32)
-    offsets[TOTAL, 0] = total
-    for slot in range(GROUP):
-        offsets[OX, total + slot] = jnp.int32(0)
-        offsets[OY, total + slot] = jnp.int32(0)
-        factors[total + slot] = jnp.float32(0.0)
-
-
-def used_slots(id_parts, shift, weight):
-    count = sum(ids.size for ids in id_parts)
-    places = count + GROUP
+        line = jnp.where(lane == FACTOR, found * (2.0 / SLOTS / PUPIL / PUPIL), line)
+        lines[pl.ds(pl.multiple_of(row * SLOTS, SLOTS), SLOTS), :] = line
+        return carry
+
+    lax.fori_loop(0, ids.shape[0], one, jnp.int32(0), unroll=ids.shape[0] <= 4)
+
+
+def slot_lines(ids, shift, weight):
     return pl.pallas_call(
-        list_kernel,
-        out_shape=(
-            jax.ShapeDtypeStruct((3, places), jnp.int32),
-            jax.ShapeDtypeStruct((places,), jnp.float32),
-        ),
-        in_specs=[SMEM] * len(id_parts) + [VMEM, VMEM],
-        out_specs=(SMEM, SMEM),
-        scratch_shapes=[
-            pltpu.VMEM((count, LANES), jnp.float32),
-            pltpu.SMEM((count, LANES), jnp.float32),
-            pltpu.SemaphoreType.DMA,
-        ],
+        lines_kernel,
+        out_shape=jax.ShapeDtypeStruct((ids.size, LANES), jnp.float32),
+        in_specs=[SMEM, VMEM, VMEM],
+        out_specs=VMEM,
         compiler_params=pltpu.CompilerParams(vmem_limit_bytes=2 * 1024 * 1024),
         cost_estimate=pl.CostEstimate(flops=1, bytes_accessed=1, transcendentals=0),
-        name="used_slots",
-    )(*id_parts, shift, weight)
+        name="slot_lines",
+    )(ids, shift, weight)
 
 
 def adjoint_kernel(
-    n_src, own, other, offsets, factors, pupil, table, col_table, out_table,
+    n_src, own, other, own_lines, other_lines, pupil, table, col_table, out_table,
     result,
-    spec_real, spec_imag, image, table_v, col_v, out_v, result_v, sems, out_sems, *bands,
+    spec_real, spec_imag, image, table_v, col_v, out_v, result_v, lines, sems, out_sems, *bands,
 ):
     place = lax.axis_index("tile") * n_src + lax.axis_index("src")
     grid_copy = pltpu.make_async_copy(table, table_v, sems.at[0])
     out_copy = pltpu.make_async_copy(out_table.at[place], out_v, sems.at[1])
     col_copy = pltpu.make_async_copy(col_table, col_v, sems.at[2])
-    for copy in (grid_copy, out_copy, col_copy):
+    half = own_lines.shape[0]
+    own_copy = pltpu.make_async_copy(own_lines, lines.at[pl.ds(0, half), :], sems.at[3])
+    other_copy = pltpu.make_async_copy(other_lines, lines.at[pl.ds(half, half), :], sems.at[4])
+    for copy in (own_copy, other_copy, grid_copy, out_copy, col_copy):
         copy.start()
 
     scale = 1.0 / math.sqrt(TILE_ROWS * COLS)
@@ -252,21 +214,23 @@
     image[GRID:, :] = whole[2 * BAND :]
     for band in bands:
         band[...] = jnp.zeros_like(band)
-    total = offsets[TOTAL, 0]
+    own_copy.wait()
+    other_copy.wait()
     grid_copy.wait()
 
     def group(step, carry):
         starts, pupils, amplitudes = [], [], []
         for slot in range(GROUP):
             index = step * GROUP + slot
-            offset_x, offset_y = offsets[OX, index], offsets[OY, index]
+            offset_x = lines[index, OX].astype(jnp.int32)
+            offset_y = lines[index, OY].astype(jnp.int32)
             real = pltpu.roll(pupil[:PUPIL, :], offset_x, 1)
             imag = pltpu.roll(pupil[PUPIL:, :], offset_x, 1)
             rows = pl.ds(offset_y, PUPIL)
             amp_real = real * spec_real[rows, :] - imag * spec_imag[rows, :]
             amp_imag = real * spec_imag[rows, :] + imag * spec_real[rows, :]
             starts.append(offset_y)
-            pupils.append((real, imag, factors[index]))
+            pupils.append((real, imag, lines[index, FACTOR]))
             amplitudes.append(jnp.concatenate([amp_real, amp_imag], 1).astype(jnp.bfloat16))
         halfway = dot(jnp.concatenate(amplitudes, 0), table_v[COLS_IN, :]).astype(jnp.bfloat16)
         halfway = jnp.concatenate(
@@ -317,7 +281,7 @@
             band_imag[rows, :] = band_imag[rows, :] + (real * grad_imag - imag * grad_real)
         return carry
 
-    lax.fori_loop(0, (total + GROUP - 1) // GROUP, group, jnp.int32(0))
+    lax.fori_loop(0, 2 * half // GROUP, group, jnp.int32(0))
 
     real = (bands[0][...] + bands[1][...]) * scale
     imag = (bands[2][...] + bands[3][...]) * scale
@@ -341,14 +305,14 @@
         copy.wait()
 
 
-def adjoint(own, other, offsets, factors, pupil, table, col_table, out_table, n_src):
+def adjoint(own, other, own_lines, other_lines, pupil, table, col_table, out_table, n_src):
     portion = out_table.shape[1]
     columns = col_table.shape[1]
     band = pltpu.VMEM((BAND, BAND), jnp.float32)
     return pl.pallas_call(
         functools.partial(adjoint_kernel, n_src),
         out_shape=jax.ShapeDtypeStruct((1, portion, columns), jnp.float32),
-        in_specs=[VMEM, VMEM, SMEM, SMEM, VMEM, HBM, HBM, HBM],
+        in_specs=[VMEM] * 5 + [HBM] * 3,
         out_specs=HBM,
         scratch_shapes=[
             band,
@@ -358,7 +322,8 @@
             pltpu.VMEM(col_table.shape, jnp.bfloat16),
             pltpu.VMEM(out_table.shape[1:], jnp.float32),
             pltpu.VMEM((portion, columns), jnp.float32),
-            pltpu.SemaphoreType.DMA((3,)),
+            pltpu.SMEM((2 * own_lines.shape[0], LANES), jnp.float32),
+            pltpu.SemaphoreType.DMA((5,)),
             pltpu.SemaphoreType.DMA((PARTS,)),
             band,
             band,
@@ -370,7 +335,7 @@
             flops=2 * 128 * 4096 * 256, bytes_accessed=4 * 1024 * 1024, transcendentals=0
         ),
         name="adjoint",
-    )(own, other, offsets, factors, pupil, table, col_table, out_table)
+    )(own, other, own_lines, other_lines, pupil, table, col_table, out_table)
 
 
 def pupil_rows(phase):
@@ -401,22 +366,21 @@
     own, zeros = forward(mask, cotangent, col_table, row_table)
     used = jnp.arange(SLOTS, dtype=jnp.int32)[None, :] < source_count[0]
     ids = jnp.where(used, source_ids, -1) + zeros
-    id_parts = (ids,)
     step = 1
-    while step < n_src:
-        ids = jnp.concatenate(id_parts, 0) if len(id_parts) > 1 else ids
-        id_parts = (ids, swapped(ids, sizes, {"src": step}))
+    while step < n_src // 2:
+        ids = jnp.concatenate([ids, swapped(ids, sizes, {"src": step})], 0)
         step *= 2
-    offsets, factors = used_slots(
-        id_parts, shift_table.T, source_weight.reshape(-1, LANES)
-    )
+    own_lines = slot_lines(ids, shift_table.T, source_weight.reshape(-1, LANES))
+    other_lines = swapped(own_lines, sizes, {"src": step})
     step = 1
     while step < n_tile // 2:
         own = own + swapped(own, sizes, {"tile": step})
         step *= 2
     other = swapped(own, sizes, {"tile": step})
     pupil = pupil_rows(pupil_phase)
-    return adjoint(own, other, offsets, factors, pupil, grid_tables(), out_cols, out_table, n_src)
+    return adjoint(
+        own, other, own_lines, other_lines, pupil, grid_tables(), out_cols, out_table, n_src
+    )
 
 
 def solution(mesh):

time: 21.6 us -> 20.3 us (0.940)
  Pallas kernels: 9.97 us -> 8.56 us
  waiting for transfers between devices: 3.16 us -> 3.38 us
    pallas_call x1, Pallas kernels: 2.58 us -> 0.71 us  [slot_lines(): pl.pallas_call(lines_kernel, out_shape=jax.ShapeDtypeStruct((ids.size, LA...]
    pallas_call x1, Pallas kernels: 3.75 us -> 4.2 us  [adjoint(): pl.pallas_call(functools.partial(adjoint_kernel, n_src), out_shape=jax.Sh...]
    ppermute x4, waiting for transfers between devices: 3.16 us -> 3.38 us  [swapped(): return lax.ppermute(array, axes, turn)]
  transfers between devices with their start and end apart: 4 -> 4, of which waited for: 2 -> 3; matrix products, arithmetic and copies ran while one was open for 1% -> 1% of each run, Pallas kernels for 12% -> 4%
where the time goes in v3:
time: 20.3 us; the launch traced here: 20.2 us
  Pallas kernels  8.56 us (42%)
  starting transfers between devices  7.26 us (36%)
  waiting for transfers between devices  3.38 us (17%)
  between operations  0.75 us (4%)
    ppermute x4, starting transfers between devices, swapped(): return lax.ppermute(array, axes, turn)  7.26 us
    pallas_call x1, Pallas kernels, adjoint(): pl.pallas_call(functools.partial(adjoint_kernel, n_src), out_shape=jax.Sh...  4.2 us
    pallas_call x1, Pallas kernels, forward(): pl.pallas_call(forward_kernel, out_shape=(jax.ShapeDtypeStruct((SUMS, BAN...  3.64 us
    ppermute x4, waiting for transfers between devices, swapped(): return lax.ppermute(array, axes, turn)  3.38 us
    pallas_call x1, Pallas kernels, slot_lines(): pl.pallas_call(lines_kernel, out_shape=jax.ShapeDtypeStruct((ids.size, LA...  0.71 us
  transfers between devices with their start and end apart: 4, of which 3 were waited for; matrix products, arithmetic and copies ran while one was open for 1% of the time, Pallas kernels for 4%

profile of v3, /device:TPU:0, one launch (start us, length us, event | category | flops | bytes accessed | tf_op | source)
XLA Modules:
  0.0 20.2 jit_solution(12712206300289448694)
XLA Ops:
  0.7 0.0 copy-start.4
  0.7 0.0 copy-start.3
  0.7 0.0 copy-start.1
  0.7 0.0 copy-start.2
  0.7 0.0 copy-start
  0.7 3.6 %forward.1 = (f32[384,128]{1,0:T(8,128)S(1)}, s32[1,8]{1,0:T(1,128)S(1)}) custom-call(bf16[512,2048]{1,0:T(8,128)(2,1)} %mask.1, bf16[512,2048]{1,0:T(8,128)(2,1)} %cotangent.1, bf16[2048,384]{1,0:T(8,128)(2,1)} %constant.30.clone.col_table, bf16[4,384,512]{2,1,0:T(8,128)(2,1)} %constant.31.clone.row_table), custom_call_target="tpu_custom_call" | custom-call | flops 805306368 | bytes 6291456 | tf_op jit(solution)/shard_map/forward/pallas_call | solution.py:131
  4.4 0.0 copy-done.4
  4.4 3.1 %collective-permute-start.2 = (s32[1,8]{1,0:T(1,128)S(1)}, s32[1,8]{1,0:T(1,128)S(1)}, u32[]{:S(2)}, u32[]{:S(2)}) collective-permute-start(s32[1,8]{1,0:T(1,128)S(1)} %fusion), channel_id=1, source_target_pairs={{0,4},{1,5},{2,6},{3,7},{4,0},{5,1},{6,2},{7,3},{8,12},{9,13},{10,... | collective-permute-start | bytes 104 | tf_op jit(solution)/shard_map/ppermute | solution.py:358
  7.5 0.0 collective-permute-start
  7.5 0.0 copy-done.3
  7.5 0.1 cosine_select_fusion
  7.6 1.3 %collective-permute-done = f32[384,128]{1,0:T(8,128)S(1)} collective-permute-done((f32[384,128]{1,0:T(8,128)S(1)}, f32[384,128]{1,0:T(8,128)S(1)}, u32[]{:S(2)}, u32[]{:S(2)}) %collective-permute-start) | collective-permute-done | bytes 196640 | tf_op jit(solution)/shard_map/ppermute | solution.py:358
  8.9 1.6 %collective-permute-start.1 = (f32[384,128]{1,0:T(8,128)S(1)}, f32[384,128]{1,0:T(8,128)S(1)}, u32[]{:S(2)}, u32[]{:S(2)}) collective-permute-start(f32[384,128]{1,0:T(8,128)S(1)} %add.57.own), channel_id=1, source_target_pairs={{0,2},{1,3},{2,0},{3,1},{4,6},{5,7},{6,4},{7,5},{8,10},{9,11},{10,... | collective-permute-start | bytes 589832 | tf_op jit(solution)/shard_map/ppermute | solution.py:358
  10.5 0.0 collective-permute-done.2
  10.5 0.0 copy-done.1
  10.5 0.0 copy-done.2
  10.5 0.7 %slot_lines.1.own_lines = f32[16,128]{1,0:T(8,128)S(1)} custom-call(s32[2,8]{1,0:T(2,128)S(1)} %pad_add_fusion.ids, s32[2,12288]{1,0:T(2,128)S(1)} %bitcast.4, f32[96,128]{1,0:T(8,128)S(1)} %bitcast.5), custom_call_target="tpu_custom_call" | custom-call | flops 1 | bytes 1 | tf_op jit(solution)/shard_map/slot_lines/pallas_call | solution.py:182
  11.2 2.6 %collective-permute-start.3 = (f32[16,128]{1,0:T(8,128)S(1)}, f32[16,128]{1,0:T(8,128)S(1)}, u32[]{:S(2)}, u32[]{:S(2)}) collective-permute-start(f32[16,128]{1,0:T(8,128)S(1)} %slot_lines.1.own_lines), channel_id=1, source_target_pairs={{0,8},{1,9},{2,10},{3,11},{4,12},{5,13},{6,14},{7,15},{8,0},{9,1},... | collective-permute-start | bytes 24584 | tf_op jit(solution)/shard_map/ppermute | solution.py:358
  13.9 2.0 %collective-permute-done.3.other_lines = f32[16,128]{1,0:T(8,128)S(1)} collective-permute-done((f32[16,128]{1,0:T(8,128)S(1)}, f32[16,128]{1,0:T(8,128)S(1)}, u32[]{:S(2)}, u32[]{:S(2)}) %collective-permute-start.3) | collective-permute-done | bytes 8224 | tf_op jit(solution)/shard_map/ppermute | solution.py:358
  15.8 0.1 collective-permute-done.1.other
  16.0 0.0 copy-done
  16.0 4.2 %adjoint.1 = f32[1,128,2048]{2,1,0:T(8,128)} custom-call(f32[384,128]{1,0:T(8,128)S(1)} %add.57.own, f32[384,128]{1,0:T(8,128)S(1)} %collective-permute-done.1.other, f32[16,128]{1,0:T(8,128)S(1)} %slot_lines.1.own_lines, f32[16,128]{1,0:T(8,128)S(1)} %collective-permute-done.3.other_lines, f32[128,128]{1,0:T(8,128)S(1)} %select_maximum_fusion.pupil, ...), custom_call_target="tpu_custom_call" | custom-call | flops 268435456 | bytes 4194304 | tf_op jit(solution)/shard_map/adjoint/pallas_call | solution.py:312
  (5 shorter events, 0.1 us)
Async XLA Ops:
  0.7 3.7 %copy-start.4 = (s32[1,8]{1,0:T(1,128)S(1)}, s32[1,8]{1,0:T(1,128)}, u32[]{:S(2)}) copy-start(s32[1,8]{1,0:T(1,128)} %param.17) | copy-start | bytes 100
  0.7 6.8 %copy-start.3 = (f32[64,64]{1,0:T(8,128)S(1)}, f32[64,64]{1,0:T(8,128)}, u32[]{:S(2)}) copy-start(f32[64,64]{1,0:T(8,128)} %param.14) | copy-start | bytes 49156
  0.7 9.8 %copy-start.1 = (s32[12288,2]{0,1:T(2,128)S(1)}, s32[12288,2]{0,1:T(2,128)}, u32[]{:S(2)}) copy-start(s32[12288,2]{0,1:T(2,128)} %param.16) | copy-start | bytes 294916
  0.7 9.8 %copy-start.2 = (f32[12288]{0:T(1024)S(1)}, f32[12288]{0:T(1024)}, u32[]{:S(2)}) copy-start(f32[12288]{0:T(1024)} %param.15) | copy-start | bytes 147460
  0.7 15.3 %copy-start = (bf16[768,256]{1,0:T(8,128)(2,1)S(1)}, bf16[768,256]{1,0:T(8,128)(2,1)}, u32[]{:S(2)}) copy-start(bf16[768,256]{1,0:T(8,128)(2,1)} %constant.32.clone.table) | copy-start | bytes 1179652
  4.4 6.1 %collective-permute-start.2 = (s32[1,8]{1,0:T(1,128)S(1)}, s32[1,8]{1,0:T(1,128)S(1)}, u32[]{:S(2)}, u32[]{:S(2)}) collective-permute-start(s32[1,8]{1,0:T(1,128)S(1)} %fusion), channel_id=1, source_target_pairs={{0,4},{1,5},{2,6},{3,7},{4,0},{5,1},{6,2},{7,3},{8,12},{9,13},{10,... | collective-permute-start | bytes 104 | tf_op jit(solution)/shard_map/ppermute | solution.py:358
  7.5 1.4 %collective-permute-start = (f32[384,128]{1,0:T(8,128)S(1)}, f32[384,128]{1,0:T(8,128)S(1)}, u32[]{:S(2)}, u32[]{:S(2)}) collective-permute-start(f32[384,128]{1,0:T(8,128)S(1)} %get-tuple-element.7), channel_id=1, source_target_pairs={{0,1},{1,0},{2,3},{3,2},{4,5},{5,4},{6,7},{7,6},{8,9},{9,8},{10,11... | collective-permute-start | bytes 589832 | tf_op jit(solution)/shard_map/ppermute | solution.py:358
  8.9 7.0 %collective-permute-start.1 = (f32[384,128]{1,0:T(8,128)S(1)}, f32[384,128]{1,0:T(8,128)S(1)}, u32[]{:S(2)}, u32[]{:S(2)}) collective-permute-start(f32[384,128]{1,0:T(8,128)S(1)} %add.57.own), channel_id=1, source_target_pairs={{0,2},{1,3},{2,0},{3,1},{4,6},{5,7},{6,4},{7,5},{8,10},{9,11},{10,... | collective-permute-start | bytes 589832 | tf_op jit(solution)/shard_map/ppermute | solution.py:358
  11.2 4.6 %collective-permute-start.3 = (f32[16,128]{1,0:T(8,128)S(1)}, f32[16,128]{1,0:T(8,128)S(1)}, u32[]{:S(2)}, u32[]{:S(2)}) collective-permute-start(f32[16,128]{1,0:T(8,128)S(1)} %slot_lines.1.own_lines), channel_id=1, source_target_pairs={{0,8},{1,9},{2,10},{3,11},{4,12},{5,13},{6,14},{7,15},{8,0},{9,1},... | collective-permute-start | bytes 24584 | tf_op jit(solution)/shard_map/ppermute | solution.py:358

commit v4 on v3

--- a/solution.py
+++ b/solution.py
@@ -366,18 +366,19 @@
     own, zeros = forward(mask, cotangent, col_table, row_table)
     used = jnp.arange(SLOTS, dtype=jnp.int32)[None, :] < source_count[0]
     ids = jnp.where(used, source_ids, -1) + zeros
-    step = 1
-    while step < n_src // 2:
-        ids = jnp.concatenate([ids, swapped(ids, sizes, {"src": step})], 0)
-        step *= 2
-    own_lines = slot_lines(ids, shift_table.T, source_weight.reshape(-1, LANES))
-    other_lines = swapped(own_lines, sizes, {"src": step})
+    bit = 1
+    while bit < n_src // 2:
+        ids = jnp.concatenate([ids, swapped(ids, sizes, {"src": bit})], 0)
+        bit *= 2
     step = 1
     while step < n_tile // 2:
         own = own + swapped(own, sizes, {"tile": step})
         step *= 2
+    zero = own[BAND + BAND // 2, BAND // 2]
+    own_lines = slot_lines(ids + zero.astype(jnp.int32), shift_table.T, source_weight.reshape(-1, LANES))
+    other_lines = swapped(own_lines, sizes, {"src": bit})
     other = swapped(own, sizes, {"tile": step})
-    pupil = pupil_rows(pupil_phase)
+    pupil = pupil_rows(pupil_phase + zero)
     return adjoint(
         own, other, own_lines, other_lines, pupil, grid_tables(), out_cols, out_table, n_src
     )

time: 20.3 us -> 20 us (0.985)
  waiting for transfers between devices: 3.38 us -> 1.16 us
  other arithmetic: 0.19 us -> 0.83 us
  between operations: 0.75 us -> 1.39 us
  local copies, waits for them, and re-layouts: 0.02 us -> 0.6 us
    ppermute x4, waiting for transfers between devices: 3.38 us -> 1.16 us  [swapped(): return lax.ppermute(array, axes, turn)]
    select_n x1, other arithmetic: 0.13 us -> 0.78 us  [pupil_rows(): jnp.where(inside, jnp.cos(phase), 0.0)]
    slice x0 -> x1, local copies, waits for them, and re-layouts: none -> 0.58 us  [body(): zero = own[BAND + BAND // 2, BAND // 2]]
  transfers between devices with their start and end apart: 4 -> 4, of which waited for: 3 -> 1; matrix products, arithmetic and copies ran while one was open for 1% -> 7% of each run, Pallas kernels for 4% -> 4%
where the time goes in v4:
time: 20 us; the launch traced here: 19.8 us
  Pallas kernels  8.54 us (43%)
  starting transfers between devices  7.28 us (36%)
  between operations  1.39 us (7%)
  waiting for transfers between devices  1.16 us (6%)
  other arithmetic  0.83 us (4%)
  local copies, waits for them, and re-layouts  0.6 us (3%)
    ppermute x4, starting transfers between devices, swapped(): return lax.ppermute(array, axes, turn)  7.28 us
    pallas_call x1, Pallas kernels, adjoint(): pl.pallas_call(functools.partial(adjoint_kernel, n_src), out_shape=jax.Sh...  4.19 us
    pallas_call x1, Pallas kernels, forward(): pl.pallas_call(forward_kernel, out_shape=(jax.ShapeDtypeStruct((SUMS, BAN...  3.64 us
    ppermute x4, waiting for transfers between devices, swapped(): return lax.ppermute(array, axes, turn)  1.16 us
    select_n x1, other arithmetic, pupil_rows(): jnp.where(inside, jnp.cos(phase), 0.0)  0.78 us
    pallas_call x1, Pallas kernels, slot_lines(): pl.pallas_call(lines_kernel, out_shape=jax.ShapeDtypeStruct((ids.size, LA...  0.71 us
    slice x1, local copies, waits for them, and re-layouts, body(): zero = own[BAND + BAND // 2, BAND // 2]  0.58 us
  transfers between devices with their start and end apart: 4, of which 1 were waited for; matrix products, arithmetic and copies ran while one was open for 7% of the time, Pallas kernels for 4%

profile of v4, /device:TPU:0, one launch (start us, length us, event | category | flops | bytes accessed | tf_op | source)
XLA Modules:
  0.0 19.8 jit_solution(1287130898846583786)
XLA Ops:
  0.0 0.0 copy-start
  0.0 0.0 copy-start.4
  0.0 0.0 copy-start.1
  0.0 0.0 copy-start.2
  0.0 0.0 copy-start.3
  0.0 3.6 %forward.1 = (f32[384,128]{1,0:T(8,128)S(1)}, s32[1,8]{1,0:T(1,128)S(1)}) custom-call(bf16[512,2048]{1,0:T(8,128)(2,1)} %mask.1, bf16[512,2048]{1,0:T(8,128)(2,1)} %cotangent.1, bf16[2048,384]{1,0:T(8,128)(2,1)} %constant.30.clone.col_table, bf16[4,384,512]{2,1,0:T(8,128)(2,1)} %constant.31.clone.row_table), custom_call_target="tpu_custom_call" | custom-call | flops 805306368 | bytes 6291456 | tf_op jit(solution)/shard_map/forward/pallas_call | solution.py:131
  3.7 0.5 %collective-permute-start = (f32[384,128]{1,0:T(8,128)S(1)}, f32[384,128]{1,0:T(8,128)S(1)}, u32[]{:S(2)}, u32[]{:S(2)}) collective-permute-start(f32[384,128]{1,0:T(8,128)S(1)} %get-tuple-element.7), channel_id=1, source_target_pairs={{0,1},{1,0},{2,3},{3,2},{4,5},{5,4},{6,7},{7,6},{8,9},{9,8},{10,11... | collective-permute-start | bytes 589832 | tf_op jit(solution)/shard_map/ppermute | solution.py:358
  4.8 0.0 copy-done.4
  4.9 2.6 %collective-permute-start.2 = (s32[1,8]{1,0:T(1,128)S(1)}, s32[1,8]{1,0:T(1,128)S(1)}, u32[]{:S(2)}, u32[]{:S(2)}) collective-permute-start(s32[1,8]{1,0:T(1,128)S(1)} %fusion), channel_id=1, source_target_pairs={{0,4},{1,5},{2,6},{3,7},{4,0},{5,1},{6,2},{7,3},{8,12},{9,13},{10,... | collective-permute-start | bytes 104 | tf_op jit(solution)/shard_map/ppermute | solution.py:358
  7.5 0.0 collective-permute-done
  7.5 0.6 %slice.4 = f32[1,1]{1,0:T(1,128)} slice(f32[384,128]{1,0:T(8,128)S(1)} %add.69.own), slice={[192:193], [64:65]} | slice | bytes 8 | tf_op jit(solution)/shard_map/slice | solution.py:377
  8.1 1.5 %collective-permute-start.1 = (f32[384,128]{1,0:T(8,128)S(1)}, f32[384,128]{1,0:T(8,128)S(1)}, u32[]{:S(2)}, u32[]{:S(2)}) collective-permute-start(f32[384,128]{1,0:T(8,128)S(1)} %add.69.own), channel_id=1, source_target_pairs={{0,2},{1,3},{2,0},{3,1},{4,6},{5,7},{6,4},{7,5},{8,10},{9,11},{10,... | collective-permute-start | bytes 589832 | tf_op jit(solution)/shard_map/ppermute | solution.py:358
  10.3 0.0 collective-permute-done.2
  10.3 0.0 copy-done.1
  10.3 0.0 copy-done.2
  10.3 0.7 %slot_lines.1.own_lines = f32[16,128]{1,0:T(8,128)S(1)} custom-call(s32[2,8]{1,0:T(2,128)S(1)} %add_add_fusion.ids, s32[2,12288]{1,0:T(2,128)S(1)} %bitcast.5, f32[96,128]{1,0:T(8,128)S(1)} %bitcast.6), custom_call_target="tpu_custom_call" | custom-call | flops 1 | bytes 1 | tf_op jit(solution)/shard_map/slot_lines/pallas_call | solution.py:182
  11.0 2.6 %collective-permute-start.3 = (f32[16,128]{1,0:T(8,128)S(1)}, f32[16,128]{1,0:T(8,128)S(1)}, u32[]{:S(2)}, u32[]{:S(2)}) collective-permute-start(f32[16,128]{1,0:T(8,128)S(1)} %slot_lines.1.own_lines), channel_id=1, source_target_pairs={{0,8},{1,9},{2,10},{3,11},{4,12},{5,13},{6,14},{7,15},{8,0},{9,1},... | collective-permute-start | bytes 24584 | tf_op jit(solution)/shard_map/ppermute | solution.py:358
  13.6 0.0 copy-done.3
  13.6 0.8 %cosine_select_fusion = (f32[64,64]{1,0:T(8,128)S(1)}, f32[64,64]{1,0:T(8,128)S(1)}) fusion(f32[64,64]{1,0:T(8,128)S(1)} %copy-done.3, f32[]{:T(128)} %bitcast.1, s32[64]{0:T(128)S(1)} %add_multiply_fusion), kind=kLoop, calls=%fused_computation.3 | loop fusion | flops 20480 | bytes 49412 | tf_op jit(solution)/shard_map/jit(_where)/select_n | solution.py:346
  14.4 1.2 %collective-permute-done.3.other_lines = f32[16,128]{1,0:T(8,128)S(1)} collective-permute-done((f32[16,128]{1,0:T(8,128)S(1)}, f32[16,128]{1,0:T(8,128)S(1)}, u32[]{:S(2)}, u32[]{:S(2)}) %collective-permute-start.3) | collective-permute-done | bytes 8224 | tf_op jit(solution)/shard_map/ppermute | solution.py:358
  15.6 0.0 collective-permute-done.1.other
  15.6 0.0 copy-done
  15.6 4.2 %adjoint.1 = f32[1,128,2048]{2,1,0:T(8,128)} custom-call(f32[384,128]{1,0:T(8,128)S(1)} %add.69.own, f32[384,128]{1,0:T(8,128)S(1)} %collective-permute-done.1.other, f32[16,128]{1,0:T(8,128)S(1)} %slot_lines.1.own_lines, f32[16,128]{1,0:T(8,128)S(1)} %collective-permute-done.3.other_lines, f32[128,128]{1,0:T(8,128)S(1)} %select_maximum_fusion.pupil, ...), custom_call_target="tpu_custom_call" | custom-call | flops 268435456 | bytes 4194304 | tf_op jit(solution)/shard_map/adjoint/pallas_call | solution.py:312
  (5 shorter events, 0.1 us)
Async XLA Ops:
  0.0 15.6 %copy-start = (bf16[768,256]{1,0:T(8,128)(2,1)S(1)}, bf16[768,256]{1,0:T(8,128)(2,1)}, u32[]{:S(2)}) copy-start(bf16[768,256]{1,0:T(8,128)(2,1)} %constant.32.clone.table) | copy-start | bytes 1179652
  0.0 4.8 %copy-start.4 = (s32[1,8]{1,0:T(1,128)S(1)}, s32[1,8]{1,0:T(1,128)}, u32[]{:S(2)}) copy-start(s32[1,8]{1,0:T(1,128)} %param.17) | copy-start | bytes 100
  0.0 10.3 %copy-start.1 = (s32[12288,2]{0,1:T(2,128)S(1)}, s32[12288,2]{0,1:T(2,128)}, u32[]{:S(2)}) copy-start(s32[12288,2]{0,1:T(2,128)} %param.16) | copy-start | bytes 294916
  0.0 10.3 %copy-start.2 = (f32[12288]{0:T(1024)S(1)}, f32[12288]{0:T(1024)}, u32[]{:S(2)}) copy-start(f32[12288]{0:T(1024)} %param.15) | copy-start | bytes 147460
  0.0 13.6 %copy-start.3 = (f32[64,64]{1,0:T(8,128)S(1)}, f32[64,64]{1,0:T(8,128)}, u32[]{:S(2)}) copy-start(f32[64,64]{1,0:T(8,128)} %param.14) | copy-start | bytes 49156
  3.7 3.9 %collective-permute-start = (f32[384,128]{1,0:T(8,128)S(1)}, f32[384,128]{1,0:T(8,128)S(1)}, u32[]{:S(2)}, u32[]{:S(2)}) collective-permute-start(f32[384,128]{1,0:T(8,128)S(1)} %get-tuple-element.7), channel_id=1, source_target_pairs={{0,1},{1,0},{2,3},{3,2},{4,5},{5,4},{6,7},{7,6},{8,9},{9,8},{10,11... | collective-permute-start | bytes 589832 | tf_op jit(solution)/shard_map/ppermute | solution.py:358
  4.9 5.4 %collective-permute-start.2 = (s32[1,8]{1,0:T(1,128)S(1)}, s32[1,8]{1,0:T(1,128)S(1)}, u32[]{:S(2)}, u32[]{:S(2)}) collective-permute-start(s32[1,8]{1,0:T(1,128)S(1)} %fusion), channel_id=1, source_target_pairs={{0,4},{1,5},{2,6},{3,7},{4,0},{5,1},{6,2},{7,3},{8,12},{9,13},{10,... | collective-permute-start | bytes 104 | tf_op jit(solution)/shard_map/ppermute | solution.py:358
  8.1 7.5 %collective-permute-start.1 = (f32[384,128]{1,0:T(8,128)S(1)}, f32[384,128]{1,0:T(8,128)S(1)}, u32[]{:S(2)}, u32[]{:S(2)}) collective-permute-start(f32[384,128]{1,0:T(8,128)S(1)} %add.69.own), channel_id=1, source_target_pairs={{0,2},{1,3},{2,0},{3,1},{4,6},{5,7},{6,4},{7,5},{8,10},{9,11},{10,... | collective-permute-start | bytes 589832 | tf_op jit(solution)/shard_map/ppermute | solution.py:358
  11.0 4.6 %collective-permute-start.3 = (f32[16,128]{1,0:T(8,128)S(1)}, f32[16,128]{1,0:T(8,128)S(1)}, u32[]{:S(2)}, u32[]{:S(2)}) collective-permute-start(f32[16,128]{1,0:T(8,128)S(1)} %slot_lines.1.own_lines), channel_id=1, source_target_pairs={{0,8},{1,9},{2,10},{3,11},{4,12},{5,13},{6,14},{7,15},{8,0},{9,1},... | collective-permute-start | bytes 24584 | tf_op jit(solution)/shard_map/ppermute | solution.py:358

commit v5 on v4

--- a/solution.py
+++ b/solution.py
@@ -132,7 +132,7 @@
         forward_kernel,
         out_shape=(
             jax.ShapeDtypeStruct((SUMS, BAND), jnp.float32),
-            jax.ShapeDtypeStruct((1, SLOTS), jnp.int32),
+            jax.ShapeDtypeStruct((1, SLOTS + 1), jnp.int32),
         ),
         in_specs=[HBM] * 4,
         out_specs=(VMEM, VMEM),
@@ -151,18 +151,19 @@
     )(mask, cotangent, col_table, row_table)
 
 
-def lines_kernel(ids, shift, weight, lines):
+def lines_kernel(ids, shift, weight, before, lines):
+    del before
     lane = lax.broadcasted_iota(jnp.int32, (SLOTS, LANES), 1)
     place = lax.broadcasted_iota(jnp.int32, (SLOTS, LANES), 0)
 
     def one(row, carry):
         blocks, weights, there = [], [], jnp.full_like(lane, -1)
         for slot in range(SLOTS):
-            source = jnp.maximum(ids[row, slot], 0)
+            source = ids[row, slot]
             start = pl.multiple_of(source // LANES * LANES, LANES)
             blocks.append(shift[:, pl.ds(start, LANES)])
             weights.append(weight[pl.ds(source // LANES, 1), :])
-            found = jnp.where(ids[row, slot] >= 0, source % LANES, -1)
+            found = jnp.where(slot < ids[row, SLOTS], source % LANES, -1)
             there = jnp.where(place == slot, found, there)
         here = lane == there
         line = jnp.zeros((SLOTS, LANES), jnp.float32)
@@ -178,16 +179,17 @@
     lax.fori_loop(0, ids.shape[0], one, jnp.int32(0), unroll=ids.shape[0] <= 4)
 
 
-def slot_lines(ids, shift, weight):
+def slot_lines(ids, shift, weight, before):
+    count = ids.shape[0] * SLOTS
     return pl.pallas_call(
         lines_kernel,
-        out_shape=jax.ShapeDtypeStruct((ids.size, LANES), jnp.float32),
-        in_specs=[SMEM, VMEM, VMEM],
+        out_shape=jax.ShapeDtypeStruct((count, LANES), jnp.float32),
+        in_specs=[SMEM, VMEM, VMEM, pl.BlockSpec(memory_space=pl.ANY)],
         out_specs=VMEM,
         compiler_params=pltpu.CompilerParams(vmem_limit_bytes=2 * 1024 * 1024),
         cost_estimate=pl.CostEstimate(flops=1, bytes_accessed=1, transcendentals=0),
         name="slot_lines",
-    )(ids, shift, weight)
+    )(ids, shift, weight, before)
 
 
 def adjoint_kernel(
@@ -364,8 +366,7 @@
     col_table, row_table, out_table, out_cols = image_tables(columns, height, n_tile, n_src)
     sizes = {"src": n_src, "tile": n_tile}
     own, zeros = forward(mask, cotangent, col_table, row_table)
-    used = jnp.arange(SLOTS, dtype=jnp.int32)[None, :] < source_count[0]
-    ids = jnp.where(used, source_ids, -1) + zeros
+    ids = jnp.concatenate([source_ids, source_count[:, None]], 1) + zeros
     bit = 1
     while bit < n_src // 2:
         ids = jnp.concatenate([ids, swapped(ids, sizes, {"src": bit})], 0)
@@ -374,11 +375,10 @@
     while step < n_tile // 2:
         own = own + swapped(own, sizes, {"tile": step})
         step *= 2
-    zero = own[BAND + BAND // 2, BAND // 2]
-    own_lines = slot_lines(ids + zero.astype(jnp.int32), shift_table.T, source_weight.reshape(-1, LANES))
+    own_lines = slot_lines(ids, shift_table.T, source_weight.reshape(-1, LANES), own)
     other_lines = swapped(own_lines, sizes, {"src": bit})
     other = swapped(own, sizes, {"tile": step})
-    pupil = pupil_rows(pupil_phase + zero)
+    pupil = pupil_rows(pupil_phase)
     return adjoint(
         own, other, own_lines, other_lines, pupil, grid_tables(), out_cols, out_table, n_src
     )

time: 20 us -> 20.3 us (1.015)
  waiting for transfers between devices: 1.16 us -> 3.35 us
  between operations: 1.39 us -> 0.74 us
  local copies, waits for them, and re-layouts: 0.6 us -> 0.02 us
  other arithmetic: 0.83 us -> 0.26 us
    ppermute x4, waiting for transfers between devices: 1.16 us -> 3.35 us  [swapped(): return lax.ppermute(array, axes, turn)]
    select_n x1, other arithmetic: 0.78 us -> 0.13 us  [pupil_rows(): jnp.where(inside, jnp.cos(phase), 0.0)]
    slice x1 -> x0, local copies, waits for them, and re-layouts: 0.58 us -> none  [body(): zero = own[BAND + BAND // 2, BAND // 2]]
  transfers between devices with their start and end apart: 4 -> 4, of which waited for: 1 -> 3; matrix products, arithmetic and copies ran while one was open for 7% -> 1% of each run, Pallas kernels for 4% -> 4%
where the time goes in v5:
time: 20.3 us; the launch traced here: 20.2 us
  Pallas kernels  8.59 us (42%)
  starting transfers between devices  7.19 us (35%)
  waiting for transfers between devices  3.35 us (17%)
  between operations  0.74 us (4%)
  other arithmetic  0.26 us (1%)
    ppermute x4, starting transfers between devices, swapped(): return lax.ppermute(array, axes, turn)  7.19 us
    pallas_call x1, Pallas kernels, adjoint(): pl.pallas_call(functools.partial(adjoint_kernel, n_src), out_shape=jax.Sh...  4.2 us
    pallas_call x1, Pallas kernels, forward(): pl.pallas_call(forward_kernel, out_shape=(jax.ShapeDtypeStruct((SUMS, BAN...  3.64 us
    ppermute x4, waiting for transfers between devices, swapped(): return lax.ppermute(array, axes, turn)  3.35 us
    pallas_call x1, Pallas kernels, slot_lines(): pl.pallas_call(lines_kernel, out_shape=jax.ShapeDtypeStruct((count, LANES...  0.75 us
  transfers between devices with their start and end apart: 4, of which 3 were waited for; matrix products, arithmetic and copies ran while one was open for 1% of the time, Pallas kernels for 4%

profile of v5, /device:TPU:0, one launch (start us, length us, event | category | flops | bytes accessed | tf_op | source)
XLA Modules:
  0.0 20.2 jit_solution(2989590842409898060)
XLA Ops:
  0.7 0.0 copy-start.4
  0.7 0.0 copy-start.3
  0.7 0.0 copy-start.1
  0.7 0.0 copy-start.2
  0.7 0.0 copy-start
  0.7 3.6 %forward.1 = (f32[384,128]{1,0:T(8,128)S(1)}, s32[1,9]{1,0:T(1,128)S(1)}) custom-call(bf16[512,2048]{1,0:T(8,128)(2,1)} %mask.1, bf16[512,2048]{1,0:T(8,128)(2,1)} %cotangent.1, bf16[2048,384]{1,0:T(8,128)(2,1)} %constant.28.clone.col_table, bf16[4,384,512]{2,1,0:T(8,128)(2,1)} %constant.29.clone.row_table), custom_call_target="tpu_custom_call" | custom-call | flops 805306368 | bytes 6291456 | tf_op jit(solution)/shard_map/forward/pallas_call | solution.py:131
  4.4 0.0 copy-done.4
  4.4 0.1 add_add_fusion
  4.4 3.0 %collective-permute-start.2 = (s32[1,9]{1,0:T(1,128)S(1)}, s32[1,9]{1,0:T(1,128)S(1)}, u32[]{:S(2)}, u32[]{:S(2)}) collective-permute-start(s32[1,9]{1,0:T(1,128)S(1)} %add_add_fusion), channel_id=1, source_target_pairs={{0,4},{1,5},{2,6},{3,7},{4,0},{5,1},{6,2},{7,3},{8,12},{9,13},{10,... | collective-permute-start | bytes 116 | tf_op jit(solution)/shard_map/ppermute | solution.py:360
  7.5 0.0 collective-permute-start
  7.5 0.0 copy-done.3
  7.5 0.1 cosine_select_fusion
  7.6 1.3 %collective-permute-done = f32[384,128]{1,0:T(8,128)S(1)} collective-permute-done((f32[384,128]{1,0:T(8,128)S(1)}, f32[384,128]{1,0:T(8,128)S(1)}, u32[]{:S(2)}, u32[]{:S(2)}) %collective-permute-start) | collective-permute-done | bytes 196640 | tf_op jit(solution)/shard_map/ppermute | solution.py:360
  8.9 1.6 %collective-permute-start.1 = (f32[384,128]{1,0:T(8,128)S(1)}, f32[384,128]{1,0:T(8,128)S(1)}, u32[]{:S(2)}, u32[]{:S(2)}) collective-permute-start(f32[384,128]{1,0:T(8,128)S(1)} %add.57.before.own), channel_id=1, source_target_pairs={{0,2},{1,3},{2,0},{3,1},{4,6},{5,7},{6,4},{7,5},{8,10},{9,11},{10,... | collective-permute-start | bytes 589832 | tf_op jit(solution)/shard_map/ppermute | solution.py:360
  10.5 0.0 collective-permute-done.2
  10.5 0.0 copy-done.1
  10.5 0.0 copy-done.2
  10.5 0.7 %slot_lines.1.own_lines = f32[16,128]{1,0:T(8,128)S(1)} custom-call(s32[2,9]{1,0:T(2,128)S(1)} %pad_add_fusion.ids, s32[2,12288]{1,0:T(2,128)S(1)} %bitcast.4, f32[96,128]{1,0:T(8,128)S(1)} %bitcast.5, f32[384,128]{1,0:T(8,128)S(1)} %add.57.before.own), custom_call_target="tpu_custom_call" | custom-call | flops 1 | bytes 1 | tf_op jit(solution)/shard_map/slot_lines/pallas_call | solution.py:184
  11.3 2.6 %collective-permute-start.3 = (f32[16,128]{1,0:T(8,128)S(1)}, f32[16,128]{1,0:T(8,128)S(1)}, u32[]{:S(2)}, u32[]{:S(2)}) collective-permute-start(f32[16,128]{1,0:T(8,128)S(1)} %slot_lines.1.own_lines), channel_id=1, source_target_pairs={{0,8},{1,9},{2,10},{3,11},{4,12},{5,13},{6,14},{7,15},{8,0},{9,1},... | collective-permute-start | bytes 24584 | tf_op jit(solution)/shard_map/ppermute | solution.py:360
  13.9 2.0 %collective-permute-done.3.other_lines = f32[16,128]{1,0:T(8,128)S(1)} collective-permute-done((f32[16,128]{1,0:T(8,128)S(1)}, f32[16,128]{1,0:T(8,128)S(1)}, u32[]{:S(2)}, u32[]{:S(2)}) %collective-permute-start.3) | collective-permute-done | bytes 8224 | tf_op jit(solution)/shard_map/ppermute | solution.py:360
  15.9 0.1 collective-permute-done.1.other
  16.0 0.0 copy-done
  16.0 4.2 %adjoint.1 = f32[1,128,2048]{2,1,0:T(8,128)} custom-call(f32[384,128]{1,0:T(8,128)S(1)} %add.57.before.own, f32[384,128]{1,0:T(8,128)S(1)} %collective-permute-done.1.other, f32[16,128]{1,0:T(8,128)S(1)} %slot_lines.1.own_lines, f32[16,128]{1,0:T(8,128)S(1)} %collective-permute-done.3.other_lines, f32[128,128]{1,0:T(8,128)S(1)} %select_maximum_fusion.pupil, ...), custom_call_target="tpu_custom_call" | custom-call | flops 268435456 | bytes 4194304 | tf_op jit(solution)/shard_map/adjoint/pallas_call | solution.py:314
  (4 shorter events, 0.1 us)
Async XLA Ops:
  0.7 3.7 %copy-start.4 = (s32[1,8]{1,0:T(1,128)S(1)}, s32[1,8]{1,0:T(1,128)}, u32[]{:S(2)}) copy-start(s32[1,8]{1,0:T(1,128)} %param.17) | copy-start | bytes 100
  0.7 6.8 %copy-start.3 = (f32[64,64]{1,0:T(8,128)S(1)}, f32[64,64]{1,0:T(8,128)}, u32[]{:S(2)}) copy-start(f32[64,64]{1,0:T(8,128)} %param.14) | copy-start | bytes 49156
  0.7 9.8 %copy-start.1 = (s32[12288,2]{0,1:T(2,128)S(1)}, s32[12288,2]{0,1:T(2,128)}, u32[]{:S(2)}) copy-start(s32[12288,2]{0,1:T(2,128)} %param.16) | copy-start | bytes 294916
  0.7 9.8 %copy-start.2 = (f32[12288]{0:T(1024)S(1)}, f32[12288]{0:T(1024)}, u32[]{:S(2)}) copy-start(f32[12288]{0:T(1024)} %param.15) | copy-start | bytes 147460
  0.7 15.3 %copy-start = (bf16[768,256]{1,0:T(8,128)(2,1)S(1)}, bf16[768,256]{1,0:T(8,128)(2,1)}, u32[]{:S(2)}) copy-start(bf16[768,256]{1,0:T(8,128)(2,1)} %constant.30.clone.table) | copy-start | bytes 1179652
  4.4 6.1 %collective-permute-start.2 = (s32[1,9]{1,0:T(1,128)S(1)}, s32[1,9]{1,0:T(1,128)S(1)}, u32[]{:S(2)}, u32[]{:S(2)}) collective-permute-start(s32[1,9]{1,0:T(1,128)S(1)} %add_add_fusion), channel_id=1, source_target_pairs={{0,4},{1,5},{2,6},{3,7},{4,0},{5,1},{6,2},{7,3},{8,12},{9,13},{10,... | collective-permute-start | bytes 116 | tf_op jit(solution)/shard_map/ppermute | solution.py:360
  7.5 1.4 %collective-permute-start = (f32[384,128]{1,0:T(8,128)S(1)}, f32[384,128]{1,0:T(8,128)S(1)}, u32[]{:S(2)}, u32[]{:S(2)}) collective-permute-start(f32[384,128]{1,0:T(8,128)S(1)} %get-tuple-element.7), channel_id=1, source_target_pairs={{0,1},{1,0},{2,3},{3,2},{4,5},{5,4},{6,7},{7,6},{8,9},{9,8},{10,11... | collective-permute-start | bytes 589832 | tf_op jit(solution)/shard_map/ppermute | solution.py:360
  8.9 7.0 %collective-permute-start.1 = (f32[384,128]{1,0:T(8,128)S(1)}, f32[384,128]{1,0:T(8,128)S(1)}, u32[]{:S(2)}, u32[]{:S(2)}) collective-permute-start(f32[384,128]{1,0:T(8,128)S(1)} %add.57.before.own), channel_id=1, source_target_pairs={{0,2},{1,3},{2,0},{3,1},{4,6},{5,7},{6,4},{7,5},{8,10},{9,11},{10,... | collective-permute-start | bytes 589832 | tf_op jit(solution)/shard_map/ppermute | solution.py:360
  11.3 4.6 %collective-permute-start.3 = (f32[16,128]{1,0:T(8,128)S(1)}, f32[16,128]{1,0:T(8,128)S(1)}, u32[]{:S(2)}, u32[]{:S(2)}) collective-permute-start(f32[16,128]{1,0:T(8,128)S(1)} %slot_lines.1.own_lines), channel_id=1, source_target_pairs={{0,8},{1,9},{2,10},{3,11},{4,12},{5,13},{6,14},{7,15},{8,0},{9,1},... | collective-permute-start | bytes 24584 | tf_op jit(solution)/shard_map/ppermute | solution.py:360

commit v6 on v5

--- a/solution.py
+++ b/solution.py
@@ -121,7 +121,8 @@
     blocks = dot(row_v[: 2 * BAND, :], mask_part.astype(jnp.bfloat16))
     partial[:BAND, :] = blocks[:BAND, :BAND] + blocks[BAND:, BAND:]
     partial[BAND : 2 * BAND, :] = blocks[:BAND, BAND:] - blocks[BAND:, :BAND]
-    partial[2 * BAND :, :] = dot(row_v[2 * BAND :, :], cot_part.astype(jnp.bfloat16))
+    partial[2 * BAND : SUMS, :] = dot(row_v[2 * BAND :, :], cot_part.astype(jnp.bfloat16))
+    partial[SUMS:, :] = jnp.zeros((8, BAND), jnp.float32)
     zeros[...] = jnp.zeros_like(zeros)
 
 
@@ -131,7 +132,7 @@
     return pl.pallas_call(
         forward_kernel,
         out_shape=(
-            jax.ShapeDtypeStruct((SUMS, BAND), jnp.float32),
+            jax.ShapeDtypeStruct((SUMS + 8, BAND), jnp.float32),
             jax.ShapeDtypeStruct((1, SLOTS + 1), jnp.int32),
         ),
         in_specs=[HBM] * 4,
@@ -151,8 +152,7 @@
     )(mask, cotangent, col_table, row_table)
 
 
-def lines_kernel(ids, shift, weight, before, lines):
-    del before
+def lines_kernel(ids, shift, weight, lines):
     lane = lax.broadcasted_iota(jnp.int32, (SLOTS, LANES), 1)
     place = lax.broadcasted_iota(jnp.int32, (SLOTS, LANES), 0)
 
@@ -179,17 +179,17 @@
     lax.fori_loop(0, ids.shape[0], one, jnp.int32(0), unroll=ids.shape[0] <= 4)
 
 
-def slot_lines(ids, shift, weight, before):
+def slot_lines(ids, shift, weight):
     count = ids.shape[0] * SLOTS
     return pl.pallas_call(
         lines_kernel,
         out_shape=jax.ShapeDtypeStruct((count, LANES), jnp.float32),
-        in_specs=[SMEM, VMEM, VMEM, pl.BlockSpec(memory_space=pl.ANY)],
+        in_specs=[SMEM, VMEM, VMEM],
         out_specs=VMEM,
         compiler_params=pltpu.CompilerParams(vmem_limit_bytes=2 * 1024 * 1024),
         cost_estimate=pl.CostEstimate(flops=1, bytes_accessed=1, transcendentals=0),
         name="slot_lines",
-    )(ids, shift, weight, before)
+    )(ids, shift, weight)
 
 
 def adjoint_kernel(
@@ -208,7 +208,7 @@
         copy.start()
 
     scale = 1.0 / math.sqrt(TILE_ROWS * COLS)
-    whole = own[...] + other[...]
+    whole = own[:SUMS, :] + other[:SUMS, :]
     spec = (whole[: 2 * BAND] * scale).astype(jnp.bfloat16).astype(jnp.float32)
     spec_real[...] = spec[:BAND]
     spec_imag[...] = spec[BAND:]
@@ -375,10 +375,10 @@
     while step < n_tile // 2:
         own = own + swapped(own, sizes, {"tile": step})
         step *= 2
-    own_lines = slot_lines(ids, shift_table.T, source_weight.reshape(-1, LANES), own)
+    own_lines = slot_lines(ids + own[SUMS : SUMS + 1, : SLOTS + 1].astype(jnp.int32), shift_table.T, source_weight.reshape(-1, LANES))
     other_lines = swapped(own_lines, sizes, {"src": bit})
     other = swapped(own, sizes, {"tile": step})
-    pupil = pupil_rows(pupil_phase)
+    pupil = pupil_rows(pupil_phase + own[SUMS : SUMS + 1, :PUPIL])
     return adjoint(
         own, other, own_lines, other_lines, pupil, grid_tables(), out_cols, out_table, n_src
     )

time: 20.3 us -> 19.1 us (0.941)
  waiting for transfers between devices: 3.35 us -> 1.74 us
  starting transfers between devices: 7.19 us -> 7.62 us
    ppermute x4, waiting for transfers between devices: 3.35 us -> 1.74 us  [swapped(): return lax.ppermute(array, axes, turn)]
    ppermute x4, starting transfers between devices: 7.19 us -> 7.62 us  [swapped(): return lax.ppermute(array, axes, turn)]
  transfers between devices with their start and end apart: 4 -> 4, of which waited for: 3 -> 2; matrix products, arithmetic and copies ran while one was open for 1% -> 1% of each run, Pallas kernels for 4% -> 4%
where the time goes in v6:
time: 19.1 us; the launch traced here: 19 us
  Pallas kernels  8.59 us (45%)
  starting transfers between devices  7.62 us (40%)
  waiting for transfers between devices  1.74 us (9%)
  between operations  0.72 us (4%)
  other arithmetic  0.27 us (1%)
    ppermute x4, starting transfers between devices, swapped(): return lax.ppermute(array, axes, turn)  7.62 us
    pallas_call x1, Pallas kernels, adjoint(): pl.pallas_call(functools.partial(adjoint_kernel, n_src), out_shape=jax.Sh...  4.2 us
    pallas_call x1, Pallas kernels, forward(): pl.pallas_call(forward_kernel, out_shape=(jax.ShapeDtypeStruct((SUMS + 8,...  3.64 us
    ppermute x4, waiting for transfers between devices, swapped(): return lax.ppermute(array, axes, turn)  1.74 us
    pallas_call x1, Pallas kernels, slot_lines(): pl.pallas_call(lines_kernel, out_shape=jax.ShapeDtypeStruct((count, LANES...  0.75 us
  transfers between devices with their start and end apart: 4, of which 2 were waited for; matrix products, arithmetic and copies ran while one was open for 1% of the time, Pallas kernels for 4%

profile of v6, /device:TPU:0, one launch (start us, length us, event | category | flops | bytes accessed | tf_op | source)
XLA Modules:
  0.0 19.0 jit_solution(2395212720518664286)
XLA Ops:
  0.0 0.0 copy-start
  0.0 0.0 copy-start.4
  0.0 0.0 copy-start.1
  0.0 0.0 copy-start.2
  0.0 0.0 copy-start.3
  0.0 3.6 %forward.1 = (f32[392,128]{1,0:T(8,128)S(1)}, s32[1,9]{1,0:T(1,128)S(1)}) custom-call(bf16[512,2048]{1,0:T(8,128)(2,1)} %mask.1, bf16[512,2048]{1,0:T(8,128)(2,1)} %cotangent.1, bf16[2048,384]{1,0:T(8,128)(2,1)} %constant.28.clone.col_table, bf16[4,384,512]{2,1,0:T(8,128)(2,1)} %constant.29.clone.row_table), custom_call_target="tpu_custom_call" | custom-call | flops 805306368 | bytes 6291456 | tf_op jit(solution)/shard_map/forward/pallas_call | solution.py:132
  3.7 0.5 %collective-permute-start = (f32[392,128]{1,0:T(8,128)S(1)}, f32[392,128]{1,0:T(8,128)S(1)}, u32[]{:S(2)}, u32[]{:S(2)}) collective-permute-start(f32[392,128]{1,0:T(8,128)S(1)} %get-tuple-element.7), channel_id=1, source_target_pairs={{0,1},{1,0},{2,3},{3,2},{4,5},{5,4},{6,7},{7,6},{8,9},{9,8},{10,11... | collective-permute-start | bytes 602120 | tf_op jit(solution)/shard_map/ppermute | solution.py:360
  4.8 0.0 copy-done.4
  4.9 0.1 add_add_fusion.1
  4.9 2.6 %collective-permute-start.2 = (s32[1,9]{1,0:T(1,128)S(1)}, s32[1,9]{1,0:T(1,128)S(1)}, u32[]{:S(2)}, u32[]{:S(2)}) collective-permute-start(s32[1,9]{1,0:T(1,128)S(1)} %add_add_fusion.1), channel_id=1, source_target_pairs={{0,4},{1,5},{2,6},{3,7},{4,0},{5,1},{6,2},{7,3},{8,12},{9,13},{10,... | collective-permute-start | bytes 116 | tf_op jit(solution)/shard_map/ppermute | solution.py:360
  7.5 0.0 collective-permute-done
  7.6 1.6 %collective-permute-start.1 = (f32[392,128]{1,0:T(8,128)S(1)}, f32[392,128]{1,0:T(8,128)S(1)}, u32[]{:S(2)}, u32[]{:S(2)}) collective-permute-start(f32[392,128]{1,0:T(8,128)S(1)} %add.77.own), channel_id=1, source_target_pairs={{0,2},{1,3},{2,0},{3,1},{4,6},{5,7},{6,4},{7,5},{8,10},{9,11},{10,... | collective-permute-start | bytes 602120 | tf_op jit(solution)/shard_map/ppermute | solution.py:360
  9.1 0.0 collective-permute-done.2
  9.2 0.0 copy-done.1
  9.2 0.0 copy-done.2
  9.2 0.7 %slot_lines.1.own_lines = f32[16,128]{1,0:T(8,128)S(1)} custom-call(s32[2,9]{1,0:T(2,128)S(1)} %add_add_fusion.ids, s32[2,12288]{1,0:T(2,128)S(1)} %bitcast.8, f32[96,128]{1,0:T(8,128)S(1)} %bitcast.9), custom_call_target="tpu_custom_call" | custom-call | flops 1 | bytes 1 | tf_op jit(solution)/shard_map/slot_lines/pallas_call | solution.py:184
  9.9 2.9 %collective-permute-start.3 = (f32[16,128]{1,0:T(8,128)S(1)}, f32[16,128]{1,0:T(8,128)S(1)}, u32[]{:S(2)}, u32[]{:S(2)}) collective-permute-start(f32[16,128]{1,0:T(8,128)S(1)} %slot_lines.1.own_lines), channel_id=1, source_target_pairs={{0,8},{1,9},{2,10},{3,11},{4,12},{5,13},{6,14},{7,15},{8,0},{9,1},... | collective-permute-start | bytes 24584 | tf_op jit(solution)/shard_map/ppermute | solution.py:360
  12.9 0.0 copy-done.3
  12.9 0.1 cosine_select_fusion
  13.0 1.5 %collective-permute-done.3.other_lines = f32[16,128]{1,0:T(8,128)S(1)} collective-permute-done((f32[16,128]{1,0:T(8,128)S(1)}, f32[16,128]{1,0:T(8,128)S(1)}, u32[]{:S(2)}, u32[]{:S(2)}) %collective-permute-start.3) | collective-permute-done | bytes 8224 | tf_op jit(solution)/shard_map/ppermute | solution.py:360
  14.5 0.3 %collective-permute-done.1.other = f32[392,128]{1,0:T(8,128)S(1)} collective-permute-done((f32[392,128]{1,0:T(8,128)S(1)}, f32[392,128]{1,0:T(8,128)S(1)}, u32[]{:S(2)}, u32[]{:S(2)}) %collective-permute-start.1) | collective-permute-done | bytes 200736 | tf_op jit(solution)/shard_map/ppermute | solution.py:360
  14.8 0.0 copy-done
  14.8 4.2 %adjoint.1 = f32[1,128,2048]{2,1,0:T(8,128)} custom-call(f32[392,128]{1,0:T(8,128)S(1)} %add.77.own, f32[392,128]{1,0:T(8,128)S(1)} %collective-permute-done.1.other, f32[16,128]{1,0:T(8,128)S(1)} %slot_lines.1.own_lines, f32[16,128]{1,0:T(8,128)S(1)} %collective-permute-done.3.other_lines, f32[128,128]{1,0:T(8,128)S(1)} %select_maximum_fusion.pupil, ...), custom_call_target="tpu_custom_call" | custom-call | flops 268435456 | bytes 4194304 | tf_op jit(solution)/shard_map/adjoint/pallas_call | solution.py:314
  (6 shorter events, 0.1 us)
Async XLA Ops:
  0.0 14.8 %copy-start = (bf16[768,256]{1,0:T(8,128)(2,1)S(1)}, bf16[768,256]{1,0:T(8,128)(2,1)}, u32[]{:S(2)}) copy-start(bf16[768,256]{1,0:T(8,128)(2,1)} %constant.30.clone.table) | copy-start | bytes 1179652
  0.0 4.8 %copy-start.4 = (s32[1,8]{1,0:T(1,128)S(1)}, s32[1,8]{1,0:T(1,128)}, u32[]{:S(2)}) copy-start(s32[1,8]{1,0:T(1,128)} %param.17) | copy-start | bytes 100
  0.0 9.1 %copy-start.1 = (s32[12288,2]{0,1:T(2,128)S(1)}, s32[12288,2]{0,1:T(2,128)}, u32[]{:S(2)}) copy-start(s32[12288,2]{0,1:T(2,128)} %param.16) | copy-start | bytes 294916
  0.0 9.2 %copy-start.2 = (f32[12288]{0:T(1024)S(1)}, f32[12288]{0:T(1024)}, u32[]{:S(2)}) copy-start(f32[12288]{0:T(1024)} %param.15) | copy-start | bytes 147460
  0.0 12.9 %copy-start.3 = (f32[64,64]{1,0:T(8,128)S(1)}, f32[64,64]{1,0:T(8,128)}, u32[]{:S(2)}) copy-start(f32[64,64]{1,0:T(8,128)} %param.14) | copy-start | bytes 49156
  3.7 3.9 %collective-permute-start = (f32[392,128]{1,0:T(8,128)S(1)}, f32[392,128]{1,0:T(8,128)S(1)}, u32[]{:S(2)}, u32[]{:S(2)}) collective-permute-start(f32[392,128]{1,0:T(8,128)S(1)} %get-tuple-element.7), channel_id=1, source_target_pairs={{0,1},{1,0},{2,3},{3,2},{4,5},{5,4},{6,7},{7,6},{8,9},{9,8},{10,11... | collective-permute-start | bytes 602120 | tf_op jit(solution)/shard_map/ppermute | solution.py:360
  4.9 4.2 %collective-permute-start.2 = (s32[1,9]{1,0:T(1,128)S(1)}, s32[1,9]{1,0:T(1,128)S(1)}, u32[]{:S(2)}, u32[]{:S(2)}) collective-permute-start(s32[1,9]{1,0:T(1,128)S(1)} %add_add_fusion.1), channel_id=1, source_target_pairs={{0,4},{1,5},{2,6},{3,7},{4,0},{5,1},{6,2},{7,3},{8,12},{9,13},{10,... | collective-permute-start | bytes 116 | tf_op jit(solution)/shard_map/ppermute | solution.py:360
  7.6 7.2 %collective-permute-start.1 = (f32[392,128]{1,0:T(8,128)S(1)}, f32[392,128]{1,0:T(8,128)S(1)}, u32[]{:S(2)}, u32[]{:S(2)}) collective-permute-start(f32[392,128]{1,0:T(8,128)S(1)} %add.77.own), channel_id=1, source_target_pairs={{0,2},{1,3},{2,0},{3,1},{4,6},{5,7},{6,4},{7,5},{8,10},{9,11},{10,... | collective-permute-start | bytes 602120 | tf_op jit(solution)/shard_map/ppermute | solution.py:360
  9.9 4.6 %collective-permute-start.3 = (f32[16,128]{1,0:T(8,128)S(1)}, f32[16,128]{1,0:T(8,128)S(1)}, u32[]{:S(2)}, u32[]{:S(2)}) collective-permute-start(f32[16,128]{1,0:T(8,128)S(1)} %slot_lines.1.own_lines), channel_id=1, source_target_pairs={{0,8},{1,9},{2,10},{3,11},{4,12},{5,13},{6,14},{7,15},{8,0},{9,1},... | collective-permute-start | bytes 24584 | tf_op jit(solution)/shard_map/ppermute | solution.py:360

commit v7 on v6

--- a/solution.py
+++ b/solution.py
@@ -16,9 +16,9 @@
 PUPIL = 64
 SLOTS = 8
 GRID = 128
-CHUNKS = 4
-GROUP = 32
-OX, OY, FACTOR = range(3)
+CHUNKS = (1, 1, 2, 2, 1, 1)
+GROUPS = (16, 20, 24, 32)
+OX, OY, FACTOR, COUNT = range(4)
 PARTS = 4
 LANES = 128
 SUMS = 2 * BAND + GRID
@@ -91,29 +91,28 @@
     partial, zeros,
     mask_v, cot_v, col_v, row_v, sems,
 ):
-    height, columns = mask.shape
-    width = columns // CHUNKS
+    columns = mask.shape[1]
+    ends = np.cumsum(CHUNKS) * (columns // sum(CHUNKS))
+    parts = [pl.ds(int(low), int(high - low)) for low, high in zip([0, *ends], ends)]
     tile = lax.axis_index("tile")
     chunk_copies = []
-    for step in range(CHUNKS):
-        part = pl.ds(step * width, width)
+    for step, part in enumerate(parts):
         copies = [
             pltpu.make_async_copy(col_table.at[part, :], col_v.at[part, :], sems.at[step, 0]),
-            pltpu.make_async_copy(mask.at[:, part], mask_v.at[step], sems.at[step, 1]),
-            pltpu.make_async_copy(cotangent.at[:, part], cot_v.at[step], sems.at[step, 2]),
+            pltpu.make_async_copy(mask.at[:, part], mask_v.at[:, part], sems.at[step, 1]),
+            pltpu.make_async_copy(cotangent.at[:, part], cot_v.at[:, part], sems.at[step, 2]),
         ]
         for copy in copies:
             copy.start()
         chunk_copies.append(copies)
-    row_copy = pltpu.make_async_copy(row_table.at[tile], row_v, sems.at[CHUNKS, 0])
+    row_copy = pltpu.make_async_copy(row_table.at[tile], row_v, sems.at[len(CHUNKS), 0])
     row_copy.start()
 
-    for step in range(CHUNKS):
+    for step, part in enumerate(parts):
         for copy in chunk_copies[step]:
             copy.wait()
-        part = pl.ds(step * width, width)
-        mask_add = dot(mask_v[step], col_v[part, : 2 * BAND])
-        cot_add = dot(cot_v[step], col_v[part, 2 * BAND :])
+        mask_add = dot(mask_v[:, part], col_v[part, : 2 * BAND])
+        cot_add = dot(cot_v[:, part], col_v[part, 2 * BAND :])
         mask_part = mask_add if step == 0 else mask_part + mask_add
         cot_part = cot_add if step == 0 else cot_part + cot_add
 
@@ -128,7 +127,6 @@
 
 def forward(mask, cotangent, col_table, row_table):
     height, columns = mask.shape
-    width = columns // CHUNKS
     return pl.pallas_call(
         forward_kernel,
         out_shape=(
@@ -138,11 +136,11 @@
         in_specs=[HBM] * 4,
         out_specs=(VMEM, VMEM),
         scratch_shapes=[
-            pltpu.VMEM((CHUNKS, height, width), jnp.bfloat16),
-            pltpu.VMEM((CHUNKS, height, width), jnp.bfloat16),
+            pltpu.VMEM(mask.shape, jnp.bfloat16),
+            pltpu.VMEM(mask.shape, jnp.bfloat16),
             pltpu.VMEM(col_table.shape, jnp.bfloat16),
             pltpu.VMEM(row_table.shape[1:], jnp.bfloat16),
-            pltpu.SemaphoreType.DMA((CHUNKS + 1, 3)),
+            pltpu.SemaphoreType.DMA((len(CHUNKS) + 1, 3)),
         ],
         compiler_params=pltpu.CompilerParams(vmem_limit_bytes=GRANT),
         cost_estimate=pl.CostEstimate(
@@ -173,6 +171,7 @@
             line = jnp.where(lane == into, found, line)
         found = jnp.sum(jnp.where(here, jnp.concatenate(weights, 0), 0.0), 1, keepdims=True)
         line = jnp.where(lane == FACTOR, found * (2.0 / SLOTS / PUPIL / PUPIL), line)
+        line = jnp.where(lane == COUNT, ids[row, SLOTS].astype(jnp.float32), line)
         lines[pl.ds(pl.multiple_of(row * SLOTS, SLOTS), SLOTS), :] = line
         return carry
 
@@ -195,7 +194,7 @@
 def adjoint_kernel(
     n_src, own, other, own_lines, other_lines, pupil, table, col_table, out_table,
     result,
-    spec_real, spec_imag, image, table_v, col_v, out_v, result_v, lines, sems, out_sems, *bands,
+    spec_real, spec_imag, image, table_v, col_v, out_v, result_v, lines, used, sems, out_sems, *bands,
 ):
     place = lax.axis_index("tile") * n_src + lax.axis_index("src")
     grid_copy = pltpu.make_async_copy(table, table_v, sems.at[0])
@@ -216,14 +215,27 @@
     image[GRID:, :] = whole[2 * BAND :]
     for band in bands:
         band[...] = jnp.zeros_like(band)
+    for slot in range(2 * half + GROUPS[-1]):
+        used[slot] = jnp.int32(0)
     own_copy.wait()
     other_copy.wait()
+
+    def add(block, total):
+        first = block * SLOTS
+        for slot in range(SLOTS):
+            used[total + slot] = first + slot
+        return total + lines[first, COUNT].astype(jnp.int32)
+
+    blocks = 2 * half // SLOTS
+    total = lax.fori_loop(0, blocks, add, jnp.int32(0), unroll=blocks <= 8)
     grid_copy.wait()
 
-    def group(step, carry):
+    def group(first, size):
         starts, pupils, amplitudes = [], [], []
-        for slot in range(GROUP):
-            index = step * GROUP + slot
+        for slot in range(size):
+            place = first + slot
+            index = used[place]
+            factor = jnp.where(place < total, lines[index, FACTOR], 0.0)
             offset_x = lines[index, OX].astype(jnp.int32)
             offset_y = lines[index, OY].astype(jnp.int32)
             real = pltpu.roll(pupil[:PUPIL, :], offset_x, 1)
@@ -232,7 +244,7 @@
             amp_real = real * spec_real[rows, :] - imag * spec_imag[rows, :]
             amp_imag = real * spec_imag[rows, :] + imag * spec_real[rows, :]
             starts.append(offset_y)
-            pupils.append((real, imag, lines[index, FACTOR]))
+            pupils.append((real, imag, factor))
             amplitudes.append(jnp.concatenate([amp_real, amp_imag], 1).astype(jnp.bfloat16))
         halfway = dot(jnp.concatenate(amplitudes, 0), table_v[COLS_IN, :]).astype(jnp.bfloat16)
         halfway = jnp.concatenate(
@@ -244,7 +256,7 @@
                     ],
                     0,
                 )
-                for slot in range(GROUP)
+                for slot in range(size)
             ],
             1,
         )
@@ -254,7 +266,7 @@
         field_grad = jnp.concatenate(
             [
                 (field[:, slot * GRID : (slot + 1) * GRID] * image[...]).astype(jnp.bfloat16)
-                for slot in range(GROUP)
+                for slot in range(size)
             ],
             1,
         )
@@ -268,12 +280,12 @@
                     ],
                     1,
                 )
-                for slot in range(GROUP)
+                for slot in range(size)
             ],
             0,
         )
         grad = dot(back, table_v[COLS_OUT, :])
-        for slot in range(GROUP):
+        for slot in range(size):
             real, imag, factor = pupils[slot]
             grad_real = grad[slot * PUPIL : (slot + 1) * PUPIL, :BAND] * factor
             grad_imag = grad[slot * PUPIL : (slot + 1) * PUPIL, BAND:] * factor
@@ -281,9 +293,21 @@
             band_real, band_imag = bands[slot % 2], bands[2 + slot % 2]
             band_real[rows, :] = band_real[rows, :] + (real * grad_real + imag * grad_imag)
             band_imag[rows, :] = band_imag[rows, :] + (real * grad_imag - imag * grad_real)
+
+    largest, second = GROUPS[-1], GROUPS[-2]
+    whole_groups = (total + largest - 1 - second) // largest
+
+    def whole_group(step, carry):
+        group(step * largest, largest)
         return carry
 
-    lax.fori_loop(0, 2 * half // GROUP, group, jnp.int32(0))
+    lax.fori_loop(0, whole_groups, whole_group, jnp.int32(0))
+    rest = total - whole_groups * largest
+    for below, size in zip((0, *GROUPS), GROUPS[:-1]):
+
+        @pl.when((rest > below) & (rest <= size))
+        def _():
+            group(whole_groups * largest, size)
 
     real = (bands[0][...] + bands[1][...]) * scale
     imag = (bands[2][...] + bands[3][...]) * scale
@@ -325,6 +349,7 @@
             pltpu.VMEM(out_table.shape[1:], jnp.float32),
             pltpu.VMEM((portion, columns), jnp.float32),
             pltpu.SMEM((2 * own_lines.shape[0], LANES), jnp.float32),
+            pltpu.SMEM((2 * own_lines.shape[0] + GROUPS[-1],), jnp.int32),
             pltpu.SemaphoreType.DMA((5,)),
             pltpu.SemaphoreType.DMA((PARTS,)),
             band,

time: 19.1 us -> 18.5 us (0.969)
  Pallas kernels: 8.59 us -> 8.04 us
    pallas_call x1, Pallas kernels: 4.2 us -> 3.71 us  [adjoint(): pl.pallas_call(functools.partial(adjoint_kernel, n_src), out_shape=jax.Sh...]
  transfers between devices with their start and end apart: 4 -> 4, of which waited for: 2 -> 2; matrix products, arithmetic and copies ran while one was open for 1% -> 2% of each run, Pallas kernels for 4% -> 4%
where the time goes in v7:
time: 18.5 us; the launch traced here: 18.4 us
  Pallas kernels  8.04 us (43%)
  starting transfers between devices  7.66 us (41%)
  waiting for transfers between devices  1.71 us (9%)
  between operations  0.72 us (4%)
  other arithmetic  0.27 us (1%)
    ppermute x4, starting transfers between devices, swapped(): return lax.ppermute(array, axes, turn)  7.66 us
    pallas_call x1, Pallas kernels, adjoint(): pl.pallas_call(functools.partial(adjoint_kernel, n_src), out_shape=jax.Sh...  3.71 us
    pallas_call x1, Pallas kernels, forward(): pl.pallas_call(forward_kernel, out_shape=(jax.ShapeDtypeStruct((SUMS + 8,...  3.59 us
    ppermute x4, waiting for transfers between devices, swapped(): return lax.ppermute(array, axes, turn)  1.71 us
    pallas_call x1, Pallas kernels, slot_lines(): pl.pallas_call(lines_kernel, out_shape=jax.ShapeDtypeStruct((count, LANES...  0.75 us
  transfers between devices with their start and end apart: 4, of which 2 were waited for; matrix products, arithmetic and copies ran while one was open for 2% of the time, Pallas kernels for 4%

profile of v7, /device:TPU:0, one launch (start us, length us, event | category | flops | bytes accessed | tf_op | source)
XLA Modules:
  0.0 18.4 jit_solution(5348073465796956829)
XLA Ops:
  0.0 0.0 copy-start
  0.0 0.0 copy-start.4
  0.0 0.0 copy-start.1
  0.0 0.0 copy-start.2
  0.0 0.0 copy-start.3
  0.0 3.6 %forward.1 = (f32[392,128]{1,0:T(8,128)S(1)}, s32[1,9]{1,0:T(1,128)S(1)}) custom-call(bf16[512,2048]{1,0:T(8,128)(2,1)} %mask.1, bf16[512,2048]{1,0:T(8,128)(2,1)} %cotangent.1, bf16[2048,384]{1,0:T(8,128)(2,1)} %constant.28.clone.col_table, bf16[4,384,512]{2,1,0:T(8,128)(2,1)} %constant.29.clone.row_table), custom_call_target="tpu_custom_call" | custom-call | flops 805306368 | bytes 6291456 | tf_op jit(solution)/shard_map/forward/pallas_call | solution.py:130
  3.6 0.5 %collective-permute-start = (f32[392,128]{1,0:T(8,128)S(1)}, f32[392,128]{1,0:T(8,128)S(1)}, u32[]{:S(2)}, u32[]{:S(2)}) collective-permute-start(f32[392,128]{1,0:T(8,128)S(1)} %get-tuple-element.7), channel_id=1, source_target_pairs={{0,1},{1,0},{2,3},{3,2},{4,5},{5,4},{6,7},{7,6},{8,9},{9,8},{10,11... | collective-permute-start | bytes 602120 | tf_op jit(solution)/shard_map/ppermute | solution.py:385
  4.8 0.0 copy-done.4
  4.8 0.1 add_add_fusion.1
  4.9 2.6 %collective-permute-start.2 = (s32[1,9]{1,0:T(1,128)S(1)}, s32[1,9]{1,0:T(1,128)S(1)}, u32[]{:S(2)}, u32[]{:S(2)}) collective-permute-start(s32[1,9]{1,0:T(1,128)S(1)} %add_add_fusion.1), channel_id=1, source_target_pairs={{0,4},{1,5},{2,6},{3,7},{4,0},{5,1},{6,2},{7,3},{8,12},{9,13},{10,... | collective-permute-start | bytes 116 | tf_op jit(solution)/shard_map/ppermute | solution.py:385
  7.5 0.0 collective-permute-done
  7.5 1.6 %collective-permute-start.1 = (f32[392,128]{1,0:T(8,128)S(1)}, f32[392,128]{1,0:T(8,128)S(1)}, u32[]{:S(2)}, u32[]{:S(2)}) collective-permute-start(f32[392,128]{1,0:T(8,128)S(1)} %add.77.own), channel_id=1, source_target_pairs={{0,2},{1,3},{2,0},{3,1},{4,6},{5,7},{6,4},{7,5},{8,10},{9,11},{10,... | collective-permute-start | bytes 602120 | tf_op jit(solution)/shard_map/ppermute | solution.py:385
  9.1 0.0 collective-permute-done.2
  9.1 0.0 copy-done.1
  9.1 0.0 copy-done.2
  9.1 0.7 %slot_lines.1.own_lines = f32[16,128]{1,0:T(8,128)S(1)} custom-call(s32[2,9]{1,0:T(2,128)S(1)} %add_add_fusion.ids, s32[2,12288]{1,0:T(2,128)S(1)} %bitcast.8, f32[96,128]{1,0:T(8,128)S(1)} %bitcast.9), custom_call_target="tpu_custom_call" | custom-call | flops 1 | bytes 1 | tf_op jit(solution)/shard_map/slot_lines/pallas_call | solution.py:183
  9.9 3.0 %collective-permute-start.3 = (f32[16,128]{1,0:T(8,128)S(1)}, f32[16,128]{1,0:T(8,128)S(1)}, u32[]{:S(2)}, u32[]{:S(2)}) collective-permute-start(f32[16,128]{1,0:T(8,128)S(1)} %slot_lines.1.own_lines), channel_id=1, source_target_pairs={{0,8},{1,9},{2,10},{3,11},{4,12},{5,13},{6,14},{7,15},{8,0},{9,1},... | collective-permute-start | bytes 24584 | tf_op jit(solution)/shard_map/ppermute | solution.py:385
  12.9 0.0 copy-done.3
  12.9 0.1 cosine_select_fusion
  13.0 1.5 %collective-permute-done.3.other_lines = f32[16,128]{1,0:T(8,128)S(1)} collective-permute-done((f32[16,128]{1,0:T(8,128)S(1)}, f32[16,128]{1,0:T(8,128)S(1)}, u32[]{:S(2)}, u32[]{:S(2)}) %collective-permute-start.3) | collective-permute-done | bytes 8224 | tf_op jit(solution)/shard_map/ppermute | solution.py:385
  14.5 0.2 %collective-permute-done.1.other = f32[392,128]{1,0:T(8,128)S(1)} collective-permute-done((f32[392,128]{1,0:T(8,128)S(1)}, f32[392,128]{1,0:T(8,128)S(1)}, u32[]{:S(2)}, u32[]{:S(2)}) %collective-permute-start.1) | collective-permute-done | bytes 200736 | tf_op jit(solution)/shard_map/ppermute | solution.py:385
  14.7 0.0 copy-done
  14.7 3.7 %adjoint.1 = f32[1,128,2048]{2,1,0:T(8,128)} custom-call(f32[392,128]{1,0:T(8,128)S(1)} %add.77.own, f32[392,128]{1,0:T(8,128)S(1)} %collective-permute-done.1.other, f32[16,128]{1,0:T(8,128)S(1)} %slot_lines.1.own_lines, f32[16,128]{1,0:T(8,128)S(1)} %collective-permute-done.3.other_lines, f32[128,128]{1,0:T(8,128)S(1)} %select_maximum_fusion.pupil, ...), custom_call_target="tpu_custom_call" | custom-call | flops 268435456 | bytes 4194304 | tf_op jit(solution)/shard_map/adjoint/pallas_call | solution.py:338
  (6 shorter events, 0.1 us)
Async XLA Ops:
  0.0 14.7 %copy-start = (bf16[768,256]{1,0:T(8,128)(2,1)S(1)}, bf16[768,256]{1,0:T(8,128)(2,1)}, u32[]{:S(2)}) copy-start(bf16[768,256]{1,0:T(8,128)(2,1)} %constant.30.clone.table) | copy-start | bytes 1179652
  0.0 4.8 %copy-start.4 = (s32[1,8]{1,0:T(1,128)S(1)}, s32[1,8]{1,0:T(1,128)}, u32[]{:S(2)}) copy-start(s32[1,8]{1,0:T(1,128)} %param.17) | copy-start | bytes 100
  0.0 9.1 %copy-start.1 = (s32[12288,2]{0,1:T(2,128)S(1)}, s32[12288,2]{0,1:T(2,128)}, u32[]{:S(2)}) copy-start(s32[12288,2]{0,1:T(2,128)} %param.16) | copy-start | bytes 294916
  0.0 9.1 %copy-start.2 = (f32[12288]{0:T(1024)S(1)}, f32[12288]{0:T(1024)}, u32[]{:S(2)}) copy-start(f32[12288]{0:T(1024)} %param.15) | copy-start | bytes 147460
  0.0 12.8 %copy-start.3 = (f32[64,64]{1,0:T(8,128)S(1)}, f32[64,64]{1,0:T(8,128)}, u32[]{:S(2)}) copy-start(f32[64,64]{1,0:T(8,128)} %param.14) | copy-start | bytes 49156
  3.6 3.9 %collective-permute-start = (f32[392,128]{1,0:T(8,128)S(1)}, f32[392,128]{1,0:T(8,128)S(1)}, u32[]{:S(2)}, u32[]{:S(2)}) collective-permute-start(f32[392,128]{1,0:T(8,128)S(1)} %get-tuple-element.7), channel_id=1, source_target_pairs={{0,1},{1,0},{2,3},{3,2},{4,5},{5,4},{6,7},{7,6},{8,9},{9,8},{10,11... | collective-permute-start | bytes 602120 | tf_op jit(solution)/shard_map/ppermute | solution.py:385
  4.9 4.2 %collective-permute-start.2 = (s32[1,9]{1,0:T(1,128)S(1)}, s32[1,9]{1,0:T(1,128)S(1)}, u32[]{:S(2)}, u32[]{:S(2)}) collective-permute-start(s32[1,9]{1,0:T(1,128)S(1)} %add_add_fusion.1), channel_id=1, source_target_pairs={{0,4},{1,5},{2,6},{3,7},{4,0},{5,1},{6,2},{7,3},{8,12},{9,13},{10,... | collective-permute-start | bytes 116 | tf_op jit(solution)/shard_map/ppermute | solution.py:385
  7.5 7.2 %collective-permute-start.1 = (f32[392,128]{1,0:T(8,128)S(1)}, f32[392,128]{1,0:T(8,128)S(1)}, u32[]{:S(2)}, u32[]{:S(2)}) collective-permute-start(f32[392,128]{1,0:T(8,128)S(1)} %add.77.own), channel_id=1, source_target_pairs={{0,2},{1,3},{2,0},{3,1},{4,6},{5,7},{6,4},{7,5},{8,10},{9,11},{10,... | collective-permute-start | bytes 602120 | tf_op jit(solution)/shard_map/ppermute | solution.py:385
  9.9 4.6 %collective-permute-start.3 = (f32[16,128]{1,0:T(8,128)S(1)}, f32[16,128]{1,0:T(8,128)S(1)}, u32[]{:S(2)}, u32[]{:S(2)}) collective-permute-start(f32[16,128]{1,0:T(8,128)S(1)} %slot_lines.1.own_lines), channel_id=1, source_target_pairs={{0,8},{1,9},{2,10},{3,11},{4,12},{5,13},{6,14},{7,15},{8,0},{9,1},... | collective-permute-start | bytes 24584 | tf_op jit(solution)/shard_map/ppermute | solution.py:385

commit v8 on v7

--- a/solution.py
+++ b/solution.py
@@ -18,6 +18,7 @@
 GRID = 128
 CHUNKS = (1, 1, 2, 2, 1, 1)
 GROUPS = (16, 20, 24, 32)
+PACK = 4
 OX, OY, FACTOR, COUNT = range(4)
 PARTS = 4
 LANES = 128
@@ -194,16 +195,15 @@
 def adjoint_kernel(
     n_src, own, other, own_lines, other_lines, pupil, table, col_table, out_table,
     result,
-    spec_real, spec_imag, image, table_v, col_v, out_v, result_v, lines, used, sems, out_sems, *bands,
+    spec_real, spec_imag, image, col_v, out_v, result_v, lines, used, sems, out_sems, *bands,
 ):
     place = lax.axis_index("tile") * n_src + lax.axis_index("src")
-    grid_copy = pltpu.make_async_copy(table, table_v, sems.at[0])
     out_copy = pltpu.make_async_copy(out_table.at[place], out_v, sems.at[1])
     col_copy = pltpu.make_async_copy(col_table, col_v, sems.at[2])
     half = own_lines.shape[0]
     own_copy = pltpu.make_async_copy(own_lines, lines.at[pl.ds(0, half), :], sems.at[3])
-    other_copy = pltpu.make_async_copy(other_lines, lines.at[pl.ds(half, half), :], sems.at[4])
-    for copy in (own_copy, other_copy, grid_copy, out_copy, col_copy):
+    other_copy = pltpu.make_async_copy(other_lines, lines.at[pl.ds(half, half), :], sems.at[0])
+    for copy in (own_copy, other_copy, out_copy, col_copy):
         copy.start()
 
     scale = 1.0 / math.sqrt(TILE_ROWS * COLS)
@@ -228,71 +228,67 @@
 
     blocks = 2 * half // SLOTS
     total = lax.fori_loop(0, blocks, add, jnp.int32(0), unroll=blocks <= 8)
-    grid_copy.wait()
 
     def group(first, size):
-        starts, pupils, amplitudes = [], [], []
-        for slot in range(size):
-            place = first + slot
-            index = used[place]
-            factor = jnp.where(place < total, lines[index, FACTOR], 0.0)
-            offset_x = lines[index, OX].astype(jnp.int32)
-            offset_y = lines[index, OY].astype(jnp.int32)
-            real = pltpu.roll(pupil[:PUPIL, :], offset_x, 1)
-            imag = pltpu.roll(pupil[PUPIL:, :], offset_x, 1)
-            rows = pl.ds(offset_y, PUPIL)
-            amp_real = real * spec_real[rows, :] - imag * spec_imag[rows, :]
-            amp_imag = real * spec_imag[rows, :] + imag * spec_real[rows, :]
-            starts.append(offset_y)
-            pupils.append((real, imag, factor))
-            amplitudes.append(jnp.concatenate([amp_real, amp_imag], 1).astype(jnp.bfloat16))
-        halfway = dot(jnp.concatenate(amplitudes, 0), table_v[COLS_IN, :]).astype(jnp.bfloat16)
-        halfway = jnp.concatenate(
-            [
-                jnp.concatenate(
-                    [
-                        halfway[slot * PUPIL : (slot + 1) * PUPIL, :GRID],
-                        halfway[slot * PUPIL : (slot + 1) * PUPIL, GRID:],
-                    ],
-                    0,
-                )
-                for slot in range(size)
-            ],
-            1,
-        )
-        rows_in = table_v[ROWS_IN, :]
-        rows_in = jnp.concatenate([rows_in[:, : 2 * PUPIL], rows_in[:, 2 * PUPIL :]], 0)
-        field = dot(rows_in, halfway)
-        field_grad = jnp.concatenate(
-            [
-                (field[:, slot * GRID : (slot + 1) * GRID] * image[...]).astype(jnp.bfloat16)
-                for slot in range(size)
-            ],
-            1,
-        )
-        back = dot(table_v[ROWS_OUT, :], field_grad).astype(jnp.bfloat16)
-        back = jnp.concatenate(
-            [
-                jnp.concatenate(
-                    [
-                        back[:PUPIL, slot * GRID : (slot + 1) * GRID],
-                        back[PUPIL:, slot * GRID : (slot + 1) * GRID],
-                    ],
-                    1,
-                )
-                for slot in range(size)
-            ],
-            0,
-        )
-        grad = dot(back, table_v[COLS_OUT, :])
-        for slot in range(size):
-            real, imag, factor = pupils[slot]
-            grad_real = grad[slot * PUPIL : (slot + 1) * PUPIL, :BAND] * factor
-            grad_imag = grad[slot * PUPIL : (slot + 1) * PUPIL, BAND:] * factor
-            rows = pl.ds(starts[slot], PUPIL)
-            band_real, band_imag = bands[slot % 2], bands[2 + slot % 2]
-            band_real[rows, :] = band_real[rows, :] + (real * grad_real + imag * grad_imag)
-            band_imag[rows, :] = band_imag[rows, :] + (real * grad_imag - imag * grad_real)
+        held = [None] * (size // PACK)
+        slots = [None] * (size // PACK)
+
+        def amplitude(pack):
+            slots[pack], parts = [], []
+            for slot in range(PACK):
+                place = first + pack * PACK + slot
+                index = used[place]
+                factor = jnp.where(place < total, lines[index, FACTOR], 0.0)
+                offset_x = lines[index, OX].astype(jnp.int32)
+                rows = pl.ds(lines[index, OY].astype(jnp.int32), PUPIL)
+                real = pltpu.roll(pupil[:PUPIL, :], offset_x, 1)
+                imag = pltpu.roll(pupil[PUPIL:, :], offset_x, 1)
+                amp_real = real * spec_real[rows, :] - imag * spec_imag[rows, :]
+                amp_imag = real * spec_imag[rows, :] + imag * spec_real[rows, :]
+                slots[pack].append((rows, real, imag, factor))
+                parts.append(jnp.concatenate([amp_real, amp_imag], 1).astype(jnp.bfloat16))
+            held[pack] = jnp.concatenate(parts, 0)
+
+        def halfway(pack):
+            found = dot(held[pack], table[COLS_IN, :]).astype(jnp.bfloat16)
+            parts = []
+            for slot in range(PACK):
+                block = found[slot * PUPIL : (slot + 1) * PUPIL, :]
+                parts.append(jnp.concatenate([block[:, :GRID], block[:, GRID:]], 0))
+            held[pack] = jnp.concatenate(parts, 1)
+
+        def field_grad(pack):
+            rows_in = table[ROWS_IN, :]
+            rows_in = jnp.concatenate([rows_in[:, : 2 * PUPIL], rows_in[:, 2 * PUPIL :]], 0)
+            field = dot(rows_in, held[pack])
+            parts = []
+            for slot in range(PACK):
+                block = field[:, slot * GRID : (slot + 1) * GRID]
+                parts.append((block * image[...]).astype(jnp.bfloat16))
+            held[pack] = jnp.concatenate(parts, 1)
+
+        def back(pack):
+            found = dot(table[ROWS_OUT, :], held[pack]).astype(jnp.bfloat16)
+            parts = []
+            for slot in range(PACK):
+                block = found[:, slot * GRID : (slot + 1) * GRID]
+                parts.append(jnp.concatenate([block[:PUPIL], block[PUPIL:]], 1))
+            held[pack] = jnp.concatenate(parts, 0)
+
+        def gradient(pack):
+            grad = dot(held[pack], table[COLS_OUT, :])
+            for slot, (rows, real, imag, factor) in enumerate(slots[pack]):
+                block = grad[slot * PUPIL : (slot + 1) * PUPIL, :] * factor
+                grad_real, grad_imag = block[:, :BAND], block[:, BAND:]
+                band_real, band_imag = bands[slot % 2], bands[2 + slot % 2]
+                band_real[rows, :] = band_real[rows, :] + (real * grad_real + imag * grad_imag)
+                band_imag[rows, :] = band_imag[rows, :] + (real * grad_imag - imag * grad_real)
+
+        stages = (amplitude, halfway, field_grad, back, gradient)
+        for step in range(len(held) + len(stages) - 1):
+            for late, stage in reversed(list(enumerate(stages))):
+                if 0 <= step - late < len(held):
+                    stage(step - late)
 
     largest, second = GROUPS[-1], GROUPS[-2]
     whole_groups = (total + largest - 1 - second) // largest
@@ -338,19 +334,18 @@
     return pl.pallas_call(
         functools.partial(adjoint_kernel, n_src),
         out_shape=jax.ShapeDtypeStruct((1, portion, columns), jnp.float32),
-        in_specs=[VMEM] * 5 + [HBM] * 3,
+        in_specs=[VMEM] * 6 + [HBM] * 2,
         out_specs=HBM,
         scratch_shapes=[
             band,
             band,
             pltpu.VMEM((2 * GRID, GRID), jnp.float32),
-            pltpu.VMEM(table.shape, jnp.bfloat16),
             pltpu.VMEM(col_table.shape, jnp.bfloat16),
             pltpu.VMEM(out_table.shape[1:], jnp.float32),
             pltpu.VMEM((portion, columns), jnp.float32),
             pltpu.SMEM((2 * own_lines.shape[0], LANES), jnp.float32),
             pltpu.SMEM((2 * own_lines.shape[0] + GROUPS[-1],), jnp.int32),
-            pltpu.SemaphoreType.DMA((5,)),
+            pltpu.SemaphoreType.DMA((4,)),
             pltpu.SemaphoreType.DMA((PARTS,)),
             band,
             band,

time: 18.5 us -> 18.7 us (1.011)
  transfers between devices with their start and end apart: 4 -> 4, of which waited for: 2 -> 2; matrix products, arithmetic and copies ran while one was open for 2% -> 1% of each run, Pallas kernels for 4% -> 4%
where the time goes in v8:
time: 18.7 us; the launch traced here: 18.6 us
  Pallas kernels  8.19 us (44%)
  starting transfers between devices  7.66 us (41%)
  waiting for transfers between devices  1.71 us (9%)
  between operations  0.72 us (4%)
  other arithmetic  0.27 us (1%)
    ppermute x4, starting transfers between devices, swapped(): return lax.ppermute(array, axes, turn)  7.66 us
    pallas_call x1, Pallas kernels, adjoint(): pl.pallas_call(functools.partial(adjoint_kernel, n_src), out_shape=jax.Sh...  3.85 us
    pallas_call x1, Pallas kernels, forward(): pl.pallas_call(forward_kernel, out_shape=(jax.ShapeDtypeStruct((SUMS + 8,...  3.59 us
    ppermute x4, waiting for transfers between devices, swapped(): return lax.ppermute(array, axes, turn)  1.71 us
    pallas_call x1, Pallas kernels, slot_lines(): pl.pallas_call(lines_kernel, out_shape=jax.ShapeDtypeStruct((count, LANES...  0.75 us
  transfers between devices with their start and end apart: 4, of which 2 were waited for; matrix products, arithmetic and copies ran while one was open for 1% of the time, Pallas kernels for 4%

profile of v8, /device:TPU:0, one launch (start us, length us, event | category | flops | bytes accessed | tf_op | source)
XLA Modules:
  0.0 18.6 jit_solution(2997950986994069932)
XLA Ops:
  0.0 0.0 copy-start
  0.0 0.0 copy-start.4
  0.0 0.0 copy-start.1
  0.0 0.0 copy-start.2
  0.0 0.0 copy-start.3
  0.0 3.6 %forward.1 = (f32[392,128]{1,0:T(8,128)S(1)}, s32[1,9]{1,0:T(1,128)S(1)}) custom-call(bf16[512,2048]{1,0:T(8,128)(2,1)} %mask.1, bf16[512,2048]{1,0:T(8,128)(2,1)} %cotangent.1, bf16[2048,384]{1,0:T(8,128)(2,1)} %constant.28.clone.col_table, bf16[4,384,512]{2,1,0:T(8,128)(2,1)} %constant.29.clone.row_table), custom_call_target="tpu_custom_call" | custom-call | flops 805306368 | bytes 6291456 | tf_op jit(solution)/shard_map/forward/pallas_call | solution.py:131
  3.6 0.5 %collective-permute-start = (f32[392,128]{1,0:T(8,128)S(1)}, f32[392,128]{1,0:T(8,128)S(1)}, u32[]{:S(2)}, u32[]{:S(2)}) collective-permute-start(f32[392,128]{1,0:T(8,128)S(1)} %get-tuple-element.7), channel_id=1, source_target_pairs={{0,1},{1,0},{2,3},{3,2},{4,5},{5,4},{6,7},{7,6},{8,9},{9,8},{10,11... | collective-permute-start | bytes 602120 | tf_op jit(solution)/shard_map/ppermute | solution.py:380
  4.8 0.0 copy-done.4
  4.8 0.1 add_add_fusion.1
  4.9 2.6 %collective-permute-start.2 = (s32[1,9]{1,0:T(1,128)S(1)}, s32[1,9]{1,0:T(1,128)S(1)}, u32[]{:S(2)}, u32[]{:S(2)}) collective-permute-start(s32[1,9]{1,0:T(1,128)S(1)} %add_add_fusion.1), channel_id=1, source_target_pairs={{0,4},{1,5},{2,6},{3,7},{4,0},{5,1},{6,2},{7,3},{8,12},{9,13},{10,... | collective-permute-start | bytes 116 | tf_op jit(solution)/shard_map/ppermute | solution.py:380
  7.5 0.0 collective-permute-done
  7.5 1.6 %collective-permute-start.1 = (f32[392,128]{1,0:T(8,128)S(1)}, f32[392,128]{1,0:T(8,128)S(1)}, u32[]{:S(2)}, u32[]{:S(2)}) collective-permute-start(f32[392,128]{1,0:T(8,128)S(1)} %add.77.own), channel_id=1, source_target_pairs={{0,2},{1,3},{2,0},{3,1},{4,6},{5,7},{6,4},{7,5},{8,10},{9,11},{10,... | collective-permute-start | bytes 602120 | tf_op jit(solution)/shard_map/ppermute | solution.py:380
  9.1 0.0 collective-permute-done.2
  9.1 0.0 copy-done.1
  9.1 0.0 copy-done.2
  9.1 0.7 %slot_lines.1.own_lines = f32[16,128]{1,0:T(8,128)S(1)} custom-call(s32[2,9]{1,0:T(2,128)S(1)} %add_add_fusion.ids, s32[2,12288]{1,0:T(2,128)S(1)} %bitcast.8, f32[96,128]{1,0:T(8,128)S(1)} %bitcast.9), custom_call_target="tpu_custom_call" | custom-call | flops 1 | bytes 1 | tf_op jit(solution)/shard_map/slot_lines/pallas_call | solution.py:184
  9.9 3.0 %collective-permute-start.3 = (f32[16,128]{1,0:T(8,128)S(1)}, f32[16,128]{1,0:T(8,128)S(1)}, u32[]{:S(2)}, u32[]{:S(2)}) collective-permute-start(f32[16,128]{1,0:T(8,128)S(1)} %slot_lines.1.own_lines), channel_id=1, source_target_pairs={{0,8},{1,9},{2,10},{3,11},{4,12},{5,13},{6,14},{7,15},{8,0},{9,1},... | collective-permute-start | bytes 24584 | tf_op jit(solution)/shard_map/ppermute | solution.py:380
  12.9 0.0 copy-done.3
  12.9 0.1 cosine_select_fusion
  13.0 1.5 %collective-permute-done.3.other_lines = f32[16,128]{1,0:T(8,128)S(1)} collective-permute-done((f32[16,128]{1,0:T(8,128)S(1)}, f32[16,128]{1,0:T(8,128)S(1)}, u32[]{:S(2)}, u32[]{:S(2)}) %collective-permute-start.3) | collective-permute-done | bytes 8224 | tf_op jit(solution)/shard_map/ppermute | solution.py:380
  14.5 0.2 %collective-permute-done.1.other = f32[392,128]{1,0:T(8,128)S(1)} collective-permute-done((f32[392,128]{1,0:T(8,128)S(1)}, f32[392,128]{1,0:T(8,128)S(1)}, u32[]{:S(2)}, u32[]{:S(2)}) %collective-permute-start.1) | collective-permute-done | bytes 200736 | tf_op jit(solution)/shard_map/ppermute | solution.py:380
  14.7 0.0 copy-done
  14.7 3.9 %adjoint.1 = f32[1,128,2048]{2,1,0:T(8,128)} custom-call(f32[392,128]{1,0:T(8,128)S(1)} %add.77.own, f32[392,128]{1,0:T(8,128)S(1)} %collective-permute-done.1.other, f32[16,128]{1,0:T(8,128)S(1)} %slot_lines.1.own_lines, f32[16,128]{1,0:T(8,128)S(1)} %collective-permute-done.3.other_lines, f32[128,128]{1,0:T(8,128)S(1)} %select_maximum_fusion.pupil, ...), custom_call_target="tpu_custom_call" | custom-call | flops 268435456 | bytes 4194304 | tf_op jit(solution)/shard_map/adjoint/pallas_call | solution.py:334
  (6 shorter events, 0.1 us)
Async XLA Ops:
  0.0 14.7 %copy-start = (bf16[768,256]{1,0:T(8,128)(2,1)S(1)}, bf16[768,256]{1,0:T(8,128)(2,1)}, u32[]{:S(2)}) copy-start(bf16[768,256]{1,0:T(8,128)(2,1)} %constant.30.clone.table) | copy-start | bytes 1179652
  0.0 4.8 %copy-start.4 = (s32[1,8]{1,0:T(1,128)S(1)}, s32[1,8]{1,0:T(1,128)}, u32[]{:S(2)}) copy-start(s32[1,8]{1,0:T(1,128)} %param.17) | copy-start | bytes 100
  0.0 9.1 %copy-start.1 = (s32[12288,2]{0,1:T(2,128)S(1)}, s32[12288,2]{0,1:T(2,128)}, u32[]{:S(2)}) copy-start(s32[12288,2]{0,1:T(2,128)} %param.16) | copy-start | bytes 294916
  0.0 9.1 %copy-start.2 = (f32[12288]{0:T(1024)S(1)}, f32[12288]{0:T(1024)}, u32[]{:S(2)}) copy-start(f32[12288]{0:T(1024)} %param.15) | copy-start | bytes 147460
  0.0 12.8 %copy-start.3 = (f32[64,64]{1,0:T(8,128)S(1)}, f32[64,64]{1,0:T(8,128)}, u32[]{:S(2)}) copy-start(f32[64,64]{1,0:T(8,128)} %param.14) | copy-start | bytes 49156
  3.6 3.9 %collective-permute-start = (f32[392,128]{1,0:T(8,128)S(1)}, f32[392,128]{1,0:T(8,128)S(1)}, u32[]{:S(2)}, u32[]{:S(2)}) collective-permute-start(f32[392,128]{1,0:T(8,128)S(1)} %get-tuple-element.7), channel_id=1, source_target_pairs={{0,1},{1,0},{2,3},{3,2},{4,5},{5,4},{6,7},{7,6},{8,9},{9,8},{10,11... | collective-permute-start | bytes 602120 | tf_op jit(solution)/shard_map/ppermute | solution.py:380
  4.9 4.2 %collective-permute-start.2 = (s32[1,9]{1,0:T(1,128)S(1)}, s32[1,9]{1,0:T(1,128)S(1)}, u32[]{:S(2)}, u32[]{:S(2)}) collective-permute-start(s32[1,9]{1,0:T(1,128)S(1)} %add_add_fusion.1), channel_id=1, source_target_pairs={{0,4},{1,5},{2,6},{3,7},{4,0},{5,1},{6,2},{7,3},{8,12},{9,13},{10,... | collective-permute-start | bytes 116 | tf_op jit(solution)/shard_map/ppermute | solution.py:380
  7.5 7.2 %collective-permute-start.1 = (f32[392,128]{1,0:T(8,128)S(1)}, f32[392,128]{1,0:T(8,128)S(1)}, u32[]{:S(2)}, u32[]{:S(2)}) collective-permute-start(f32[392,128]{1,0:T(8,128)S(1)} %add.77.own), channel_id=1, source_target_pairs={{0,2},{1,3},{2,0},{3,1},{4,6},{5,7},{6,4},{7,5},{8,10},{9,11},{10,... | collective-permute-start | bytes 602120 | tf_op jit(solution)/shard_map/ppermute | solution.py:380
  9.9 4.6 %collective-permute-start.3 = (f32[16,128]{1,0:T(8,128)S(1)}, f32[16,128]{1,0:T(8,128)S(1)}, u32[]{:S(2)}, u32[]{:S(2)}) collective-permute-start(f32[16,128]{1,0:T(8,128)S(1)} %slot_lines.1.own_lines), channel_id=1, source_target_pairs={{0,8},{1,9},{2,10},{3,11},{4,12},{5,13},{6,14},{7,15},{8,0},{9,1},... | collective-permute-start | bytes 24584 | tf_op jit(solution)/shard_map/ppermute | solution.py:380

commit v9 on v8

--- a/solution.py
+++ b/solution.py
@@ -18,7 +18,7 @@
 GRID = 128
 CHUNKS = (1, 1, 2, 2, 1, 1)
 GROUPS = (16, 20, 24, 32)
-PACK = 4
+PACKS = 2
 OX, OY, FACTOR, COUNT = range(4)
 PARTS = 4
 LANES = 128
@@ -230,13 +230,13 @@
     total = lax.fori_loop(0, blocks, add, jnp.int32(0), unroll=blocks <= 8)
 
     def group(first, size):
-        held = [None] * (size // PACK)
-        slots = [None] * (size // PACK)
+        width = size // PACKS
+        held, slots = [None] * PACKS, [None] * PACKS
 
         def amplitude(pack):
             slots[pack], parts = [], []
-            for slot in range(PACK):
-                place = first + pack * PACK + slot
+            for slot in range(width):
+                place = first + pack * width + slot
                 index = used[place]
                 factor = jnp.where(place < total, lines[index, FACTOR], 0.0)
                 offset_x = lines[index, OX].astype(jnp.int32)
@@ -252,7 +252,7 @@
         def halfway(pack):
             found = dot(held[pack], table[COLS_IN, :]).astype(jnp.bfloat16)
             parts = []
-            for slot in range(PACK):
+            for slot in range(width):
                 block = found[slot * PUPIL : (slot + 1) * PUPIL, :]
                 parts.append(jnp.concatenate([block[:, :GRID], block[:, GRID:]], 0))
             held[pack] = jnp.concatenate(parts, 1)
@@ -262,7 +262,7 @@
             rows_in = jnp.concatenate([rows_in[:, : 2 * PUPIL], rows_in[:, 2 * PUPIL :]], 0)
             field = dot(rows_in, held[pack])
             parts = []
-            for slot in range(PACK):
+            for slot in range(width):
                 block = field[:, slot * GRID : (slot + 1) * GRID]
                 parts.append((block * image[...]).astype(jnp.bfloat16))
             held[pack] = jnp.concatenate(parts, 1)
@@ -270,7 +270,7 @@
         def back(pack):
             found = dot(table[ROWS_OUT, :], held[pack]).astype(jnp.bfloat16)
             parts = []
-            for slot in range(PACK):
+            for slot in range(width):
                 block = found[:, slot * GRID : (slot + 1) * GRID]
                 parts.append(jnp.concatenate([block[:PUPIL], block[PUPIL:]], 1))
             held[pack] = jnp.concatenate(parts, 0)
@@ -285,9 +285,9 @@
                 band_imag[rows, :] = band_imag[rows, :] + (real * grad_imag - imag * grad_real)
 
         stages = (amplitude, halfway, field_grad, back, gradient)
-        for step in range(len(held) + len(stages) - 1):
+        for step in range(PACKS + len(stages) - 1):
             for late, stage in reversed(list(enumerate(stages))):
-                if 0 <= step - late < len(held):
+                if 0 <= step - late < PACKS:
                     stage(step - late)
 
     largest, second = GROUPS[-1], GROUPS[-2]

time: 18.7 us -> 18.5 us (0.989)
  transfers between devices with their start and end apart: 4 -> 4, of which waited for: 2 -> 2; matrix products, arithmetic and copies ran while one was open for 1% -> 2% of each run, Pallas kernels for 4% -> 4%
where the time goes in v9:
time: 18.5 us
  Pallas kernels  8.1 us (44%)
  starting transfers between devices  7.66 us (41%)
  waiting for transfers between devices  1.71 us (9%)
  between operations  0.72 us (4%)
  other arithmetic  0.27 us (1%)
    ppermute x4, starting transfers between devices, swapped(): return lax.ppermute(array, axes, turn)  7.66 us
    pallas_call x1, Pallas kernels, adjoint(): pl.pallas_call(functools.partial(adjoint_kernel, n_src), out_shape=jax.Sh...  3.76 us
    pallas_call x1, Pallas kernels, forward(): pl.pallas_call(forward_kernel, out_shape=(jax.ShapeDtypeStruct((SUMS + 8,...  3.59 us
    ppermute x4, waiting for transfers between devices, swapped(): return lax.ppermute(array, axes, turn)  1.71 us
    pallas_call x1, Pallas kernels, slot_lines(): pl.pallas_call(lines_kernel, out_shape=jax.ShapeDtypeStruct((count, LANES...  0.75 us
  transfers between devices with their start and end apart: 4, of which 2 were waited for; matrix products, arithmetic and copies ran while one was open for 2% of the time, Pallas kernels for 4%

profile of v9, /device:TPU:0, one launch (start us, length us, event | category | flops | bytes accessed | tf_op | source)
XLA Modules:
  0.0 18.5 jit_solution(14503313126894103339)
XLA Ops:
  0.0 0.0 copy-start
  0.0 0.0 copy-start.4
  0.0 0.0 copy-start.1
  0.0 0.0 copy-start.2
  0.0 0.0 copy-start.3
  0.0 3.6 %forward.1 = (f32[392,128]{1,0:T(8,128)S(1)}, s32[1,9]{1,0:T(1,128)S(1)}) custom-call(bf16[512,2048]{1,0:T(8,128)(2,1)} %mask.1, bf16[512,2048]{1,0:T(8,128)(2,1)} %cotangent.1, bf16[2048,384]{1,0:T(8,128)(2,1)} %constant.28.clone.col_table, bf16[4,384,512]{2,1,0:T(8,128)(2,1)} %constant.29.clone.row_table), custom_call_target="tpu_custom_call" | custom-call | flops 805306368 | bytes 6291456 | tf_op jit(solution)/shard_map/forward/pallas_call | solution.py:131
  3.6 0.5 %collective-permute-start = (f32[392,128]{1,0:T(8,128)S(1)}, f32[392,128]{1,0:T(8,128)S(1)}, u32[]{:S(2)}, u32[]{:S(2)}) collective-permute-start(f32[392,128]{1,0:T(8,128)S(1)} %get-tuple-element.7), channel_id=1, source_target_pairs={{0,1},{1,0},{2,3},{3,2},{4,5},{5,4},{6,7},{7,6},{8,9},{9,8},{10,11... | collective-permute-start | bytes 602120 | tf_op jit(solution)/shard_map/ppermute | solution.py:380
  4.8 0.0 copy-done.4
  4.8 0.1 add_add_fusion.1
  4.9 2.6 %collective-permute-start.2 = (s32[1,9]{1,0:T(1,128)S(1)}, s32[1,9]{1,0:T(1,128)S(1)}, u32[]{:S(2)}, u32[]{:S(2)}) collective-permute-start(s32[1,9]{1,0:T(1,128)S(1)} %add_add_fusion.1), channel_id=1, source_target_pairs={{0,4},{1,5},{2,6},{3,7},{4,0},{5,1},{6,2},{7,3},{8,12},{9,13},{10,... | collective-permute-start | bytes 116 | tf_op jit(solution)/shard_map/ppermute | solution.py:380
  7.5 0.0 collective-permute-done
  7.5 1.6 %collective-permute-start.1 = (f32[392,128]{1,0:T(8,128)S(1)}, f32[392,128]{1,0:T(8,128)S(1)}, u32[]{:S(2)}, u32[]{:S(2)}) collective-permute-start(f32[392,128]{1,0:T(8,128)S(1)} %add.77.own), channel_id=1, source_target_pairs={{0,2},{1,3},{2,0},{3,1},{4,6},{5,7},{6,4},{7,5},{8,10},{9,11},{10,... | collective-permute-start | bytes 602120 | tf_op jit(solution)/shard_map/ppermute | solution.py:380
  9.1 0.0 collective-permute-done.2
  9.1 0.0 copy-done.1
  9.1 0.0 copy-done.2
  9.1 0.7 %slot_lines.1.own_lines = f32[16,128]{1,0:T(8,128)S(1)} custom-call(s32[2,9]{1,0:T(2,128)S(1)} %add_add_fusion.ids, s32[2,12288]{1,0:T(2,128)S(1)} %bitcast.8, f32[96,128]{1,0:T(8,128)S(1)} %bitcast.9), custom_call_target="tpu_custom_call" | custom-call | flops 1 | bytes 1 | tf_op jit(solution)/shard_map/slot_lines/pallas_call | solution.py:184
  9.9 3.0 %collective-permute-start.3 = (f32[16,128]{1,0:T(8,128)S(1)}, f32[16,128]{1,0:T(8,128)S(1)}, u32[]{:S(2)}, u32[]{:S(2)}) collective-permute-start(f32[16,128]{1,0:T(8,128)S(1)} %slot_lines.1.own_lines), channel_id=1, source_target_pairs={{0,8},{1,9},{2,10},{3,11},{4,12},{5,13},{6,14},{7,15},{8,0},{9,1},... | collective-permute-start | bytes 24584 | tf_op jit(solution)/shard_map/ppermute | solution.py:380
  12.9 0.0 copy-done.3
  12.9 0.1 cosine_select_fusion
  13.0 1.5 %collective-permute-done.3.other_lines = f32[16,128]{1,0:T(8,128)S(1)} collective-permute-done((f32[16,128]{1,0:T(8,128)S(1)}, f32[16,128]{1,0:T(8,128)S(1)}, u32[]{:S(2)}, u32[]{:S(2)}) %collective-permute-start.3) | collective-permute-done | bytes 8224 | tf_op jit(solution)/shard_map/ppermute | solution.py:380
  14.5 0.2 %collective-permute-done.1.other = f32[392,128]{1,0:T(8,128)S(1)} collective-permute-done((f32[392,128]{1,0:T(8,128)S(1)}, f32[392,128]{1,0:T(8,128)S(1)}, u32[]{:S(2)}, u32[]{:S(2)}) %collective-permute-start.1) | collective-permute-done | bytes 200736 | tf_op jit(solution)/shard_map/ppermute | solution.py:380
  14.7 0.0 copy-done
  14.7 3.8 %adjoint.1 = f32[1,128,2048]{2,1,0:T(8,128)} custom-call(f32[392,128]{1,0:T(8,128)S(1)} %add.77.own, f32[392,128]{1,0:T(8,128)S(1)} %collective-permute-done.1.other, f32[16,128]{1,0:T(8,128)S(1)} %slot_lines.1.own_lines, f32[16,128]{1,0:T(8,128)S(1)} %collective-permute-done.3.other_lines, f32[128,128]{1,0:T(8,128)S(1)} %select_maximum_fusion.pupil, ...), custom_call_target="tpu_custom_call" | custom-call | flops 268435456 | bytes 4194304 | tf_op jit(solution)/shard_map/adjoint/pallas_call | solution.py:334
  (6 shorter events, 0.1 us)
Async XLA Ops:
  0.0 14.7 %copy-start = (bf16[768,256]{1,0:T(8,128)(2,1)S(1)}, bf16[768,256]{1,0:T(8,128)(2,1)}, u32[]{:S(2)}) copy-start(bf16[768,256]{1,0:T(8,128)(2,1)} %constant.30.clone.table) | copy-start | bytes 1179652
  0.0 4.8 %copy-start.4 = (s32[1,8]{1,0:T(1,128)S(1)}, s32[1,8]{1,0:T(1,128)}, u32[]{:S(2)}) copy-start(s32[1,8]{1,0:T(1,128)} %param.17) | copy-start | bytes 100
  0.0 9.1 %copy-start.1 = (s32[12288,2]{0,1:T(2,128)S(1)}, s32[12288,2]{0,1:T(2,128)}, u32[]{:S(2)}) copy-start(s32[12288,2]{0,1:T(2,128)} %param.16) | copy-start | bytes 294916
  0.0 9.1 %copy-start.2 = (f32[12288]{0:T(1024)S(1)}, f32[12288]{0:T(1024)}, u32[]{:S(2)}) copy-start(f32[12288]{0:T(1024)} %param.15) | copy-start | bytes 147460
  0.0 12.8 %copy-start.3 = (f32[64,64]{1,0:T(8,128)S(1)}, f32[64,64]{1,0:T(8,128)}, u32[]{:S(2)}) copy-start(f32[64,64]{1,0:T(8,128)} %param.14) | copy-start | bytes 49156
  3.6 3.9 %collective-permute-start = (f32[392,128]{1,0:T(8,128)S(1)}, f32[392,128]{1,0:T(8,128)S(1)}, u32[]{:S(2)}, u32[]{:S(2)}) collective-permute-start(f32[392,128]{1,0:T(8,128)S(1)} %get-tuple-element.7), channel_id=1, source_target_pairs={{0,1},{1,0},{2,3},{3,2},{4,5},{5,4},{6,7},{7,6},{8,9},{9,8},{10,11... | collective-permute-start | bytes 602120 | tf_op jit(solution)/shard_map/ppermute | solution.py:380
  4.9 4.2 %collective-permute-start.2 = (s32[1,9]{1,0:T(1,128)S(1)}, s32[1,9]{1,0:T(1,128)S(1)}, u32[]{:S(2)}, u32[]{:S(2)}) collective-permute-start(s32[1,9]{1,0:T(1,128)S(1)} %add_add_fusion.1), channel_id=1, source_target_pairs={{0,4},{1,5},{2,6},{3,7},{4,0},{5,1},{6,2},{7,3},{8,12},{9,13},{10,... | collective-permute-start | bytes 116 | tf_op jit(solution)/shard_map/ppermute | solution.py:380
  7.5 7.2 %collective-permute-start.1 = (f32[392,128]{1,0:T(8,128)S(1)}, f32[392,128]{1,0:T(8,128)S(1)}, u32[]{:S(2)}, u32[]{:S(2)}) collective-permute-start(f32[392,128]{1,0:T(8,128)S(1)} %add.77.own), channel_id=1, source_target_pairs={{0,2},{1,3},{2,0},{3,1},{4,6},{5,7},{6,4},{7,5},{8,10},{9,11},{10,... | collective-permute-start | bytes 602120 | tf_op jit(solution)/shard_map/ppermute | solution.py:380
  9.9 4.6 %collective-permute-start.3 = (f32[16,128]{1,0:T(8,128)S(1)}, f32[16,128]{1,0:T(8,128)S(1)}, u32[]{:S(2)}, u32[]{:S(2)}) collective-permute-start(f32[16,128]{1,0:T(8,128)S(1)} %slot_lines.1.own_lines), channel_id=1, source_target_pairs={{0,8},{1,9},{2,10},{3,11},{4,12},{5,13},{6,14},{7,15},{8,0},{9,1},... | collective-permute-start | bytes 24584 | tf_op jit(solution)/shard_map/ppermute | solution.py:380

commit v10 on v9

--- a/solution.py
+++ b/solution.py
@@ -16,11 +16,11 @@
 PUPIL = 64
 SLOTS = 8
 GRID = 128
-CHUNKS = (1, 1, 2, 2, 1, 1)
+CHUNKS = (2, 3, 3)
 GROUPS = (16, 20, 24, 32)
-PACKS = 2
+PACKS = 1
 OX, OY, FACTOR, COUNT = range(4)
-PARTS = 4
+PARTS = 8
 LANES = 128
 SUMS = 2 * BAND + GRID
 GRANT = 53 * 1024 * 1024

time: 18.5 us -> 18.7 us (1.011); the launches traced: 18.5 us -> 18.4 us
    pallas_call x1, Pallas kernels: 3.76 us -> 3.51 us  [adjoint(): pl.pallas_call(functools.partial(adjoint_kernel, n_src), out_shape=jax.Sh...]
    pallas_call x1, Pallas kernels: 3.59 us -> 3.8 us  [forward(): pl.pallas_call(forward_kernel, out_shape=(jax.ShapeDtypeStruct((SUMS + 8,...]
where the time goes in v10:
time: 18.7 us; the launch traced here: 18.4 us
  Pallas kernels  8.06 us (43%)
  starting transfers between devices  7.64 us (41%)
  waiting for transfers between devices  1.72 us (9%)
  between operations  0.72 us (4%)
  other arithmetic  0.27 us (1%)
    ppermute x4, starting transfers between devices, swapped(): return lax.ppermute(array, axes, turn)  7.64 us
    pallas_call x1, Pallas kernels, forward(): pl.pallas_call(forward_kernel, out_shape=(jax.ShapeDtypeStruct((SUMS + 8,...  3.8 us
    pallas_call x1, Pallas kernels, adjoint(): pl.pallas_call(functools.partial(adjoint_kernel, n_src), out_shape=jax.Sh...  3.51 us
    ppermute x4, waiting for transfers between devices, swapped(): return lax.ppermute(array, axes, turn)  1.72 us
    pallas_call x1, Pallas kernels, slot_lines(): pl.pallas_call(lines_kernel, out_shape=jax.ShapeDtypeStruct((count, LANES...  0.75 us
  transfers between devices with their start and end apart: 4, of which 2 were waited for; matrix products, arithmetic and copies ran while one was open for 2% of the time, Pallas kernels for 4%

profile of v10, /device:TPU:0, one launch (start us, length us, event | category | flops | bytes accessed | tf_op | source)
XLA Modules:
  0.0 18.4 jit_solution(608142195744911623)
XLA Ops:
  0.0 0.0 copy-start
  0.0 0.0 copy-start.4
  0.0 0.0 copy-start.1
  0.0 0.0 copy-start.2
  0.0 0.0 copy-start.3
  0.0 3.8 %forward.1 = (f32[392,128]{1,0:T(8,128)S(1)}, s32[1,9]{1,0:T(1,128)S(1)}) custom-call(bf16[512,2048]{1,0:T(8,128)(2,1)} %mask.1, bf16[512,2048]{1,0:T(8,128)(2,1)} %cotangent.1, bf16[2048,384]{1,0:T(8,128)(2,1)} %constant.28.clone.col_table, bf16[4,384,512]{2,1,0:T(8,128)(2,1)} %constant.29.clone.row_table), custom_call_target="tpu_custom_call" | custom-call | flops 805306368 | bytes 6291456 | tf_op jit(solution)/shard_map/forward/pallas_call | solution.py:131
  3.8 0.5 %collective-permute-start = (f32[392,128]{1,0:T(8,128)S(1)}, f32[392,128]{1,0:T(8,128)S(1)}, u32[]{:S(2)}, u32[]{:S(2)}) collective-permute-start(f32[392,128]{1,0:T(8,128)S(1)} %get-tuple-element.7), channel_id=1, source_target_pairs={{0,1},{1,0},{2,3},{3,2},{4,5},{5,4},{6,7},{7,6},{8,9},{9,8},{10,11... | collective-permute-start | bytes 602120 | tf_op jit(solution)/shard_map/ppermute | solution.py:380
  5.0 0.0 copy-done.4
  5.0 0.1 add_add_fusion.1
  5.1 2.6 %collective-permute-start.2 = (s32[1,9]{1,0:T(1,128)S(1)}, s32[1,9]{1,0:T(1,128)S(1)}, u32[]{:S(2)}, u32[]{:S(2)}) collective-permute-start(s32[1,9]{1,0:T(1,128)S(1)} %add_add_fusion.1), channel_id=1, source_target_pairs={{0,4},{1,5},{2,6},{3,7},{4,0},{5,1},{6,2},{7,3},{8,12},{9,13},{10,... | collective-permute-start | bytes 116 | tf_op jit(solution)/shard_map/ppermute | solution.py:380
  7.7 0.0 collective-permute-done
  7.7 1.6 %collective-permute-start.1 = (f32[392,128]{1,0:T(8,128)S(1)}, f32[392,128]{1,0:T(8,128)S(1)}, u32[]{:S(2)}, u32[]{:S(2)}) collective-permute-start(f32[392,128]{1,0:T(8,128)S(1)} %add.77.own), channel_id=1, source_target_pairs={{0,2},{1,3},{2,0},{3,1},{4,6},{5,7},{6,4},{7,5},{8,10},{9,11},{10,... | collective-permute-start | bytes 602120 | tf_op jit(solution)/shard_map/ppermute | solution.py:380
  9.3 0.0 collective-permute-done.2
  9.3 0.0 copy-done.1
  9.3 0.0 copy-done.2
  9.3 0.7 %slot_lines.1.own_lines = f32[16,128]{1,0:T(8,128)S(1)} custom-call(s32[2,9]{1,0:T(2,128)S(1)} %add_add_fusion.ids, s32[2,12288]{1,0:T(2,128)S(1)} %bitcast.8, f32[96,128]{1,0:T(8,128)S(1)} %bitcast.9), custom_call_target="tpu_custom_call" | custom-call | flops 1 | bytes 1 | tf_op jit(solution)/shard_map/slot_lines/pallas_call | solution.py:184
  10.1 3.0 %collective-permute-start.3 = (f32[16,128]{1,0:T(8,128)S(1)}, f32[16,128]{1,0:T(8,128)S(1)}, u32[]{:S(2)}, u32[]{:S(2)}) collective-permute-start(f32[16,128]{1,0:T(8,128)S(1)} %slot_lines.1.own_lines), channel_id=1, source_target_pairs={{0,8},{1,9},{2,10},{3,11},{4,12},{5,13},{6,14},{7,15},{8,0},{9,1},... | collective-permute-start | bytes 24584 | tf_op jit(solution)/shard_map/ppermute | solution.py:380
  13.0 0.0 copy-done.3
  13.0 0.1 cosine_select_fusion
  13.2 1.5 %collective-permute-done.3.other_lines = f32[16,128]{1,0:T(8,128)S(1)} collective-permute-done((f32[16,128]{1,0:T(8,128)S(1)}, f32[16,128]{1,0:T(8,128)S(1)}, u32[]{:S(2)}, u32[]{:S(2)}) %collective-permute-start.3) | collective-permute-done | bytes 8224 | tf_op jit(solution)/shard_map/ppermute | solution.py:380
  14.7 0.2 %collective-permute-done.1.other = f32[392,128]{1,0:T(8,128)S(1)} collective-permute-done((f32[392,128]{1,0:T(8,128)S(1)}, f32[392,128]{1,0:T(8,128)S(1)}, u32[]{:S(2)}, u32[]{:S(2)}) %collective-permute-start.1) | collective-permute-done | bytes 200736 | tf_op jit(solution)/shard_map/ppermute | solution.py:380
  14.9 0.0 copy-done
  14.9 3.5 %adjoint.1 = f32[1,128,2048]{2,1,0:T(8,128)} custom-call(f32[392,128]{1,0:T(8,128)S(1)} %add.77.own, f32[392,128]{1,0:T(8,128)S(1)} %collective-permute-done.1.other, f32[16,128]{1,0:T(8,128)S(1)} %slot_lines.1.own_lines, f32[16,128]{1,0:T(8,128)S(1)} %collective-permute-done.3.other_lines, f32[128,128]{1,0:T(8,128)S(1)} %select_maximum_fusion.pupil, ...), custom_call_target="tpu_custom_call" | custom-call | flops 268435456 | bytes 4194304 | tf_op jit(solution)/shard_map/adjoint/pallas_call | solution.py:334
  (6 shorter events, 0.1 us)
Async XLA Ops:
  0.0 14.9 %copy-start = (bf16[768,256]{1,0:T(8,128)(2,1)S(1)}, bf16[768,256]{1,0:T(8,128)(2,1)}, u32[]{:S(2)}) copy-start(bf16[768,256]{1,0:T(8,128)(2,1)} %constant.30.clone.table) | copy-start | bytes 1179652
  0.0 5.0 %copy-start.4 = (s32[1,8]{1,0:T(1,128)S(1)}, s32[1,8]{1,0:T(1,128)}, u32[]{:S(2)}) copy-start(s32[1,8]{1,0:T(1,128)} %param.17) | copy-start | bytes 100
  0.0 9.3 %copy-start.1 = (s32[12288,2]{0,1:T(2,128)S(1)}, s32[12288,2]{0,1:T(2,128)}, u32[]{:S(2)}) copy-start(s32[12288,2]{0,1:T(2,128)} %param.16) | copy-start | bytes 294916
  0.0 9.3 %copy-start.2 = (f32[12288]{0:T(1024)S(1)}, f32[12288]{0:T(1024)}, u32[]{:S(2)}) copy-start(f32[12288]{0:T(1024)} %param.15) | copy-start | bytes 147460
  0.0 13.0 %copy-start.3 = (f32[64,64]{1,0:T(8,128)S(1)}, f32[64,64]{1,0:T(8,128)}, u32[]{:S(2)}) copy-start(f32[64,64]{1,0:T(8,128)} %param.14) | copy-start | bytes 49156
  3.8 3.9 %collective-permute-start = (f32[392,128]{1,0:T(8,128)S(1)}, f32[392,128]{1,0:T(8,128)S(1)}, u32[]{:S(2)}, u32[]{:S(2)}) collective-permute-start(f32[392,128]{1,0:T(8,128)S(1)} %get-tuple-element.7), channel_id=1, source_target_pairs={{0,1},{1,0},{2,3},{3,2},{4,5},{5,4},{6,7},{7,6},{8,9},{9,8},{10,11... | collective-permute-start | bytes 602120 | tf_op jit(solution)/shard_map/ppermute | solution.py:380
  5.1 4.2 %collective-permute-start.2 = (s32[1,9]{1,0:T(1,128)S(1)}, s32[1,9]{1,0:T(1,128)S(1)}, u32[]{:S(2)}, u32[]{:S(2)}) collective-permute-start(s32[1,9]{1,0:T(1,128)S(1)} %add_add_fusion.1), channel_id=1, source_target_pairs={{0,4},{1,5},{2,6},{3,7},{4,0},{5,1},{6,2},{7,3},{8,12},{9,13},{10,... | collective-permute-start | bytes 116 | tf_op jit(solution)/shard_map/ppermute | solution.py:380
  7.7 7.2 %collective-permute-start.1 = (f32[392,128]{1,0:T(8,128)S(1)}, f32[392,128]{1,0:T(8,128)S(1)}, u32[]{:S(2)}, u32[]{:S(2)}) collective-permute-start(f32[392,128]{1,0:T(8,128)S(1)} %add.77.own), channel_id=1, source_target_pairs={{0,2},{1,3},{2,0},{3,1},{4,6},{5,7},{6,4},{7,5},{8,10},{9,11},{10,... | collective-permute-start | bytes 602120 | tf_op jit(solution)/shard_map/ppermute | solution.py:380
  10.1 4.6 %collective-permute-start.3 = (f32[16,128]{1,0:T(8,128)S(1)}, f32[16,128]{1,0:T(8,128)S(1)}, u32[]{:S(2)}, u32[]{:S(2)}) collective-permute-start(f32[16,128]{1,0:T(8,128)S(1)} %slot_lines.1.own_lines), channel_id=1, source_target_pairs={{0,8},{1,9},{2,10},{3,11},{4,12},{5,13},{6,14},{7,15},{8,0},{9,1},... | collective-permute-start | bytes 24584 | tf_op jit(solution)/shard_map/ppermute | solution.py:380

commit v11 on v7

--- a/solution.py
+++ b/solution.py
@@ -16,8 +16,9 @@
 PUPIL = 64
 SLOTS = 8
 GRID = 128
-CHUNKS = (1, 1, 2, 2, 1, 1)
+CHUNKS = (1,) * 8
 GROUPS = (16, 20, 24, 32)
+STEP = 8
 OX, OY, FACTOR, COUNT = range(4)
 PARTS = 4
 LANES = 128
@@ -194,27 +195,28 @@
 def adjoint_kernel(
     n_src, own, other, own_lines, other_lines, pupil, table, col_table, out_table,
     result,
-    spec_real, spec_imag, image, table_v, col_v, out_v, result_v, lines, used, sems, out_sems, *bands,
+    spec_real, spec_imag, image, band_real, band_imag, col_v, out_v, result_v, lines, used, sems, out_sems,
 ):
     place = lax.axis_index("tile") * n_src + lax.axis_index("src")
-    grid_copy = pltpu.make_async_copy(table, table_v, sems.at[0])
     out_copy = pltpu.make_async_copy(out_table.at[place], out_v, sems.at[1])
     col_copy = pltpu.make_async_copy(col_table, col_v, sems.at[2])
     half = own_lines.shape[0]
     own_copy = pltpu.make_async_copy(own_lines, lines.at[pl.ds(0, half), :], sems.at[3])
-    other_copy = pltpu.make_async_copy(other_lines, lines.at[pl.ds(half, half), :], sems.at[4])
-    for copy in (own_copy, other_copy, grid_copy, out_copy, col_copy):
+    other_copy = pltpu.make_async_copy(other_lines, lines.at[pl.ds(half, half), :], sems.at[0])
+    for copy in (own_copy, other_copy, out_copy, col_copy):
         copy.start()
 
     scale = 1.0 / math.sqrt(TILE_ROWS * COLS)
     whole = own[:SUMS, :] + other[:SUMS, :]
     spec = (whole[: 2 * BAND] * scale).astype(jnp.bfloat16).astype(jnp.float32)
-    spec_real[...] = spec[:BAND]
-    spec_imag[...] = spec[BAND:]
+    for step in range(STEP):
+        rows = BAND - STEP if step else BAND
+        spec_real[step, :rows, :] = spec[step : step + rows]
+        spec_imag[step, :rows, :] = spec[BAND + step : BAND + step + rows]
+    band_real[...] = jnp.zeros_like(band_real)
+    band_imag[...] = jnp.zeros_like(band_imag)
     image[:GRID, :] = whole[2 * BAND :]
     image[GRID:, :] = whole[2 * BAND :]
-    for band in bands:
-        band[...] = jnp.zeros_like(band)
     for slot in range(2 * half + GROUPS[-1]):
         used[slot] = jnp.int32(0)
     own_copy.wait()
@@ -228,71 +230,47 @@
 
     blocks = 2 * half // SLOTS
     total = lax.fori_loop(0, blocks, add, jnp.int32(0), unroll=blocks <= 8)
-    grid_copy.wait()
 
     def group(first, size):
-        starts, pupils, amplitudes = [], [], []
+        slots, amplitudes = [], []
         for slot in range(size):
             place = first + slot
             index = used[place]
             factor = jnp.where(place < total, lines[index, FACTOR], 0.0)
             offset_x = lines[index, OX].astype(jnp.int32)
             offset_y = lines[index, OY].astype(jnp.int32)
+            copy = offset_y % STEP
+            rows = pl.ds(pl.multiple_of(offset_y - copy, STEP), PUPIL)
             real = pltpu.roll(pupil[:PUPIL, :], offset_x, 1)
             imag = pltpu.roll(pupil[PUPIL:, :], offset_x, 1)
-            rows = pl.ds(offset_y, PUPIL)
-            amp_real = real * spec_real[rows, :] - imag * spec_imag[rows, :]
-            amp_imag = real * spec_imag[rows, :] + imag * spec_real[rows, :]
-            starts.append(offset_y)
-            pupils.append((real, imag, factor))
+            here_real, here_imag = spec_real[copy, rows, :], spec_imag[copy, rows, :]
+            amp_real = real * here_real - imag * here_imag
+            amp_imag = real * here_imag + imag * here_real
+            slots.append((copy, rows, real, imag, factor))
             amplitudes.append(jnp.concatenate([amp_real, amp_imag], 1).astype(jnp.bfloat16))
-        halfway = dot(jnp.concatenate(amplitudes, 0), table_v[COLS_IN, :]).astype(jnp.bfloat16)
-        halfway = jnp.concatenate(
-            [
-                jnp.concatenate(
-                    [
-                        halfway[slot * PUPIL : (slot + 1) * PUPIL, :GRID],
-                        halfway[slot * PUPIL : (slot + 1) * PUPIL, GRID:],
-                    ],
-                    0,
-                )
-                for slot in range(size)
-            ],
-            1,
-        )
-        rows_in = table_v[ROWS_IN, :]
+        halfway = dot(jnp.concatenate(amplitudes, 0), table[COLS_IN, :]).astype(jnp.bfloat16)
+        parts = []
+        for slot in range(size):
+            block = halfway[slot * PUPIL : (slot + 1) * PUPIL, :]
+            parts.append(jnp.concatenate([block[:, :GRID], block[:, GRID:]], 0))
+        rows_in = table[ROWS_IN, :]
         rows_in = jnp.concatenate([rows_in[:, : 2 * PUPIL], rows_in[:, 2 * PUPIL :]], 0)
-        field = dot(rows_in, halfway)
-        field_grad = jnp.concatenate(
-            [
-                (field[:, slot * GRID : (slot + 1) * GRID] * image[...]).astype(jnp.bfloat16)
-                for slot in range(size)
-            ],
-            1,
-        )
-        back = dot(table_v[ROWS_OUT, :], field_grad).astype(jnp.bfloat16)
-        back = jnp.concatenate(
-            [
-                jnp.concatenate(
-                    [
-                        back[:PUPIL, slot * GRID : (slot + 1) * GRID],
-                        back[PUPIL:, slot * GRID : (slot + 1) * GRID],
-                    ],
-                    1,
-                )
-                for slot in range(size)
-            ],
-            0,
-        )
-        grad = dot(back, table_v[COLS_OUT, :])
+        field = dot(rows_in, jnp.concatenate(parts, 1))
+        parts = []
         for slot in range(size):
-            real, imag, factor = pupils[slot]
-            grad_real = grad[slot * PUPIL : (slot + 1) * PUPIL, :BAND] * factor
-            grad_imag = grad[slot * PUPIL : (slot + 1) * PUPIL, BAND:] * factor
-            rows = pl.ds(starts[slot], PUPIL)
-            band_real, band_imag = bands[slot % 2], bands[2 + slot % 2]
-            band_real[rows, :] = band_real[rows, :] + (real * grad_real + imag * grad_imag)
-            band_imag[rows, :] = band_imag[rows, :] + (real * grad_imag - imag * grad_real)
+            block = field[:, slot * GRID : (slot + 1) * GRID]
+            parts.append((block * image[...]).astype(jnp.bfloat16))
+        back = dot(table[ROWS_OUT, :], jnp.concatenate(parts, 1)).astype(jnp.bfloat16)
+        parts = []
+        for slot in range(size):
+            block = back[:, slot * GRID : (slot + 1) * GRID]
+            parts.append(jnp.concatenate([block[:PUPIL], block[PUPIL:]], 1))
+        grad = dot(jnp.concatenate(parts, 0), table[COLS_OUT, :])
+        for slot, (copy, rows, real, imag, factor) in enumerate(slots):
+            block = grad[slot * PUPIL : (slot + 1) * PUPIL, :] * factor
+            grad_real, grad_imag = block[:, :BAND], block[:, BAND:]
+            band_real[copy, rows, :] += real * grad_real + imag * grad_imag
+            band_imag[copy, rows, :] += real * grad_imag - imag * grad_real
 
     largest, second = GROUPS[-1], GROUPS[-2]
     whole_groups = (total + largest - 1 - second) // largest
@@ -309,8 +287,11 @@
         def _():
             group(whole_groups * largest, size)
 
-    real = (bands[0][...] + bands[1][...]) * scale
-    imag = (bands[2][...] + bands[3][...]) * scale
+    for band in (band_real, band_imag):
+        for step in range(1, STEP):
+            rows = BAND - STEP
+            band[0, step : step + rows, :] += band[step, :rows, :]
+    real, imag = band_real[0] * scale, band_imag[0] * scale
     left = jnp.concatenate(
         [jnp.concatenate([real, imag], 1), jnp.concatenate([imag, -real], 1)], 0
     ).astype(jnp.bfloat16)
@@ -334,28 +315,25 @@
 def adjoint(own, other, own_lines, other_lines, pupil, table, col_table, out_table, n_src):
     portion = out_table.shape[1]
     columns = col_table.shape[1]
-    band = pltpu.VMEM((BAND, BAND), jnp.float32)
+    band = pltpu.VMEM((STEP, BAND, BAND), jnp.float32)
     return pl.pallas_call(
         functools.partial(adjoint_kernel, n_src),
         out_shape=jax.ShapeDtypeStruct((1, portion, columns), jnp.float32),
-        in_specs=[VMEM] * 5 + [HBM] * 3,
+        in_specs=[VMEM] * 6 + [HBM] * 2,
         out_specs=HBM,
         scratch_shapes=[
             band,
             band,
             pltpu.VMEM((2 * GRID, GRID), jnp.float32),
-            pltpu.VMEM(table.shape, jnp.bfloat16),
+            band,
+            band,
             pltpu.VMEM(col_table.shape, jnp.bfloat16),
             pltpu.VMEM(out_table.shape[1:], jnp.float32),
             pltpu.VMEM((portion, columns), jnp.float32),
             pltpu.SMEM((2 * own_lines.shape[0], LANES), jnp.float32),
             pltpu.SMEM((2 * own_lines.shape[0] + GROUPS[-1],), jnp.int32),
-            pltpu.SemaphoreType.DMA((5,)),
+            pltpu.SemaphoreType.DMA((4,)),
             pltpu.SemaphoreType.DMA((PARTS,)),
-            band,
-            band,
-            band,
-            band,
         ],
         compiler_params=pltpu.CompilerParams(vmem_limit_bytes=GRANT),
         cost_estimate=pl.CostEstimate(

time: 18.5 us -> 18.4 us (level)
  no operation moved by 1% of the time
where the time goes in v11:
time: 18.4 us; the launch traced here: 18.3 us
  Pallas kernels  7.9 us (43%)
  starting transfers between devices  7.65 us (42%)
  waiting for transfers between devices  1.71 us (9%)
  between operations  0.72 us (4%)
  other arithmetic  0.27 us (1%)
    ppermute x4, starting transfers between devices, swapped(): return lax.ppermute(array, axes, turn)  7.65 us
    pallas_call x1, Pallas kernels, forward(): pl.pallas_call(forward_kernel, out_shape=(jax.ShapeDtypeStruct((SUMS + 8,...  3.59 us
    pallas_call x1, Pallas kernels, adjoint(): pl.pallas_call(functools.partial(adjoint_kernel, n_src), out_shape=jax.Sh...  3.56 us
    ppermute x4, waiting for transfers between devices, swapped(): return lax.ppermute(array, axes, turn)  1.71 us
    pallas_call x1, Pallas kernels, slot_lines(): pl.pallas_call(lines_kernel, out_shape=jax.ShapeDtypeStruct((count, LANES...  0.75 us
  transfers between devices with their start and end apart: 4, of which 2 were waited for; matrix products, arithmetic and copies ran while one was open for 2% of the time, Pallas kernels for 4%

profile of v11, /device:TPU:0, one launch (start us, length us, event | category | flops | bytes accessed | tf_op | source)
XLA Modules:
  0.0 18.3 jit_solution(5718583257701725817)
XLA Ops:
  0.0 0.0 copy-start
  0.0 0.0 copy-start.4
  0.0 0.0 copy-start.1
  0.0 0.0 copy-start.2
  0.0 0.0 copy-start.3
  0.0 3.6 %forward.1 = (f32[392,128]{1,0:T(8,128)S(1)}, s32[1,9]{1,0:T(1,128)S(1)}) custom-call(bf16[512,2048]{1,0:T(8,128)(2,1)} %mask.1, bf16[512,2048]{1,0:T(8,128)(2,1)} %cotangent.1, bf16[2048,384]{1,0:T(8,128)(2,1)} %constant.28.clone.col_table, bf16[4,384,512]{2,1,0:T(8,128)(2,1)} %constant.29.clone.row_table), custom_call_target="tpu_custom_call" | custom-call | flops 805306368 | bytes 6291456 | tf_op jit(solution)/shard_map/forward/pallas_call | solution.py:131
  3.6 0.5 %collective-permute-start = (f32[392,128]{1,0:T(8,128)S(1)}, f32[392,128]{1,0:T(8,128)S(1)}, u32[]{:S(2)}, u32[]{:S(2)}) collective-permute-start(f32[392,128]{1,0:T(8,128)S(1)} %get-tuple-element.7), channel_id=1, source_target_pairs={{0,1},{1,0},{2,3},{3,2},{4,5},{5,4},{6,7},{7,6},{8,9},{9,8},{10,11... | collective-permute-start | bytes 602120 | tf_op jit(solution)/shard_map/ppermute | solution.py:363
  4.8 0.0 copy-done.4
  4.8 0.1 add_add_fusion.1
  4.9 2.6 %collective-permute-start.2 = (s32[1,9]{1,0:T(1,128)S(1)}, s32[1,9]{1,0:T(1,128)S(1)}, u32[]{:S(2)}, u32[]{:S(2)}) collective-permute-start(s32[1,9]{1,0:T(1,128)S(1)} %add_add_fusion.1), channel_id=1, source_target_pairs={{0,4},{1,5},{2,6},{3,7},{4,0},{5,1},{6,2},{7,3},{8,12},{9,13},{10,... | collective-permute-start | bytes 116 | tf_op jit(solution)/shard_map/ppermute | solution.py:363
  7.5 0.0 collective-permute-done
  7.5 1.6 %collective-permute-start.1 = (f32[392,128]{1,0:T(8,128)S(1)}, f32[392,128]{1,0:T(8,128)S(1)}, u32[]{:S(2)}, u32[]{:S(2)}) collective-permute-start(f32[392,128]{1,0:T(8,128)S(1)} %add.77.own), channel_id=1, source_target_pairs={{0,2},{1,3},{2,0},{3,1},{4,6},{5,7},{6,4},{7,5},{8,10},{9,11},{10,... | collective-permute-start | bytes 602120 | tf_op jit(solution)/shard_map/ppermute | solution.py:363
  9.1 0.0 collective-permute-done.2
  9.1 0.0 copy-done.1
  9.1 0.0 copy-done.2
  9.1 0.7 %slot_lines.1.own_lines = f32[16,128]{1,0:T(8,128)S(1)} custom-call(s32[2,9]{1,0:T(2,128)S(1)} %add_add_fusion.ids, s32[2,12288]{1,0:T(2,128)S(1)} %bitcast.8, f32[96,128]{1,0:T(8,128)S(1)} %bitcast.9), custom_call_target="tpu_custom_call" | custom-call | flops 1 | bytes 1 | tf_op jit(solution)/shard_map/slot_lines/pallas_call | solution.py:184
  9.9 3.0 %collective-permute-start.3 = (f32[16,128]{1,0:T(8,128)S(1)}, f32[16,128]{1,0:T(8,128)S(1)}, u32[]{:S(2)}, u32[]{:S(2)}) collective-permute-start(f32[16,128]{1,0:T(8,128)S(1)} %slot_lines.1.own_lines), channel_id=1, source_target_pairs={{0,8},{1,9},{2,10},{3,11},{4,12},{5,13},{6,14},{7,15},{8,0},{9,1},... | collective-permute-start | bytes 24584 | tf_op jit(solution)/shard_map/ppermute | solution.py:363
  12.8 0.0 copy-done.3
  12.8 0.1 cosine_select_fusion
  13.0 1.5 %collective-permute-done.3.other_lines = f32[16,128]{1,0:T(8,128)S(1)} collective-permute-done((f32[16,128]{1,0:T(8,128)S(1)}, f32[16,128]{1,0:T(8,128)S(1)}, u32[]{:S(2)}, u32[]{:S(2)}) %collective-permute-start.3) | collective-permute-done | bytes 8224 | tf_op jit(solution)/shard_map/ppermute | solution.py:363
  14.5 0.2 %collective-permute-done.1.other = f32[392,128]{1,0:T(8,128)S(1)} collective-permute-done((f32[392,128]{1,0:T(8,128)S(1)}, f32[392,128]{1,0:T(8,128)S(1)}, u32[]{:S(2)}, u32[]{:S(2)}) %collective-permute-start.1) | collective-permute-done | bytes 200736 | tf_op jit(solution)/shard_map/ppermute | solution.py:363
  14.7 0.0 copy-done
  14.7 3.6 %adjoint.1 = f32[1,128,2048]{2,1,0:T(8,128)} custom-call(f32[392,128]{1,0:T(8,128)S(1)} %add.77.own, f32[392,128]{1,0:T(8,128)S(1)} %collective-permute-done.1.other, f32[16,128]{1,0:T(8,128)S(1)} %slot_lines.1.own_lines, f32[16,128]{1,0:T(8,128)S(1)} %collective-permute-done.3.other_lines, f32[128,128]{1,0:T(8,128)S(1)} %select_maximum_fusion.pupil, ...), custom_call_target="tpu_custom_call" | custom-call | flops 268435456 | bytes 4194304 | tf_op jit(solution)/shard_map/adjoint/pallas_call | solution.py:319
  (6 shorter events, 0.1 us)
Async XLA Ops:
  0.0 14.7 %copy-start = (bf16[768,256]{1,0:T(8,128)(2,1)S(1)}, bf16[768,256]{1,0:T(8,128)(2,1)}, u32[]{:S(2)}) copy-start(bf16[768,256]{1,0:T(8,128)(2,1)} %constant.30.clone.table) | copy-start | bytes 1179652
  0.0 4.8 %copy-start.4 = (s32[1,8]{1,0:T(1,128)S(1)}, s32[1,8]{1,0:T(1,128)}, u32[]{:S(2)}) copy-start(s32[1,8]{1,0:T(1,128)} %param.17) | copy-start | bytes 100
  0.0 9.1 %copy-start.1 = (s32[12288,2]{0,1:T(2,128)S(1)}, s32[12288,2]{0,1:T(2,128)}, u32[]{:S(2)}) copy-start(s32[12288,2]{0,1:T(2,128)} %param.16) | copy-start | bytes 294916
  0.0 9.1 %copy-start.2 = (f32[12288]{0:T(1024)S(1)}, f32[12288]{0:T(1024)}, u32[]{:S(2)}) copy-start(f32[12288]{0:T(1024)} %param.15) | copy-start | bytes 147460
  0.0 12.8 %copy-start.3 = (f32[64,64]{1,0:T(8,128)S(1)}, f32[64,64]{1,0:T(8,128)}, u32[]{:S(2)}) copy-start(f32[64,64]{1,0:T(8,128)} %param.14) | copy-start | bytes 49156
  3.6 3.9 %collective-permute-start = (f32[392,128]{1,0:T(8,128)S(1)}, f32[392,128]{1,0:T(8,128)S(1)}, u32[]{:S(2)}, u32[]{:S(2)}) collective-permute-start(f32[392,128]{1,0:T(8,128)S(1)} %get-tuple-element.7), channel_id=1, source_target_pairs={{0,1},{1,0},{2,3},{3,2},{4,5},{5,4},{6,7},{7,6},{8,9},{9,8},{10,11... | collective-permute-start | bytes 602120 | tf_op jit(solution)/shard_map/ppermute | solution.py:363
  4.9 4.2 %collective-permute-start.2 = (s32[1,9]{1,0:T(1,128)S(1)}, s32[1,9]{1,0:T(1,128)S(1)}, u32[]{:S(2)}, u32[]{:S(2)}) collective-permute-start(s32[1,9]{1,0:T(1,128)S(1)} %add_add_fusion.1), channel_id=1, source_target_pairs={{0,4},{1,5},{2,6},{3,7},{4,0},{5,1},{6,2},{7,3},{8,12},{9,13},{10,... | collective-permute-start | bytes 116 | tf_op jit(solution)/shard_map/ppermute | solution.py:363
  7.5 7.2 %collective-permute-start.1 = (f32[392,128]{1,0:T(8,128)S(1)}, f32[392,128]{1,0:T(8,128)S(1)}, u32[]{:S(2)}, u32[]{:S(2)}) collective-permute-start(f32[392,128]{1,0:T(8,128)S(1)} %add.77.own), channel_id=1, source_target_pairs={{0,2},{1,3},{2,0},{3,1},{4,6},{5,7},{6,4},{7,5},{8,10},{9,11},{10,... | collective-permute-start | bytes 602120 | tf_op jit(solution)/shard_map/ppermute | solution.py:363
  9.9 4.6 %collective-permute-start.3 = (f32[16,128]{1,0:T(8,128)S(1)}, f32[16,128]{1,0:T(8,128)S(1)}, u32[]{:S(2)}, u32[]{:S(2)}) collective-permute-start(f32[16,128]{1,0:T(8,128)S(1)} %slot_lines.1.own_lines), channel_id=1, source_target_pairs={{0,8},{1,9},{2,10},{3,11},{4,12},{5,13},{6,14},{7,15},{8,0},{9,1},... | collective-permute-start | bytes 24584 | tf_op jit(solution)/shard_map/ppermute | solution.py:363

commit v12 on v7

--- a/solution.py
+++ b/solution.py
@@ -16,12 +16,14 @@
 PUPIL = 64
 SLOTS = 8
 GRID = 128
-CHUNKS = (1, 1, 2, 2, 1, 1)
+CHUNKS = (1,) * 8
 GROUPS = (16, 20, 24, 32)
 OX, OY, FACTOR, COUNT = range(4)
 PARTS = 4
 LANES = 128
 SUMS = 2 * BAND + GRID
+HALF = SUMS // 2
+ZEROS = 8
 GRANT = 53 * 1024 * 1024
 
 VMEM = pl.BlockSpec(memory_space=pltpu.VMEM)
@@ -88,8 +90,8 @@
 
 def forward_kernel(
     mask, cotangent, col_table, row_table,
-    partial, zeros,
-    mask_v, cot_v, col_v, row_v, sems,
+    keep, send, zeros,
+    halves, mask_v, cot_v, col_v, row_v, sems,
 ):
     columns = mask.shape[1]
     ends = np.cumsum(CHUNKS) * (columns // sum(CHUNKS))
@@ -118,10 +120,21 @@
 
     row_copy.wait()
     blocks = dot(row_v[: 2 * BAND, :], mask_part.astype(jnp.bfloat16))
-    partial[:BAND, :] = blocks[:BAND, :BAND] + blocks[BAND:, BAND:]
-    partial[BAND : 2 * BAND, :] = blocks[:BAND, BAND:] - blocks[BAND:, :BAND]
-    partial[2 * BAND : SUMS, :] = dot(row_v[2 * BAND :, :], cot_part.astype(jnp.bfloat16))
-    partial[SUMS:, :] = jnp.zeros((8, BAND), jnp.float32)
+    image = dot(row_v[2 * BAND :, :], cot_part.astype(jnp.bfloat16))
+    sums = jnp.concatenate(
+        [
+            blocks[:BAND, :BAND] + blocks[BAND:, BAND:],
+            blocks[:BAND, BAND:] - blocks[BAND:, :BAND],
+            image,
+        ],
+        0,
+    )
+    rest = jnp.zeros((ZEROS, BAND), jnp.float32)
+    for half in range(2):
+        halves[half] = jnp.concatenate([sums[half * HALF : (half + 1) * HALF], rest], 0)
+    own_half = tile % 2
+    keep[...] = halves[own_half]
+    send[...] = halves[1 - own_half]
     zeros[...] = jnp.zeros_like(zeros)
 
 
@@ -130,12 +143,14 @@
     return pl.pallas_call(
         forward_kernel,
         out_shape=(
-            jax.ShapeDtypeStruct((SUMS + 8, BAND), jnp.float32),
+            jax.ShapeDtypeStruct((HALF + ZEROS, BAND), jnp.float32),
+            jax.ShapeDtypeStruct((HALF + ZEROS, BAND), jnp.float32),
             jax.ShapeDtypeStruct((1, SLOTS + 1), jnp.int32),
         ),
         in_specs=[HBM] * 4,
-        out_specs=(VMEM, VMEM),
+        out_specs=(VMEM, VMEM, VMEM),
         scratch_shapes=[
+            pltpu.VMEM((2, HALF + ZEROS, BAND), jnp.float32),
             pltpu.VMEM(mask.shape, jnp.bfloat16),
             pltpu.VMEM(mask.shape, jnp.bfloat16),
             pltpu.VMEM(col_table.shape, jnp.bfloat16),
@@ -207,7 +222,11 @@
         copy.start()
 
     scale = 1.0 / math.sqrt(TILE_ROWS * COLS)
-    whole = own[:SUMS, :] + other[:SUMS, :]
+    first = lax.axis_index("tile") % 2 == 0
+    own_half, other_half = own[:HALF, :], other[:HALF, :]
+    whole = jnp.concatenate(
+        [jnp.where(first, own_half, other_half), jnp.where(first, other_half, own_half)], 0
+    )
     spec = (whole[: 2 * BAND] * scale).astype(jnp.bfloat16).astype(jnp.float32)
     spec_real[...] = spec[:BAND]
     spec_imag[...] = spec[BAND:]
@@ -390,20 +409,21 @@
     n_tile, n_src = lax.axis_size("tile"), lax.axis_size("src")
     col_table, row_table, out_table, out_cols = image_tables(columns, height, n_tile, n_src)
     sizes = {"src": n_src, "tile": n_tile}
-    own, zeros = forward(mask, cotangent, col_table, row_table)
+    keep, send, zeros = forward(mask, cotangent, col_table, row_table)
     ids = jnp.concatenate([source_ids, source_count[:, None]], 1) + zeros
     bit = 1
     while bit < n_src // 2:
         ids = jnp.concatenate([ids, swapped(ids, sizes, {"src": bit})], 0)
         bit *= 2
-    step = 1
-    while step < n_tile // 2:
+    own = keep + swapped(send, sizes, {"tile": 1})
+    own_lines = slot_lines(ids + own[HALF : HALF + 1, : SLOTS + 1].astype(jnp.int32), shift_table.T, source_weight.reshape(-1, LANES))
+    other_lines = swapped(own_lines, sizes, {"src": bit})
+    step = 2
+    while step < n_tile:
         own = own + swapped(own, sizes, {"tile": step})
         step *= 2
-    own_lines = slot_lines(ids + own[SUMS : SUMS + 1, : SLOTS + 1].astype(jnp.int32), shift_table.T, source_weight.reshape(-1, LANES))
-    other_lines = swapped(own_lines, sizes, {"src": bit})
-    other = swapped(own, sizes, {"tile": step})
-    pupil = pupil_rows(pupil_phase + own[SUMS : SUMS + 1, :PUPIL])
+    other = swapped(own, sizes, {"tile": 1})
+    pupil = pupil_rows(pupil_phase + own[HALF : HALF + 1, :PUPIL])
     return adjoint(
         own, other, own_lines, other_lines, pupil, grid_tables(), out_cols, out_table, n_src
     )

time: 18.5 us -> 19.8 us (1.070); the launches traced: 18.4 us -> 19.9 us
  waiting for transfers between devices: 1.71 us -> 3 us
  Pallas kernels: 8.04 us -> 8.57 us
  starting transfers between devices: 7.66 us -> 7.29 us
    ppermute x4 -> x5, waiting for transfers between devices: 1.71 us -> 3 us  [swapped(): return lax.ppermute(array, axes, turn)]
    pallas_call x1, Pallas kernels: 3.71 us -> 4.19 us  [adjoint(): pl.pallas_call(functools.partial(adjoint_kernel, n_src), out_shape=jax.Sh...]
    ppermute x4 -> x5, starting transfers between devices: 7.66 us -> 7.29 us  [swapped(): return lax.ppermute(array, axes, turn)]
  transfers between devices with their start and end apart: 4 -> 5, of which waited for: 2 -> 2; matrix products, arithmetic and copies ran while one was open for 2% -> 1% of each run, Pallas kernels for 4% -> 4%
where the time goes in v12:
time: 19.8 us; the launch traced here: 19.9 us
  Pallas kernels  8.57 us (43%)
  starting transfers between devices  7.29 us (37%)
  waiting for transfers between devices  3 us (15%)
  between operations  0.77 us (4%)
  other arithmetic  0.28 us (1%)
    ppermute x5, starting transfers between devices, swapped(): return lax.ppermute(array, axes, turn)  7.29 us
    pallas_call x1, Pallas kernels, adjoint(): pl.pallas_call(functools.partial(adjoint_kernel, n_src), out_shape=jax.Sh...  4.19 us
    pallas_call x1, Pallas kernels, forward(): pl.pallas_call(forward_kernel, out_shape=(jax.ShapeDtypeStruct((HALF + ZE...  3.63 us
    ppermute x5, waiting for transfers between devices, swapped(): return lax.ppermute(array, axes, turn)  3 us
    pallas_call x1, Pallas kernels, slot_lines(): pl.pallas_call(lines_kernel, out_shape=jax.ShapeDtypeStruct((count, LANES...  0.75 us
  transfers between devices with their start and end apart: 5, of which 2 were waited for; matrix products, arithmetic and copies ran while one was open for 1% of the time, Pallas kernels for 4%

profile of v12, /device:TPU:0, one launch (start us, length us, event | category | flops | bytes accessed | tf_op | source)
XLA Modules:
  0.0 19.9 jit_solution(9707521329150216001)
XLA Ops:
  0.7 0.0 copy-start.4
  0.7 0.0 copy-start.1
  0.7 0.0 copy-start.2
  0.7 0.0 copy-start.3
  0.7 0.0 copy-start
  0.7 3.6 %forward.1 = (f32[200,128]{1,0:T(8,128)S(1)}, f32[200,128]{1,0:T(8,128)S(1)}, s32[1,9]{1,0:T(1,128)S(1)}) custom-call(bf16[512,2048]{1,0:T(8,128)(2,1)} %mask.1, bf16[512,2048]{1,0:T(8,128)(2,1)} %cotangent.1, bf16[2048,384]{1,0:T(8,128)(2,1)} %constant.28.clone.col_table, bf16[4,384,512]{2,1,0:T(8,128)(2,1)} %constant.29.clone.row_table), custom_call_target="tpu_custom_call" | custom-call | flops 805306368 | bytes 6291456 | tf_op jit(solution)/shard_map/forward/pallas_call | solution.py:143
  4.3 0.0 copy-done.4
  4.4 0.1 add_add_fusion.1
  4.4 3.0 %collective-permute-start.3 = (s32[1,9]{1,0:T(1,128)S(1)}, s32[1,9]{1,0:T(1,128)S(1)}, u32[]{:S(2)}, u32[]{:S(2)}) collective-permute-start(s32[1,9]{1,0:T(1,128)S(1)} %add_add_fusion.1), channel_id=1, source_target_pairs={{0,4},{1,5},{2,6},{3,7},{4,0},{5,1},{6,2},{7,3},{8,12},{9,13},{10,... | collective-permute-start | bytes 116 | tf_op jit(solution)/shard_map/ppermute | solution.py:404
  7.5 0.0 collective-permute-start
  7.5 1.3 %collective-permute-done = f32[200,128]{1,0:T(8,128)S(1)} collective-permute-done((f32[200,128]{1,0:T(8,128)S(1)}, f32[200,128]{1,0:T(8,128)S(1)}, u32[]{:S(2)}, u32[]{:S(2)}) %collective-permute-start) | collective-permute-done | bytes 102432 | tf_op jit(solution)/shard_map/ppermute | solution.py:404
  8.8 1.6 %collective-permute-start.1 = (f32[200,128]{1,0:T(8,128)S(1)}, f32[200,128]{1,0:T(8,128)S(1)}, u32[]{:S(2)}, u32[]{:S(2)}) collective-permute-start(f32[200,128]{1,0:T(8,128)S(1)} %add.80), channel_id=1, source_target_pairs={{0,2},{1,3},{2,0},{3,1},{4,6},{5,7},{6,4},{7,5},{8,10},{9,11},{10,... | collective-permute-start | bytes 307208 | tf_op jit(solution)/shard_map/ppermute | solution.py:404
  10.3 0.0 collective-permute-done.3
  10.4 0.0 copy-done.1
  10.4 0.0 copy-done.2
  10.4 0.7 %slot_lines.1.own_lines = f32[16,128]{1,0:T(8,128)S(1)} custom-call(s32[2,9]{1,0:T(2,128)S(1)} %add_add_fusion.ids, s32[2,12288]{1,0:T(2,128)S(1)} %bitcast.8, f32[96,128]{1,0:T(8,128)S(1)} %bitcast.9), custom_call_target="tpu_custom_call" | custom-call | flops 1 | bytes 1 | tf_op jit(solution)/shard_map/slot_lines/pallas_call | solution.py:198
  11.1 2.6 %collective-permute-start.4 = (f32[16,128]{1,0:T(8,128)S(1)}, f32[16,128]{1,0:T(8,128)S(1)}, u32[]{:S(2)}, u32[]{:S(2)}) collective-permute-start(f32[16,128]{1,0:T(8,128)S(1)} %slot_lines.1.own_lines), channel_id=1, source_target_pairs={{0,8},{1,9},{2,10},{3,11},{4,12},{5,13},{6,14},{7,15},{8,0},{9,1},... | collective-permute-start | bytes 24584 | tf_op jit(solution)/shard_map/ppermute | solution.py:404
  13.8 0.0 collective-permute-done.1
  13.8 0.1 collective-permute-start.2
  13.9 0.0 copy-done.3
  13.9 0.1 cosine_select_fusion
  14.1 1.7 %collective-permute-done.4.other_lines = f32[16,128]{1,0:T(8,128)S(1)} collective-permute-done((f32[16,128]{1,0:T(8,128)S(1)}, f32[16,128]{1,0:T(8,128)S(1)}, u32[]{:S(2)}, u32[]{:S(2)}) %collective-permute-start.4) | collective-permute-done | bytes 8224 | tf_op jit(solution)/shard_map/ppermute | solution.py:404
  15.7 0.0 collective-permute-done.2.other
  15.7 0.0 copy-done
  15.7 4.2 %adjoint.1 = f32[1,128,2048]{2,1,0:T(8,128)} custom-call(f32[200,128]{1,0:T(8,128)S(1)} %add.81.own, f32[200,128]{1,0:T(8,128)S(1)} %collective-permute-done.2.other, f32[16,128]{1,0:T(8,128)S(1)} %slot_lines.1.own_lines, f32[16,128]{1,0:T(8,128)S(1)} %collective-permute-done.4.other_lines, f32[128,128]{1,0:T(8,128)S(1)} %select_maximum_fusion.pupil, ...), custom_call_target="tpu_custom_call" | custom-call | flops 268435456 | bytes 4194304 | tf_op jit(solution)/shard_map/adjoint/pallas_call | solution.py:357
  (7 shorter events, 0.1 us)
Async XLA Ops:
  0.7 3.7 %copy-start.4 = (s32[1,8]{1,0:T(1,128)S(1)}, s32[1,8]{1,0:T(1,128)}, u32[]{:S(2)}) copy-start(s32[1,8]{1,0:T(1,128)} %param.17) | copy-start | bytes 100
  0.7 9.7 %copy-start.1 = (s32[12288,2]{0,1:T(2,128)S(1)}, s32[12288,2]{0,1:T(2,128)}, u32[]{:S(2)}) copy-start(s32[12288,2]{0,1:T(2,128)} %param.16) | copy-start | bytes 294916
  0.7 9.7 %copy-start.2 = (f32[12288]{0:T(1024)S(1)}, f32[12288]{0:T(1024)}, u32[]{:S(2)}) copy-start(f32[12288]{0:T(1024)} %param.15) | copy-start | bytes 147460
  0.7 13.2 %copy-start.3 = (f32[64,64]{1,0:T(8,128)S(1)}, f32[64,64]{1,0:T(8,128)}, u32[]{:S(2)}) copy-start(f32[64,64]{1,0:T(8,128)} %param.14) | copy-start | bytes 49156
  0.7 15.0 %copy-start = (bf16[768,256]{1,0:T(8,128)(2,1)S(1)}, bf16[768,256]{1,0:T(8,128)(2,1)}, u32[]{:S(2)}) copy-start(bf16[768,256]{1,0:T(8,128)(2,1)} %constant.30.clone.table) | copy-start | bytes 1179652
  4.4 5.9 %collective-permute-start.3 = (s32[1,9]{1,0:T(1,128)S(1)}, s32[1,9]{1,0:T(1,128)S(1)}, u32[]{:S(2)}, u32[]{:S(2)}) collective-permute-start(s32[1,9]{1,0:T(1,128)S(1)} %add_add_fusion.1), channel_id=1, source_target_pairs={{0,4},{1,5},{2,6},{3,7},{4,0},{5,1},{6,2},{7,3},{8,12},{9,13},{10,... | collective-permute-start | bytes 116 | tf_op jit(solution)/shard_map/ppermute | solution.py:404
  7.5 1.3 %collective-permute-start = (f32[200,128]{1,0:T(8,128)S(1)}, f32[200,128]{1,0:T(8,128)S(1)}, u32[]{:S(2)}, u32[]{:S(2)}) collective-permute-start(f32[200,128]{1,0:T(8,128)S(1)} %get-tuple-element.9), channel_id=1, source_target_pairs={{0,1},{1,0},{2,3},{3,2},{4,5},{5,4},{6,7},{7,6},{8,9},{9,8},{10,11... | collective-permute-start | bytes 307208 | tf_op jit(solution)/shard_map/ppermute | solution.py:404
  8.8 5.0 %collective-permute-start.1 = (f32[200,128]{1,0:T(8,128)S(1)}, f32[200,128]{1,0:T(8,128)S(1)}, u32[]{:S(2)}, u32[]{:S(2)}) collective-permute-start(f32[200,128]{1,0:T(8,128)S(1)} %add.80), channel_id=1, source_target_pairs={{0,2},{1,3},{2,0},{3,1},{4,6},{5,7},{6,4},{7,5},{8,10},{9,11},{10,... | collective-permute-start | bytes 307208 | tf_op jit(solution)/shard_map/ppermute | solution.py:404
  11.1 4.6 %collective-permute-start.4 = (f32[16,128]{1,0:T(8,128)S(1)}, f32[16,128]{1,0:T(8,128)S(1)}, u32[]{:S(2)}, u32[]{:S(2)}) collective-permute-start(f32[16,128]{1,0:T(8,128)S(1)} %slot_lines.1.own_lines), channel_id=1, source_target_pairs={{0,8},{1,9},{2,10},{3,11},{4,12},{5,13},{6,14},{7,15},{8,0},{9,1},... | collective-permute-start | bytes 24584 | tf_op jit(solution)/shard_map/ppermute | solution.py:404
  13.8 1.9 %collective-permute-start.2 = (f32[200,128]{1,0:T(8,128)S(1)}, f32[200,128]{1,0:T(8,128)S(1)}, u32[]{:S(2)}, u32[]{:S(2)}) collective-permute-start(f32[200,128]{1,0:T(8,128)S(1)} %add.81.own), channel_id=1, source_target_pairs={{0,1},{1,0},{2,3},{3,2},{4,5},{5,4},{6,7},{7,6},{8,9},{9,8},{10,11... | collective-permute-start | bytes 307208 | tf_op jit(solution)/shard_map/ppermute | solution.py:404

commit v13 on v12

--- a/solution.py
+++ b/solution.py
@@ -385,9 +385,8 @@
 
 
 def pupil_rows(phase):
-    grid = jnp.arange(PUPIL, dtype=jnp.int32)
-    radius = (2 * grid[:, None] - PUPIL + 1) ** 2 + (2 * grid[None, :] - PUPIL + 1) ** 2
-    inside = radius <= PUPIL * PUPIL
+    grid = 2 * np.arange(PUPIL) - PUPIL + 1
+    inside = grid[:, None] ** 2 + grid[None, :] ** 2 <= PUPIL * PUPIL
     both = jnp.concatenate(
         [jnp.where(inside, jnp.cos(phase), 0.0), jnp.where(inside, jnp.sin(phase), 0.0)], 0
     )
@@ -416,14 +415,16 @@
         ids = jnp.concatenate([ids, swapped(ids, sizes, {"src": bit})], 0)
         bit *= 2
     own = keep + swapped(send, sizes, {"tile": 1})
-    own_lines = slot_lines(ids + own[HALF : HALF + 1, : SLOTS + 1].astype(jnp.int32), shift_table.T, source_weight.reshape(-1, LANES))
+    after = own[HALF : HALF + 1]
+    ids = ids + after[:, : SLOTS + 1].astype(jnp.int32)
+    own_lines = slot_lines(ids, shift_table.T, source_weight.reshape(-1, LANES))
+    pupil = pupil_rows(pupil_phase + after[:, :PUPIL])
     other_lines = swapped(own_lines, sizes, {"src": bit})
     step = 2
     while step < n_tile:
         own = own + swapped(own, sizes, {"tile": step})
         step *= 2
     other = swapped(own, sizes, {"tile": 1})
-    pupil = pupil_rows(pupil_phase + own[HALF : HALF + 1, :PUPIL])
     return adjoint(
         own, other, own_lines, other_lines, pupil, grid_tables(), out_cols, out_table, n_src
     )

time: 19.8 us -> 18.5 us (0.934); the launches traced: 19.9 us -> 18.4 us
  waiting for transfers between devices: 3 us -> 1.37 us
  starting transfers between devices: 7.29 us -> 7.73 us
  Pallas kernels: 8.57 us -> 8.23 us
    ppermute x5, waiting for transfers between devices: 3 us -> 1.37 us  [swapped(): return lax.ppermute(array, axes, turn)]
    ppermute x5, starting transfers between devices: 7.29 us -> 7.73 us  [swapped(): return lax.ppermute(array, axes, turn)]
    pallas_call x1, Pallas kernels: 4.19 us -> 3.83 us  [adjoint(): pl.pallas_call(functools.partial(adjoint_kernel, n_src), out_shape=jax.Sh...]
  transfers between devices with their start and end apart: 5 -> 5, of which waited for: 2 -> 1; matrix products, arithmetic and copies ran while one was open for 1% -> 1% of each run, Pallas kernels for 4% -> 4%
where the time goes in v13:
time: 18.5 us; the launch traced here: 18.4 us
  Pallas kernels  8.23 us (44%)
  starting transfers between devices  7.73 us (42%)
  waiting for transfers between devices  1.37 us (7%)
  between operations  0.75 us (4%)
  other arithmetic  0.27 us (1%)
    ppermute x5, starting transfers between devices, swapped(): return lax.ppermute(array, axes, turn)  7.73 us
    pallas_call x1, Pallas kernels, adjoint(): pl.pallas_call(functools.partial(adjoint_kernel, n_src), out_shape=jax.Sh...  3.83 us
    pallas_call x1, Pallas kernels, forward(): pl.pallas_call(forward_kernel, out_shape=(jax.ShapeDtypeStruct((HALF + ZE...  3.65 us
    ppermute x5, waiting for transfers between devices, swapped(): return lax.ppermute(array, axes, turn)  1.37 us
    pallas_call x1, Pallas kernels, slot_lines(): pl.pallas_call(lines_kernel, out_shape=jax.ShapeDtypeStruct((count, LANES...  0.75 us
  transfers between devices with their start and end apart: 5, of which 1 were waited for; matrix products, arithmetic and copies ran while one was open for 1% of the time, Pallas kernels for 4%

profile of v13, /device:TPU:0, one launch (start us, length us, event | category | flops | bytes accessed | tf_op | source)
XLA Modules:
  0.0 18.4 jit_solution(11177664965873580116)
XLA Ops:
  0.0 0.0 copy-start.4
  0.0 0.0 copy-start
  0.0 0.0 copy-start.5
  0.0 0.0 copy-start.1
  0.0 0.0 copy-start.2
  0.0 0.0 copy-start.3
  0.0 3.7 %forward.1 = (f32[200,128]{1,0:T(8,128)S(1)}, f32[200,128]{1,0:T(8,128)S(1)}, s32[1,9]{1,0:T(1,128)S(1)}) custom-call(bf16[512,2048]{1,0:T(8,128)(2,1)} %mask.1, bf16[512,2048]{1,0:T(8,128)(2,1)} %cotangent.1, bf16[2048,384]{1,0:T(8,128)(2,1)} %constant.16.clone.col_table, bf16[4,384,512]{2,1,0:T(8,128)(2,1)} %constant.17.clone.row_table), custom_call_target="tpu_custom_call" | custom-call | flops 805306368 | bytes 6291456 | tf_op jit(solution)/shard_map/forward/pallas_call | solution.py:143
  3.7 0.5 %collective-permute-start = (f32[200,128]{1,0:T(8,128)S(1)}, f32[200,128]{1,0:T(8,128)S(1)}, u32[]{:S(2)}, u32[]{:S(2)}) collective-permute-start(f32[200,128]{1,0:T(8,128)S(1)} %get-tuple-element.9), channel_id=1, source_target_pairs={{0,1},{1,0},{2,3},{3,2},{4,5},{5,4},{6,7},{7,6},{8,9},{9,8},{10,11... | collective-permute-start | bytes 307208 | tf_op jit(solution)/shard_map/ppermute | solution.py:403
  4.9 0.0 copy-done.5
  4.9 0.1 add_add_fusion.1
  5.0 2.6 %collective-permute-start.3 = (s32[1,9]{1,0:T(1,128)S(1)}, s32[1,9]{1,0:T(1,128)S(1)}, u32[]{:S(2)}, u32[]{:S(2)}) collective-permute-start(s32[1,9]{1,0:T(1,128)S(1)} %add_add_fusion.1), channel_id=1, source_target_pairs={{0,4},{1,5},{2,6},{3,7},{4,0},{5,1},{6,2},{7,3},{8,12},{9,13},{10,... | collective-permute-start | bytes 116 | tf_op jit(solution)/shard_map/ppermute | solution.py:403
  7.5 0.0 collective-permute-done
  7.6 1.6 %collective-permute-start.1 = (f32[200,128]{1,0:T(8,128)S(1)}, f32[200,128]{1,0:T(8,128)S(1)}, u32[]{:S(2)}, u32[]{:S(2)}) collective-permute-start(f32[200,128]{1,0:T(8,128)S(1)} %add.31), channel_id=1, source_target_pairs={{0,2},{1,3},{2,0},{3,1},{4,6},{5,7},{6,4},{7,5},{8,10},{9,11},{10,... | collective-permute-start | bytes 307208 | tf_op jit(solution)/shard_map/ppermute | solution.py:403
  9.1 0.0 collective-permute-done.3
  9.2 0.0 copy-done.1
  9.2 0.0 copy-done.2
  9.2 0.7 %slot_lines.1.own_lines = f32[16,128]{1,0:T(8,128)S(1)} custom-call(s32[2,9]{1,0:T(2,128)S(1)} %add_add_fusion.ids, s32[2,12288]{1,0:T(2,128)S(1)} %bitcast.8, f32[96,128]{1,0:T(8,128)S(1)} %bitcast.9), custom_call_target="tpu_custom_call" | custom-call | flops 1 | bytes 1 | tf_op jit(solution)/shard_map/slot_lines/pallas_call | solution.py:198
  9.9 3.0 %collective-permute-start.4 = (f32[16,128]{1,0:T(8,128)S(1)}, f32[16,128]{1,0:T(8,128)S(1)}, u32[]{:S(2)}, u32[]{:S(2)}) collective-permute-start(f32[16,128]{1,0:T(8,128)S(1)} %slot_lines.1.own_lines), channel_id=1, source_target_pairs={{0,8},{1,9},{2,10},{3,11},{4,12},{5,13},{6,14},{7,15},{8,0},{9,1},... | collective-permute-start | bytes 24584 | tf_op jit(solution)/shard_map/ppermute | solution.py:403
  12.9 0.0 copy-done.4
  12.9 0.0 copy-done.3
  12.9 0.1 cosine_select_fusion
  13.1 0.0 collective-permute-done.1
  13.1 0.1 collective-permute-start.2
  13.2 1.4 %collective-permute-done.4.other_lines = f32[16,128]{1,0:T(8,128)S(1)} collective-permute-done((f32[16,128]{1,0:T(8,128)S(1)}, f32[16,128]{1,0:T(8,128)S(1)}, u32[]{:S(2)}, u32[]{:S(2)}) %collective-permute-start.4) | collective-permute-done | bytes 8224 | tf_op jit(solution)/shard_map/ppermute | solution.py:403
  14.5 0.0 collective-permute-done.2.other
  14.5 0.0 copy-done
  14.5 3.8 %adjoint.1 = f32[1,128,2048]{2,1,0:T(8,128)} custom-call(f32[200,128]{1,0:T(8,128)S(1)} %add.32.own, f32[200,128]{1,0:T(8,128)S(1)} %collective-permute-done.2.other, f32[16,128]{1,0:T(8,128)S(1)} %slot_lines.1.own_lines, f32[16,128]{1,0:T(8,128)S(1)} %collective-permute-done.4.other_lines, f32[128,128]{1,0:T(8,128)S(1)} %select_maximum_fusion.pupil, ...), custom_call_target="tpu_custom_call" | custom-call | flops 268435456 | bytes 4194304 | tf_op jit(solution)/shard_map/adjoint/pallas_call | solution.py:357
  (6 shorter events, 0.1 us)
Async XLA Ops:
  0.0 12.9 %copy-start.4 = (pred[64,64]{1,0:T(32,128)(4,1)S(1)}, pred[64,64]{1,0:T(32,128)(4,1)}, u32[]{:S(2)}) copy-start(pred[64,64]{1,0:T(32,128)(4,1)} %constant.18.clone) | copy-start | bytes 12292
  0.0 14.5 %copy-start = (bf16[768,256]{1,0:T(8,128)(2,1)S(1)}, bf16[768,256]{1,0:T(8,128)(2,1)}, u32[]{:S(2)}) copy-start(bf16[768,256]{1,0:T(8,128)(2,1)} %constant.19.clone.table) | copy-start | bytes 1179652
  0.0 4.9 %copy-start.5 = (s32[1,8]{1,0:T(1,128)S(1)}, s32[1,8]{1,0:T(1,128)}, u32[]{:S(2)}) copy-start(s32[1,8]{1,0:T(1,128)} %param.18) | copy-start | bytes 100
  0.0 9.1 %copy-start.1 = (s32[12288,2]{0,1:T(2,128)S(1)}, s32[12288,2]{0,1:T(2,128)}, u32[]{:S(2)}) copy-start(s32[12288,2]{0,1:T(2,128)} %param.17) | copy-start | bytes 294916
  0.0 9.2 %copy-start.2 = (f32[12288]{0:T(1024)S(1)}, f32[12288]{0:T(1024)}, u32[]{:S(2)}) copy-start(f32[12288]{0:T(1024)} %param.16) | copy-start | bytes 147460
  0.0 12.9 %copy-start.3 = (f32[64,64]{1,0:T(8,128)S(1)}, f32[64,64]{1,0:T(8,128)}, u32[]{:S(2)}) copy-start(f32[64,64]{1,0:T(8,128)} %param.15) | copy-start | bytes 49156
  3.7 3.9 %collective-permute-start = (f32[200,128]{1,0:T(8,128)S(1)}, f32[200,128]{1,0:T(8,128)S(1)}, u32[]{:S(2)}, u32[]{:S(2)}) collective-permute-start(f32[200,128]{1,0:T(8,128)S(1)} %get-tuple-element.9), channel_id=1, source_target_pairs={{0,1},{1,0},{2,3},{3,2},{4,5},{5,4},{6,7},{7,6},{8,9},{9,8},{10,11... | collective-permute-start | bytes 307208 | tf_op jit(solution)/shard_map/ppermute | solution.py:403
  5.0 4.2 %collective-permute-start.3 = (s32[1,9]{1,0:T(1,128)S(1)}, s32[1,9]{1,0:T(1,128)S(1)}, u32[]{:S(2)}, u32[]{:S(2)}) collective-permute-start(s32[1,9]{1,0:T(1,128)S(1)} %add_add_fusion.1), channel_id=1, source_target_pairs={{0,4},{1,5},{2,6},{3,7},{4,0},{5,1},{6,2},{7,3},{8,12},{9,13},{10,... | collective-permute-start | bytes 116 | tf_op jit(solution)/shard_map/ppermute | solution.py:403
  7.6 5.5 %collective-permute-start.1 = (f32[200,128]{1,0:T(8,128)S(1)}, f32[200,128]{1,0:T(8,128)S(1)}, u32[]{:S(2)}, u32[]{:S(2)}) collective-permute-start(f32[200,128]{1,0:T(8,128)S(1)} %add.31), channel_id=1, source_target_pairs={{0,2},{1,3},{2,0},{3,1},{4,6},{5,7},{6,4},{7,5},{8,10},{9,11},{10,... | collective-permute-start | bytes 307208 | tf_op jit(solution)/shard_map/ppermute | solution.py:403
  9.9 4.6 %collective-permute-start.4 = (f32[16,128]{1,0:T(8,128)S(1)}, f32[16,128]{1,0:T(8,128)S(1)}, u32[]{:S(2)}, u32[]{:S(2)}) collective-permute-start(f32[16,128]{1,0:T(8,128)S(1)} %slot_lines.1.own_lines), channel_id=1, source_target_pairs={{0,8},{1,9},{2,10},{3,11},{4,12},{5,13},{6,14},{7,15},{8,0},{9,1},... | collective-permute-start | bytes 24584 | tf_op jit(solution)/shard_map/ppermute | solution.py:403
  13.1 1.5 %collective-permute-start.2 = (f32[200,128]{1,0:T(8,128)S(1)}, f32[200,128]{1,0:T(8,128)S(1)}, u32[]{:S(2)}, u32[]{:S(2)}) collective-permute-start(f32[200,128]{1,0:T(8,128)S(1)} %add.32.own), channel_id=1, source_target_pairs={{0,1},{1,0},{2,3},{3,2},{4,5},{5,4},{6,7},{7,6},{8,9},{9,8},{10,11... | collective-permute-start | bytes 307208 | tf_op jit(solution)/shard_map/ppermute | solution.py:403

commit v14 on v13

--- a/solution.py
+++ b/solution.py
@@ -166,31 +166,37 @@
 
 
 def lines_kernel(ids, shift, weight, lines):
-    lane = lax.broadcasted_iota(jnp.int32, (SLOTS, LANES), 1)
-    place = lax.broadcasted_iota(jnp.int32, (SLOTS, LANES), 0)
-
-    def one(row, carry):
-        blocks, weights, there = [], [], jnp.full_like(lane, -1)
-        for slot in range(SLOTS):
-            source = ids[row, slot]
-            start = pl.multiple_of(source // LANES * LANES, LANES)
-            blocks.append(shift[:, pl.ds(start, LANES)])
-            weights.append(weight[pl.ds(source // LANES, 1), :])
-            found = jnp.where(slot < ids[row, SLOTS], source % LANES, -1)
-            there = jnp.where(place == slot, found, there)
-        here = lane == there
-        line = jnp.zeros((SLOTS, LANES), jnp.float32)
-        for dim, into in ((0, OX), (1, OY)):
-            values = jnp.concatenate([block[dim : dim + 1, :] for block in blocks], 0)
-            found = jnp.sum(jnp.where(here, values.astype(jnp.float32), 0.0), 1, keepdims=True)
-            line = jnp.where(lane == into, found, line)
-        found = jnp.sum(jnp.where(here, jnp.concatenate(weights, 0), 0.0), 1, keepdims=True)
-        line = jnp.where(lane == FACTOR, found * (2.0 / SLOTS / PUPIL / PUPIL), line)
-        line = jnp.where(lane == COUNT, ids[row, SLOTS].astype(jnp.float32), line)
-        lines[pl.ds(pl.multiple_of(row * SLOTS, SLOTS), SLOTS), :] = line
-        return carry
-
-    lax.fori_loop(0, ids.shape[0], one, jnp.int32(0), unroll=ids.shape[0] <= 4)
+    blocks = weight.shape[0]
+    count = ids.shape[0] * SLOTS
+    slot = lax.broadcasted_iota(jnp.int32, (SLOTS, SLOTS + 1), 0)
+    column = lax.broadcasted_iota(jnp.int32, (SLOTS, SLOTS + 1), 1)
+    sources, counts, used = [], [], []
+    for row in range(ids.shape[0]):
+        entries = jnp.broadcast_to(ids[row : row + 1, :].astype(jnp.float32), slot.shape)
+        sources.append(jnp.sum(jnp.where(slot == column, entries, 0.0), 1, keepdims=True))
+        counts.append(jnp.sum(jnp.where(column == SLOTS, entries, 0.0), 1, keepdims=True))
+        used.append(jnp.where(slot[:, :1].astype(jnp.float32) < counts[-1], 1.0, 0.0))
+    sources, counts, used = (jnp.concatenate(part, 0) for part in (sources, counts, used))
+    block = jnp.floor(sources * (1.0 / LANES))
+
+    def row_of(table, index, precision):
+        lane = lax.broadcasted_iota(jnp.int32, (count, table.shape[0]), 1).astype(jnp.float32)
+        pick = jnp.where(lane == index, 1.0, 0.0).astype(table.dtype)
+        return jnp.dot(pick, table, precision=precision, preferred_element_type=jnp.float32)
+
+    lane = lax.broadcasted_iota(jnp.int32, (count, LANES), 1)
+    here = lane.astype(jnp.float32) == sources - block * LANES
+    offsets = shift[...].astype(jnp.bfloat16)
+    line = jnp.zeros((count, LANES), jnp.float32)
+    for entry, found in (
+        (OX, row_of(offsets, 2.0 * block, None)),
+        (OY, row_of(offsets, 2.0 * block + 1.0, None)),
+        (FACTOR, row_of(weight[...], block, lax.Precision.HIGHEST)),
+    ):
+        found = jnp.sum(jnp.where(here, found, 0.0), 1, keepdims=True) * used
+        line = jnp.where(lane == entry, found, line)
+    line = jnp.where(lane == FACTOR, line * (2.0 / SLOTS / PUPIL / PUPIL), line)
+    lines[...] = jnp.where(lane == COUNT, counts, line)
 
 
 def slot_lines(ids, shift, weight):
@@ -198,7 +204,7 @@
     return pl.pallas_call(
         lines_kernel,
         out_shape=jax.ShapeDtypeStruct((count, LANES), jnp.float32),
-        in_specs=[SMEM, VMEM, VMEM],
+        in_specs=[VMEM, VMEM, VMEM],
         out_specs=VMEM,
         compiler_params=pltpu.CompilerParams(vmem_limit_bytes=2 * 1024 * 1024),
         cost_estimate=pl.CostEstimate(flops=1, bytes_accessed=1, transcendentals=0),
@@ -417,7 +423,8 @@
     own = keep + swapped(send, sizes, {"tile": 1})
     after = own[HALF : HALF + 1]
     ids = ids + after[:, : SLOTS + 1].astype(jnp.int32)
-    own_lines = slot_lines(ids, shift_table.T, source_weight.reshape(-1, LANES))
+    shift = shift_table.T.reshape(2, -1, LANES).transpose(1, 0, 2).reshape(-1, LANES)
+    own_lines = slot_lines(ids, shift, source_weight.reshape(-1, LANES))
     pupil = pupil_rows(pupil_phase + after[:, :PUPIL])
     other_lines = swapped(own_lines, sizes, {"src": bit})
     step = 2

time: 18.5 us -> 18 us (0.973)
  Pallas kernels: 8.23 us -> 7.81 us
    pallas_call x1, Pallas kernels: 0.75 us -> 0.46 us  [slot_lines(): pl.pallas_call(lines_kernel, out_shape=jax.ShapeDtypeStruct((count, LANES...]
  transfers between devices with their start and end apart: 5 -> 5, of which waited for: 1 -> 1; matrix products, arithmetic and copies ran while one was open for 1% -> 2% of each run, Pallas kernels for 4% -> 3%
where the time goes in v14:
time: 18 us
  Pallas kernels  7.81 us (43%)
  starting transfers between devices  7.72 us (43%)
  waiting for transfers between devices  1.37 us (8%)
  between operations  0.75 us (4%)
  other arithmetic  0.27 us (2%)
    ppermute x5, starting transfers between devices, swapped(): return lax.ppermute(array, axes, turn)  7.72 us
    pallas_call x1, Pallas kernels, adjoint(): pl.pallas_call(functools.partial(adjoint_kernel, n_src), out_shape=jax.Sh...  3.7 us
    pallas_call x1, Pallas kernels, forward(): pl.pallas_call(forward_kernel, out_shape=(jax.ShapeDtypeStruct((HALF + ZE...  3.65 us
    ppermute x5, waiting for transfers between devices, swapped(): return lax.ppermute(array, axes, turn)  1.37 us
    pallas_call x1, Pallas kernels, slot_lines(): pl.pallas_call(lines_kernel, out_shape=jax.ShapeDtypeStruct((count, LANES...  0.46 us
  transfers between devices with their start and end apart: 5, of which 1 were waited for; matrix products, arithmetic and copies ran while one was open for 2% of the time, Pallas kernels for 3%

profile of v14, /device:TPU:0, one launch (start us, length us, event | category | flops | bytes accessed | tf_op | source)
XLA Modules:
  0.0 18.0 jit_solution(9502902459868127694)
XLA Ops:
  0.0 0.0 copy-start.4
  0.0 0.0 copy-start
  0.0 0.0 copy-start.5
  0.0 0.0 copy-start.1
  0.0 0.0 copy-start.2
  0.0 0.0 copy-start.3
  0.0 3.7 %forward.1 = (f32[200,128]{1,0:T(8,128)S(1)}, f32[200,128]{1,0:T(8,128)S(1)}, s32[1,9]{1,0:T(1,128)S(1)}) custom-call(bf16[512,2048]{1,0:T(8,128)(2,1)} %mask.1, bf16[512,2048]{1,0:T(8,128)(2,1)} %cotangent.1, bf16[2048,384]{1,0:T(8,128)(2,1)} %constant.16.clone.col_table, bf16[4,384,512]{2,1,0:T(8,128)(2,1)} %constant.17.clone.row_table), custom_call_target="tpu_custom_call" | custom-call | flops 805306368 | bytes 6291456 | tf_op jit(solution)/shard_map/forward/pallas_call | solution.py:143
  3.7 0.5 %collective-permute-start = (f32[200,128]{1,0:T(8,128)S(1)}, f32[200,128]{1,0:T(8,128)S(1)}, u32[]{:S(2)}, u32[]{:S(2)}) collective-permute-start(f32[200,128]{1,0:T(8,128)S(1)} %get-tuple-element.9), channel_id=1, source_target_pairs={{0,1},{1,0},{2,3},{3,2},{4,5},{5,4},{6,7},{7,6},{8,9},{9,8},{10,11... | collective-permute-start | bytes 307208 | tf_op jit(solution)/shard_map/ppermute | solution.py:409
  4.9 0.0 copy-done.5
  4.9 0.1 add_add_fusion.1
  5.0 2.6 %collective-permute-start.3 = (s32[1,9]{1,0:T(1,128)S(1)}, s32[1,9]{1,0:T(1,128)S(1)}, u32[]{:S(2)}, u32[]{:S(2)}) collective-permute-start(s32[1,9]{1,0:T(1,128)S(1)} %add_add_fusion.1), channel_id=1, source_target_pairs={{0,4},{1,5},{2,6},{3,7},{4,0},{5,1},{6,2},{7,3},{8,12},{9,13},{10,... | collective-permute-start | bytes 116 | tf_op jit(solution)/shard_map/ppermute | solution.py:409
  7.5 0.0 collective-permute-done
  7.6 1.6 %collective-permute-start.1 = (f32[200,128]{1,0:T(8,128)S(1)}, f32[200,128]{1,0:T(8,128)S(1)}, u32[]{:S(2)}, u32[]{:S(2)}) collective-permute-start(f32[200,128]{1,0:T(8,128)S(1)} %add.31), channel_id=1, source_target_pairs={{0,2},{1,3},{2,0},{3,1},{4,6},{5,7},{6,4},{7,5},{8,10},{9,11},{10,... | collective-permute-start | bytes 307208 | tf_op jit(solution)/shard_map/ppermute | solution.py:409
  9.1 0.0 collective-permute-done.3
  9.2 0.0 copy-done.1
  9.2 0.0 copy-done.2
  9.2 0.5 %slot_lines.1.own_lines = f32[16,128]{1,0:T(8,128)S(1)} custom-call(s32[2,9]{1,0:T(2,128)S(1)} %add_add_fusion.ids, s32[192,128]{1,0:T(8,128)S(1)} %bitcast.14, f32[96,128]{1,0:T(8,128)S(1)} %bitcast.15), custom_call_target="tpu_custom_call" | custom-call | flops 1 | bytes 1 | tf_op jit(solution)/shard_map/slot_lines/pallas_call | solution.py:204
  9.6 3.0 %collective-permute-start.4 = (f32[16,128]{1,0:T(8,128)S(1)}, f32[16,128]{1,0:T(8,128)S(1)}, u32[]{:S(2)}, u32[]{:S(2)}) collective-permute-start(f32[16,128]{1,0:T(8,128)S(1)} %slot_lines.1.own_lines), channel_id=1, source_target_pairs={{0,8},{1,9},{2,10},{3,11},{4,12},{5,13},{6,14},{7,15},{8,0},{9,1},... | collective-permute-start | bytes 24584 | tf_op jit(solution)/shard_map/ppermute | solution.py:409
  12.6 0.0 copy-done.4
  12.6 0.0 copy-done.3
  12.6 0.1 cosine_select_fusion
  12.8 0.0 collective-permute-done.1
  12.8 0.1 collective-permute-start.2
  12.9 1.4 %collective-permute-done.4.other_lines = f32[16,128]{1,0:T(8,128)S(1)} collective-permute-done((f32[16,128]{1,0:T(8,128)S(1)}, f32[16,128]{1,0:T(8,128)S(1)}, u32[]{:S(2)}, u32[]{:S(2)}) %collective-permute-start.4) | collective-permute-done | bytes 8224 | tf_op jit(solution)/shard_map/ppermute | solution.py:409
  14.2 0.0 collective-permute-done.2.other
  14.2 0.0 copy-done
  14.2 3.7 %adjoint.1 = f32[1,128,2048]{2,1,0:T(8,128)} custom-call(f32[200,128]{1,0:T(8,128)S(1)} %add.32.own, f32[200,128]{1,0:T(8,128)S(1)} %collective-permute-done.2.other, f32[16,128]{1,0:T(8,128)S(1)} %slot_lines.1.own_lines, f32[16,128]{1,0:T(8,128)S(1)} %collective-permute-done.4.other_lines, f32[128,128]{1,0:T(8,128)S(1)} %select_maximum_fusion.pupil, ...), custom_call_target="tpu_custom_call" | custom-call | flops 268435456 | bytes 4194304 | tf_op jit(solution)/shard_map/adjoint/pallas_call | solution.py:363
  (6 shorter events, 0.1 us)
Async XLA Ops:
  0.0 12.6 %copy-start.4 = (pred[64,64]{1,0:T(32,128)(4,1)S(1)}, pred[64,64]{1,0:T(32,128)(4,1)}, u32[]{:S(2)}) copy-start(pred[64,64]{1,0:T(32,128)(4,1)} %constant.18.clone) | copy-start | bytes 12292
  0.0 14.2 %copy-start = (bf16[768,256]{1,0:T(8,128)(2,1)S(1)}, bf16[768,256]{1,0:T(8,128)(2,1)}, u32[]{:S(2)}) copy-start(bf16[768,256]{1,0:T(8,128)(2,1)} %constant.19.clone.table) | copy-start | bytes 1179652
  0.0 4.9 %copy-start.5 = (s32[1,8]{1,0:T(1,128)S(1)}, s32[1,8]{1,0:T(1,128)}, u32[]{:S(2)}) copy-start(s32[1,8]{1,0:T(1,128)} %param.18) | copy-start | bytes 100
  0.0 9.1 %copy-start.1 = (s32[12288,2]{0,1:T(2,128)S(1)}, s32[12288,2]{0,1:T(2,128)}, u32[]{:S(2)}) copy-start(s32[12288,2]{0,1:T(2,128)} %param.17) | copy-start | bytes 294916
  0.0 9.2 %copy-start.2 = (f32[12288]{0:T(1024)S(1)}, f32[12288]{0:T(1024)}, u32[]{:S(2)}) copy-start(f32[12288]{0:T(1024)} %param.16) | copy-start | bytes 147460
  0.0 12.6 %copy-start.3 = (f32[64,64]{1,0:T(8,128)S(1)}, f32[64,64]{1,0:T(8,128)}, u32[]{:S(2)}) copy-start(f32[64,64]{1,0:T(8,128)} %param.15) | copy-start | bytes 49156
  3.7 3.9 %collective-permute-start = (f32[200,128]{1,0:T(8,128)S(1)}, f32[200,128]{1,0:T(8,128)S(1)}, u32[]{:S(2)}, u32[]{:S(2)}) collective-permute-start(f32[200,128]{1,0:T(8,128)S(1)} %get-tuple-element.9), channel_id=1, source_target_pairs={{0,1},{1,0},{2,3},{3,2},{4,5},{5,4},{6,7},{7,6},{8,9},{9,8},{10,11... | collective-permute-start | bytes 307208 | tf_op jit(solution)/shard_map/ppermute | solution.py:409
  5.0 4.2 %collective-permute-start.3 = (s32[1,9]{1,0:T(1,128)S(1)}, s32[1,9]{1,0:T(1,128)S(1)}, u32[]{:S(2)}, u32[]{:S(2)}) collective-permute-start(s32[1,9]{1,0:T(1,128)S(1)} %add_add_fusion.1), channel_id=1, source_target_pairs={{0,4},{1,5},{2,6},{3,7},{4,0},{5,1},{6,2},{7,3},{8,12},{9,13},{10,... | collective-permute-start | bytes 116 | tf_op jit(solution)/shard_map/ppermute | solution.py:409
  7.6 5.2 %collective-permute-start.1 = (f32[200,128]{1,0:T(8,128)S(1)}, f32[200,128]{1,0:T(8,128)S(1)}, u32[]{:S(2)}, u32[]{:S(2)}) collective-permute-start(f32[200,128]{1,0:T(8,128)S(1)} %add.31), channel_id=1, source_target_pairs={{0,2},{1,3},{2,0},{3,1},{4,6},{5,7},{6,4},{7,5},{8,10},{9,11},{10,... | collective-permute-start | bytes 307208 | tf_op jit(solution)/shard_map/ppermute | solution.py:409
  9.6 4.6 %collective-permute-start.4 = (f32[16,128]{1,0:T(8,128)S(1)}, f32[16,128]{1,0:T(8,128)S(1)}, u32[]{:S(2)}, u32[]{:S(2)}) collective-permute-start(f32[16,128]{1,0:T(8,128)S(1)} %slot_lines.1.own_lines), channel_id=1, source_target_pairs={{0,8},{1,9},{2,10},{3,11},{4,12},{5,13},{6,14},{7,15},{8,0},{9,1},... | collective-permute-start | bytes 24584 | tf_op jit(solution)/shard_map/ppermute | solution.py:409
  12.8 1.5 %collective-permute-start.2 = (f32[200,128]{1,0:T(8,128)S(1)}, f32[200,128]{1,0:T(8,128)S(1)}, u32[]{:S(2)}, u32[]{:S(2)}) collective-permute-start(f32[200,128]{1,0:T(8,128)S(1)} %add.32.own), channel_id=1, source_target_pairs={{0,1},{1,0},{2,3},{3,2},{4,5},{5,4},{6,7},{7,6},{8,9},{9,8},{10,11... | collective-permute-start | bytes 307208 | tf_op jit(solution)/shard_map/ppermute | solution.py:409

commit v15 on v14

--- a/solution.py
+++ b/solution.py
@@ -415,7 +415,9 @@
     col_table, row_table, out_table, out_cols = image_tables(columns, height, n_tile, n_src)
     sizes = {"src": n_src, "tile": n_tile}
     keep, send, zeros = forward(mask, cotangent, col_table, row_table)
-    ids = jnp.concatenate([source_ids, source_count[:, None]], 1) + zeros
+    stay = [(place, place) for place in range(n_src)]
+    count = lax.ppermute(source_count, "src", stay)
+    ids = jnp.concatenate([source_ids, count[:, None]], 1) + zeros
     bit = 1
     while bit < n_src // 2:
         ids = jnp.concatenate([ids, swapped(ids, sizes, {"src": bit})], 0)

time: 18 us -> 19.1 us (1.061); the launches traced: 18 us -> 18.8 us
  starting transfers between devices: 7.72 us -> 8.97 us
  between operations: 0.75 us -> 0.1 us
  other arithmetic: 0.27 us -> 0.83 us
  Pallas kernels: 7.81 us -> 7.51 us
    ppermute x0 -> x1, starting transfers between devices: none -> 1.23 us  [body(): count = lax.ppermute(source_count, 'src', stay)]
    add x1, other arithmetic: 0.08 us -> 0.64 us  [body(): ids = jnp.concatenate([source_ids, count[:, None]], 1) + zeros]
    pallas_call x1, Pallas kernels: 3.7 us -> 3.48 us  [adjoint(): pl.pallas_call(functools.partial(adjoint_kernel, n_src), out_shape=jax.Sh...]
  transfers between devices with their start and end apart: 5 -> 6, of which waited for: 1 -> 1; matrix products, arithmetic and copies ran while one was open for 2% -> 4% of each run, Pallas kernels for 3% -> 21%
where the time goes in v15:
time: 19.1 us; the launch traced here: 18.8 us
  starting transfers between devices  8.97 us (47%)
  Pallas kernels  7.51 us (39%)
  waiting for transfers between devices  1.37 us (7%)
  other arithmetic  0.83 us (4%)
    ppermute x5, starting transfers between devices, swapped(): return lax.ppermute(array, axes, turn)  7.75 us
    pallas_call x1, Pallas kernels, forward(): pl.pallas_call(forward_kernel, out_shape=(jax.ShapeDtypeStruct((HALF + ZE...  3.57 us
    pallas_call x1, Pallas kernels, adjoint(): pl.pallas_call(functools.partial(adjoint_kernel, n_src), out_shape=jax.Sh...  3.48 us
    ppermute x5, waiting for transfers between devices, swapped(): return lax.ppermute(array, axes, turn)  1.37 us
    ppermute x1, starting transfers between devices, body(): count = lax.ppermute(source_count, 'src', stay)  1.23 us
    add x1, other arithmetic, body(): ids = jnp.concatenate([source_ids, count[:, None]], 1) + zeros  0.64 us
    pallas_call x1, Pallas kernels, slot_lines(): pl.pallas_call(lines_kernel, out_shape=jax.ShapeDtypeStruct((count, LANES...  0.46 us
  transfers between devices with their start and end apart: 6, of which 1 were waited for; matrix products, arithmetic and copies ran while one was open for 4% of the time, Pallas kernels for 21%

profile of v15, /device:TPU:0, one launch (start us, length us, event | category | flops | bytes accessed | tf_op | source)
XLA Modules:
  0.0 18.8 jit_solution(17382739840118108588)
XLA Ops:
  0.0 0.0 copy-start.4
  0.0 0.0 copy-start
  0.0 0.0 copy-start.5
  0.0 0.0 copy-start.1
  0.0 0.0 copy-start.2
  0.0 0.0 copy-start.3
  0.0 1.2 %collective-permute-start.3 = (s32[1]{0:T(128)}, s32[1]{0:T(128)}, u32[]{:S(2)}, u32[]{:S(2)}) collective-permute-start(s32[1]{0:T(128)} %param.19), channel_id=1, source_target_pairs={{0,0},{4,4},{8,8},{12,12},{1,1},{5,5},{9,9},{13,13},{2,2},{6,6},{1... | collective-permute-start | bytes 20 | tf_op jit(solution)/shard_map/ppermute | solution.py:419
  1.2 3.6 %forward.1 = (f32[200,128]{1,0:T(8,128)S(1)}, f32[200,128]{1,0:T(8,128)S(1)}, s32[1,9]{1,0:T(1,128)S(1)}) custom-call(bf16[512,2048]{1,0:T(8,128)(2,1)} %mask.1, bf16[512,2048]{1,0:T(8,128)(2,1)} %cotangent.1, bf16[2048,384]{1,0:T(8,128)(2,1)} %constant.16.clone.col_table, bf16[4,384,512]{2,1,0:T(8,128)(2,1)} %constant.17.clone.row_table), custom_call_target="tpu_custom_call" | custom-call | flops 805306368 | bytes 6291456 | tf_op jit(solution)/shard_map/forward/pallas_call | solution.py:143
  4.8 0.5 %collective-permute-start = (f32[200,128]{1,0:T(8,128)S(1)}, f32[200,128]{1,0:T(8,128)S(1)}, u32[]{:S(2)}, u32[]{:S(2)}) collective-permute-start(f32[200,128]{1,0:T(8,128)S(1)} %get-tuple-element.9), channel_id=1, source_target_pairs={{0,1},{1,0},{2,3},{3,2},{4,5},{5,4},{6,7},{7,6},{8,9},{9,8},{10,11... | collective-permute-start | bytes 307208 | tf_op jit(solution)/shard_map/ppermute | solution.py:409
  5.4 0.0 collective-permute-done.3
  5.4 0.0 copy-done.5
  5.4 0.6 %add_add_fusion.1 = s32[1,9]{1,0:T(1,128)S(1)} fusion(s32[1,9]{1,0:T(1,128)S(1)} %get-tuple-element.10, s32[1,1]{1,0:T(1,128)} %bitcast, s32[1,8]{1,0:T(1,128)S(1)} %copy-done.5), kind=kLoop, calls=%fused_computation.8 | loop fusion | flops 18 | bytes 108 | tf_op jit(solution)/shard_map/add | solution.py:420
  6.0 2.6 %collective-permute-start.4 = (s32[1,9]{1,0:T(1,128)S(1)}, s32[1,9]{1,0:T(1,128)S(1)}, u32[]{:S(2)}, u32[]{:S(2)}) collective-permute-start(s32[1,9]{1,0:T(1,128)S(1)} %add_add_fusion.1), channel_id=1, source_target_pairs={{0,4},{1,5},{2,6},{3,7},{4,0},{5,1},{6,2},{7,3},{8,12},{9,13},{10,... | collective-permute-start | bytes 116 | tf_op jit(solution)/shard_map/ppermute | solution.py:409
  8.6 0.0 collective-permute-done
  8.7 1.6 %collective-permute-start.1 = (f32[200,128]{1,0:T(8,128)S(1)}, f32[200,128]{1,0:T(8,128)S(1)}, u32[]{:S(2)}, u32[]{:S(2)}) collective-permute-start(f32[200,128]{1,0:T(8,128)S(1)} %add.31), channel_id=1, source_target_pairs={{0,2},{1,3},{2,0},{3,1},{4,6},{5,7},{6,4},{7,5},{8,10},{9,11},{10,... | collective-permute-start | bytes 307208 | tf_op jit(solution)/shard_map/ppermute | solution.py:409
  10.2 0.0 collective-permute-done.4
  10.2 0.0 copy-done.1
  10.2 0.0 copy-done.2
  10.2 0.5 %slot_lines.1.own_lines = f32[16,128]{1,0:T(8,128)S(1)} custom-call(s32[2,9]{1,0:T(2,128)S(1)} %add_add_fusion.ids, s32[192,128]{1,0:T(8,128)S(1)} %bitcast.13, f32[96,128]{1,0:T(8,128)S(1)} %bitcast.14), custom_call_target="tpu_custom_call" | custom-call | flops 1 | bytes 1 | tf_op jit(solution)/shard_map/slot_lines/pallas_call | solution.py:204
  10.7 3.0 %collective-permute-start.5 = (f32[16,128]{1,0:T(8,128)S(1)}, f32[16,128]{1,0:T(8,128)S(1)}, u32[]{:S(2)}, u32[]{:S(2)}) collective-permute-start(f32[16,128]{1,0:T(8,128)S(1)} %slot_lines.1.own_lines), channel_id=1, source_target_pairs={{0,8},{1,9},{2,10},{3,11},{4,12},{5,13},{6,14},{7,15},{8,0},{9,1},... | collective-permute-start | bytes 24584 | tf_op jit(solution)/shard_map/ppermute | solution.py:409
  13.7 0.0 copy-done.4
  13.7 0.0 copy-done.3
  13.7 0.1 cosine_select_fusion
  13.8 0.0 collective-permute-done.1
  13.9 0.1 collective-permute-start.2
  14.0 1.4 %collective-permute-done.5.other_lines = f32[16,128]{1,0:T(8,128)S(1)} collective-permute-done((f32[16,128]{1,0:T(8,128)S(1)}, f32[16,128]{1,0:T(8,128)S(1)}, u32[]{:S(2)}, u32[]{:S(2)}) %collective-permute-start.5) | collective-permute-done | bytes 8224 | tf_op jit(solution)/shard_map/ppermute | solution.py:409
  15.3 0.0 collective-permute-done.2.other
  15.3 0.0 copy-done
  15.3 3.5 %adjoint.1 = f32[1,128,2048]{2,1,0:T(8,128)} custom-call(f32[200,128]{1,0:T(8,128)S(1)} %add.32.own, f32[200,128]{1,0:T(8,128)S(1)} %collective-permute-done.2.other, f32[16,128]{1,0:T(8,128)S(1)} %slot_lines.1.own_lines, f32[16,128]{1,0:T(8,128)S(1)} %collective-permute-done.5.other_lines, f32[128,128]{1,0:T(8,128)S(1)} %select_maximum_fusion.pupil, ...), custom_call_target="tpu_custom_call" | custom-call | flops 268435456 | bytes 4194304 | tf_op jit(solution)/shard_map/adjoint/pallas_call | solution.py:363
  (6 shorter events, 0.1 us)
Async XLA Ops:
  0.0 13.7 %copy-start.4 = (pred[64,64]{1,0:T(32,128)(4,1)S(1)}, pred[64,64]{1,0:T(32,128)(4,1)}, u32[]{:S(2)}) copy-start(pred[64,64]{1,0:T(32,128)(4,1)} %constant.18.clone) | copy-start | bytes 12292
  0.0 15.3 %copy-start = (bf16[768,256]{1,0:T(8,128)(2,1)S(1)}, bf16[768,256]{1,0:T(8,128)(2,1)}, u32[]{:S(2)}) copy-start(bf16[768,256]{1,0:T(8,128)(2,1)} %constant.19.clone.table) | copy-start | bytes 1179652
  0.0 5.4 %copy-start.5 = (s32[1,8]{1,0:T(1,128)S(1)}, s32[1,8]{1,0:T(1,128)}, u32[]{:S(2)}) copy-start(s32[1,8]{1,0:T(1,128)} %param.18) | copy-start | bytes 100
  0.0 10.2 %copy-start.1 = (s32[12288,2]{0,1:T(2,128)S(1)}, s32[12288,2]{0,1:T(2,128)}, u32[]{:S(2)}) copy-start(s32[12288,2]{0,1:T(2,128)} %param.17) | copy-start | bytes 294916
  0.0 10.2 %copy-start.2 = (f32[12288]{0:T(1024)S(1)}, f32[12288]{0:T(1024)}, u32[]{:S(2)}) copy-start(f32[12288]{0:T(1024)} %param.16) | copy-start | bytes 147460
  0.0 13.7 %copy-start.3 = (f32[64,64]{1,0:T(8,128)S(1)}, f32[64,64]{1,0:T(8,128)}, u32[]{:S(2)}) copy-start(f32[64,64]{1,0:T(8,128)} %param.15) | copy-start | bytes 49156
  0.0 5.3 %collective-permute-start.3 = (s32[1]{0:T(128)}, s32[1]{0:T(128)}, u32[]{:S(2)}, u32[]{:S(2)}) collective-permute-start(s32[1]{0:T(128)} %param.19), channel_id=1, source_target_pairs={{0,0},{4,4},{8,8},{12,12},{1,1},{5,5},{9,9},{13,13},{2,2},{6,6},{1... | collective-permute-start | bytes 20 | tf_op jit(solution)/shard_map/ppermute | solution.py:419
  4.8 3.8 %collective-permute-start = (f32[200,128]{1,0:T(8,128)S(1)}, f32[200,128]{1,0:T(8,128)S(1)}, u32[]{:S(2)}, u32[]{:S(2)}) collective-permute-start(f32[200,128]{1,0:T(8,128)S(1)} %get-tuple-element.9), channel_id=1, source_target_pairs={{0,1},{1,0},{2,3},{3,2},{4,5},{5,4},{6,7},{7,6},{8,9},{9,8},{10,11... | collective-permute-start | bytes 307208 | tf_op jit(solution)/shard_map/ppermute | solution.py:409
  6.0 4.2 %collective-permute-start.4 = (s32[1,9]{1,0:T(1,128)S(1)}, s32[1,9]{1,0:T(1,128)S(1)}, u32[]{:S(2)}, u32[]{:S(2)}) collective-permute-start(s32[1,9]{1,0:T(1,128)S(1)} %add_add_fusion.1), channel_id=1, source_target_pairs={{0,4},{1,5},{2,6},{3,7},{4,0},{5,1},{6,2},{7,3},{8,12},{9,13},{10,... | collective-permute-start | bytes 116 | tf_op jit(solution)/shard_map/ppermute | solution.py:409
  8.7 5.2 %collective-permute-start.1 = (f32[200,128]{1,0:T(8,128)S(1)}, f32[200,128]{1,0:T(8,128)S(1)}, u32[]{:S(2)}, u32[]{:S(2)}) collective-permute-start(f32[200,128]{1,0:T(8,128)S(1)} %add.31), channel_id=1, source_target_pairs={{0,2},{1,3},{2,0},{3,1},{4,6},{5,7},{6,4},{7,5},{8,10},{9,11},{10,... | collective-permute-start | bytes 307208 | tf_op jit(solution)/shard_map/ppermute | solution.py:409
  10.7 4.6 %collective-permute-start.5 = (f32[16,128]{1,0:T(8,128)S(1)}, f32[16,128]{1,0:T(8,128)S(1)}, u32[]{:S(2)}, u32[]{:S(2)}) collective-permute-start(f32[16,128]{1,0:T(8,128)S(1)} %slot_lines.1.own_lines), channel_id=1, source_target_pairs={{0,8},{1,9},{2,10},{3,11},{4,12},{5,13},{6,14},{7,15},{8,0},{9,1},... | collective-permute-start | bytes 24584 | tf_op jit(solution)/shard_map/ppermute | solution.py:409
  13.9 1.5 %collective-permute-start.2 = (f32[200,128]{1,0:T(8,128)S(1)}, f32[200,128]{1,0:T(8,128)S(1)}, u32[]{:S(2)}, u32[]{:S(2)}) collective-permute-start(f32[200,128]{1,0:T(8,128)S(1)} %add.32.own), channel_id=1, source_target_pairs={{0,1},{1,0},{2,3},{3,2},{4,5},{5,4},{6,7},{7,6},{8,9},{9,8},{10,11... | collective-permute-start | bytes 307208 | tf_op jit(solution)/shard_map/ppermute | solution.py:409

commit v16 on v14

--- a/solution.py
+++ b/solution.py
@@ -222,9 +222,7 @@
     out_copy = pltpu.make_async_copy(out_table.at[place], out_v, sems.at[1])
     col_copy = pltpu.make_async_copy(col_table, col_v, sems.at[2])
     half = own_lines.shape[0]
-    own_copy = pltpu.make_async_copy(own_lines, lines.at[pl.ds(0, half), :], sems.at[3])
-    other_copy = pltpu.make_async_copy(other_lines, lines.at[pl.ds(half, half), :], sems.at[4])
-    for copy in (own_copy, other_copy, grid_copy, out_copy, col_copy):
+    for copy in (grid_copy, out_copy, col_copy):
         copy.start()
 
     scale = 1.0 / math.sqrt(TILE_ROWS * COLS)
@@ -242,8 +240,11 @@
         band[...] = jnp.zeros_like(band)
     for slot in range(2 * half + GROUPS[-1]):
         used[slot] = jnp.int32(0)
-    own_copy.wait()
-    other_copy.wait()
+    for part, source in enumerate((own_lines, other_lines)):
+        for slot in range(half):
+            line = source[slot : slot + 1, :]
+            for entry in (OX, OY, FACTOR, COUNT) if slot % SLOTS == 0 else (OX, OY, FACTOR):
+                lines[part * half + slot, entry] = line[0, entry]
 
     def add(block, total):
         first = block * SLOTS

time: 18 us -> 17.6 us (0.978)
  Pallas kernels: 7.81 us -> 7.52 us
    pallas_call x1, Pallas kernels: 3.7 us -> 3.41 us  [adjoint(): pl.pallas_call(functools.partial(adjoint_kernel, n_src), out_shape=jax.Sh...]
where the time goes in v16:
time: 17.6 us; the launch traced here: 17.7 us
  starting transfers between devices  7.72 us (44%)
  Pallas kernels  7.52 us (43%)
  waiting for transfers between devices  1.37 us (8%)
  between operations  0.75 us (4%)
  other arithmetic  0.27 us (2%)
    ppermute x5, starting transfers between devices, swapped(): return lax.ppermute(array, axes, turn)  7.72 us
    pallas_call x1, Pallas kernels, forward(): pl.pallas_call(forward_kernel, out_shape=(jax.ShapeDtypeStruct((HALF + ZE...  3.65 us
    pallas_call x1, Pallas kernels, adjoint(): pl.pallas_call(functools.partial(adjoint_kernel, n_src), out_shape=jax.Sh...  3.41 us
    ppermute x5, waiting for transfers between devices, swapped(): return lax.ppermute(array, axes, turn)  1.37 us
    pallas_call x1, Pallas kernels, slot_lines(): pl.pallas_call(lines_kernel, out_shape=jax.ShapeDtypeStruct((count, LANES...  0.46 us
  transfers between devices with their start and end apart: 5, of which 1 were waited for; matrix products, arithmetic and copies ran while one was open for 2% of the time, Pallas kernels for 3%

profile of v16, /device:TPU:0, one launch (start us, length us, event | category | flops | bytes accessed | tf_op | source)
XLA Modules:
  0.0 17.7 jit_solution(1260567863664787486)
XLA Ops:
  0.0 0.0 copy-start.4
  0.0 0.0 copy-start
  0.0 0.0 copy-start.5
  0.0 0.0 copy-start.1
  0.0 0.0 copy-start.2
  0.0 0.0 copy-start.3
  0.0 3.7 %forward.1 = (f32[200,128]{1,0:T(8,128)S(1)}, f32[200,128]{1,0:T(8,128)S(1)}, s32[1,9]{1,0:T(1,128)S(1)}) custom-call(bf16[512,2048]{1,0:T(8,128)(2,1)} %mask.1, bf16[512,2048]{1,0:T(8,128)(2,1)} %cotangent.1, bf16[2048,384]{1,0:T(8,128)(2,1)} %constant.16.clone.col_table, bf16[4,384,512]{2,1,0:T(8,128)(2,1)} %constant.17.clone.row_table), custom_call_target="tpu_custom_call" | custom-call | flops 805306368 | bytes 6291456 | tf_op jit(solution)/shard_map/forward/pallas_call | solution.py:143
  3.7 0.5 %collective-permute-start = (f32[200,128]{1,0:T(8,128)S(1)}, f32[200,128]{1,0:T(8,128)S(1)}, u32[]{:S(2)}, u32[]{:S(2)}) collective-permute-start(f32[200,128]{1,0:T(8,128)S(1)} %get-tuple-element.9), channel_id=1, source_target_pairs={{0,1},{1,0},{2,3},{3,2},{4,5},{5,4},{6,7},{7,6},{8,9},{9,8},{10,11... | collective-permute-start | bytes 307208 | tf_op jit(solution)/shard_map/ppermute | solution.py:410
  4.9 0.0 copy-done.5
  4.9 0.1 add_add_fusion.1
  5.0 2.6 %collective-permute-start.3 = (s32[1,9]{1,0:T(1,128)S(1)}, s32[1,9]{1,0:T(1,128)S(1)}, u32[]{:S(2)}, u32[]{:S(2)}) collective-permute-start(s32[1,9]{1,0:T(1,128)S(1)} %add_add_fusion.1), channel_id=1, source_target_pairs={{0,4},{1,5},{2,6},{3,7},{4,0},{5,1},{6,2},{7,3},{8,12},{9,13},{10,... | collective-permute-start | bytes 116 | tf_op jit(solution)/shard_map/ppermute | solution.py:410
  7.5 0.0 collective-permute-done
  7.6 1.6 %collective-permute-start.1 = (f32[200,128]{1,0:T(8,128)S(1)}, f32[200,128]{1,0:T(8,128)S(1)}, u32[]{:S(2)}, u32[]{:S(2)}) collective-permute-start(f32[200,128]{1,0:T(8,128)S(1)} %add.31), channel_id=1, source_target_pairs={{0,2},{1,3},{2,0},{3,1},{4,6},{5,7},{6,4},{7,5},{8,10},{9,11},{10,... | collective-permute-start | bytes 307208 | tf_op jit(solution)/shard_map/ppermute | solution.py:410
  9.1 0.0 collective-permute-done.3
  9.2 0.0 copy-done.1
  9.2 0.0 copy-done.2
  9.2 0.5 %slot_lines.1.own_lines = f32[16,128]{1,0:T(8,128)S(1)} custom-call(s32[2,9]{1,0:T(2,128)S(1)} %add_add_fusion.ids, s32[192,128]{1,0:T(8,128)S(1)} %bitcast.14, f32[96,128]{1,0:T(8,128)S(1)} %bitcast.15), custom_call_target="tpu_custom_call" | custom-call | flops 1 | bytes 1 | tf_op jit(solution)/shard_map/slot_lines/pallas_call | solution.py:204
  9.6 3.0 %collective-permute-start.4 = (f32[16,128]{1,0:T(8,128)S(1)}, f32[16,128]{1,0:T(8,128)S(1)}, u32[]{:S(2)}, u32[]{:S(2)}) collective-permute-start(f32[16,128]{1,0:T(8,128)S(1)} %slot_lines.1.own_lines), channel_id=1, source_target_pairs={{0,8},{1,9},{2,10},{3,11},{4,12},{5,13},{6,14},{7,15},{8,0},{9,1},... | collective-permute-start | bytes 24584 | tf_op jit(solution)/shard_map/ppermute | solution.py:410
  12.6 0.0 copy-done.4
  12.6 0.0 copy-done.3
  12.6 0.1 cosine_select_fusion
  12.8 0.0 collective-permute-done.1
  12.8 0.1 collective-permute-start.2
  12.9 1.4 %collective-permute-done.4.other_lines = f32[16,128]{1,0:T(8,128)S(1)} collective-permute-done((f32[16,128]{1,0:T(8,128)S(1)}, f32[16,128]{1,0:T(8,128)S(1)}, u32[]{:S(2)}, u32[]{:S(2)}) %collective-permute-start.4) | collective-permute-done | bytes 8224 | tf_op jit(solution)/shard_map/ppermute | solution.py:410
  14.2 0.0 collective-permute-done.2.other
  14.2 0.0 copy-done
  14.2 3.4 %adjoint.1 = f32[1,128,2048]{2,1,0:T(8,128)} custom-call(f32[200,128]{1,0:T(8,128)S(1)} %add.32.own, f32[200,128]{1,0:T(8,128)S(1)} %collective-permute-done.2.other, f32[16,128]{1,0:T(8,128)S(1)} %slot_lines.1.own_lines, f32[16,128]{1,0:T(8,128)S(1)} %collective-permute-done.4.other_lines, f32[128,128]{1,0:T(8,128)S(1)} %select_maximum_fusion.pupil, ...), custom_call_target="tpu_custom_call" | custom-call | flops 268435456 | bytes 4194304 | tf_op jit(solution)/shard_map/adjoint/pallas_call | solution.py:364
  (6 shorter events, 0.1 us)
Async XLA Ops:
  0.0 12.6 %copy-start.4 = (pred[64,64]{1,0:T(32,128)(4,1)S(1)}, pred[64,64]{1,0:T(32,128)(4,1)}, u32[]{:S(2)}) copy-start(pred[64,64]{1,0:T(32,128)(4,1)} %constant.18.clone) | copy-start | bytes 12292
  0.0 14.2 %copy-start = (bf16[768,256]{1,0:T(8,128)(2,1)S(1)}, bf16[768,256]{1,0:T(8,128)(2,1)}, u32[]{:S(2)}) copy-start(bf16[768,256]{1,0:T(8,128)(2,1)} %constant.19.clone.table) | copy-start | bytes 1179652
  0.0 4.9 %copy-start.5 = (s32[1,8]{1,0:T(1,128)S(1)}, s32[1,8]{1,0:T(1,128)}, u32[]{:S(2)}) copy-start(s32[1,8]{1,0:T(1,128)} %param.18) | copy-start | bytes 100
  0.0 9.1 %copy-start.1 = (s32[12288,2]{0,1:T(2,128)S(1)}, s32[12288,2]{0,1:T(2,128)}, u32[]{:S(2)}) copy-start(s32[12288,2]{0,1:T(2,128)} %param.17) | copy-start | bytes 294916
  0.0 9.2 %copy-start.2 = (f32[12288]{0:T(1024)S(1)}, f32[12288]{0:T(1024)}, u32[]{:S(2)}) copy-start(f32[12288]{0:T(1024)} %param.16) | copy-start | bytes 147460
  0.0 12.6 %copy-start.3 = (f32[64,64]{1,0:T(8,128)S(1)}, f32[64,64]{1,0:T(8,128)}, u32[]{:S(2)}) copy-start(f32[64,64]{1,0:T(8,128)} %param.15) | copy-start | bytes 49156
  3.7 3.9 %collective-permute-start = (f32[200,128]{1,0:T(8,128)S(1)}, f32[200,128]{1,0:T(8,128)S(1)}, u32[]{:S(2)}, u32[]{:S(2)}) collective-permute-start(f32[200,128]{1,0:T(8,128)S(1)} %get-tuple-element.9), channel_id=1, source_target_pairs={{0,1},{1,0},{2,3},{3,2},{4,5},{5,4},{6,7},{7,6},{8,9},{9,8},{10,11... | collective-permute-start | bytes 307208 | tf_op jit(solution)/shard_map/ppermute | solution.py:410
  5.0 4.2 %collective-permute-start.3 = (s32[1,9]{1,0:T(1,128)S(1)}, s32[1,9]{1,0:T(1,128)S(1)}, u32[]{:S(2)}, u32[]{:S(2)}) collective-permute-start(s32[1,9]{1,0:T(1,128)S(1)} %add_add_fusion.1), channel_id=1, source_target_pairs={{0,4},{1,5},{2,6},{3,7},{4,0},{5,1},{6,2},{7,3},{8,12},{9,13},{10,... | collective-permute-start | bytes 116 | tf_op jit(solution)/shard_map/ppermute | solution.py:410
  7.6 5.2 %collective-permute-start.1 = (f32[200,128]{1,0:T(8,128)S(1)}, f32[200,128]{1,0:T(8,128)S(1)}, u32[]{:S(2)}, u32[]{:S(2)}) collective-permute-start(f32[200,128]{1,0:T(8,128)S(1)} %add.31), channel_id=1, source_target_pairs={{0,2},{1,3},{2,0},{3,1},{4,6},{5,7},{6,4},{7,5},{8,10},{9,11},{10,... | collective-permute-start | bytes 307208 | tf_op jit(solution)/shard_map/ppermute | solution.py:410
  9.6 4.6 %collective-permute-start.4 = (f32[16,128]{1,0:T(8,128)S(1)}, f32[16,128]{1,0:T(8,128)S(1)}, u32[]{:S(2)}, u32[]{:S(2)}) collective-permute-start(f32[16,128]{1,0:T(8,128)S(1)} %slot_lines.1.own_lines), channel_id=1, source_target_pairs={{0,8},{1,9},{2,10},{3,11},{4,12},{5,13},{6,14},{7,15},{8,0},{9,1},... | collective-permute-start | bytes 24584 | tf_op jit(solution)/shard_map/ppermute | solution.py:410
  12.8 1.5 %collective-permute-start.2 = (f32[200,128]{1,0:T(8,128)S(1)}, f32[200,128]{1,0:T(8,128)S(1)}, u32[]{:S(2)}, u32[]{:S(2)}) collective-permute-start(f32[200,128]{1,0:T(8,128)S(1)} %add.32.own), channel_id=1, source_target_pairs={{0,1},{1,0},{2,3},{3,2},{4,5},{5,4},{6,7},{7,6},{8,9},{9,8},{10,11... | collective-permute-start | bytes 307208 | tf_op jit(solution)/shard_map/ppermute | solution.py:410

commit v17 on v16

--- a/solution.py
+++ b/solution.py
@@ -215,14 +215,13 @@
 def adjoint_kernel(
     n_src, own, other, own_lines, other_lines, pupil, table, col_table, out_table,
     result,
-    spec_real, spec_imag, image, table_v, col_v, out_v, result_v, lines, used, sems, out_sems, *bands,
+    spec_real, spec_imag, image, col_v, out_v, result_v, lines, used, sems, out_sems, *bands,
 ):
     place = lax.axis_index("tile") * n_src + lax.axis_index("src")
-    grid_copy = pltpu.make_async_copy(table, table_v, sems.at[0])
-    out_copy = pltpu.make_async_copy(out_table.at[place], out_v, sems.at[1])
-    col_copy = pltpu.make_async_copy(col_table, col_v, sems.at[2])
+    out_copy = pltpu.make_async_copy(out_table.at[place], out_v, sems.at[0])
+    col_copy = pltpu.make_async_copy(col_table, col_v, sems.at[1])
     half = own_lines.shape[0]
-    for copy in (grid_copy, out_copy, col_copy):
+    for copy in (out_copy, col_copy):
         copy.start()
 
     scale = 1.0 / math.sqrt(TILE_ROWS * COLS)
@@ -254,7 +253,6 @@
 
     blocks = 2 * half // SLOTS
     total = lax.fori_loop(0, blocks, add, jnp.int32(0), unroll=blocks <= 8)
-    grid_copy.wait()
 
     def group(first, size):
         starts, pupils, amplitudes = [], [], []
@@ -272,7 +270,7 @@
             starts.append(offset_y)
             pupils.append((real, imag, factor))
             amplitudes.append(jnp.concatenate([amp_real, amp_imag], 1).astype(jnp.bfloat16))
-        halfway = dot(jnp.concatenate(amplitudes, 0), table_v[COLS_IN, :]).astype(jnp.bfloat16)
+        halfway = dot(jnp.concatenate(amplitudes, 0), table[COLS_IN, :]).astype(jnp.bfloat16)
         halfway = jnp.concatenate(
             [
                 jnp.concatenate(
@@ -286,7 +284,7 @@
             ],
             1,
         )
-        rows_in = table_v[ROWS_IN, :]
+        rows_in = table[ROWS_IN, :]
         rows_in = jnp.concatenate([rows_in[:, : 2 * PUPIL], rows_in[:, 2 * PUPIL :]], 0)
         field = dot(rows_in, halfway)
         field_grad = jnp.concatenate(
@@ -296,7 +294,7 @@
             ],
             1,
         )
-        back = dot(table_v[ROWS_OUT, :], field_grad).astype(jnp.bfloat16)
+        back = dot(table[ROWS_OUT, :], field_grad).astype(jnp.bfloat16)
         back = jnp.concatenate(
             [
                 jnp.concatenate(
@@ -310,7 +308,7 @@
             ],
             0,
         )
-        grad = dot(back, table_v[COLS_OUT, :])
+        grad = dot(back, table[COLS_OUT, :])
         for slot in range(size):
             real, imag, factor = pupils[slot]
             grad_real = grad[slot * PUPIL : (slot + 1) * PUPIL, :BAND] * factor
@@ -364,19 +362,18 @@
     return pl.pallas_call(
         functools.partial(adjoint_kernel, n_src),
         out_shape=jax.ShapeDtypeStruct((1, portion, columns), jnp.float32),
-        in_specs=[VMEM] * 5 + [HBM] * 3,
+        in_specs=[VMEM] * 6 + [HBM] * 2,
         out_specs=HBM,
         scratch_shapes=[
             band,
             band,
             pltpu.VMEM((2 * GRID, GRID), jnp.float32),
-            pltpu.VMEM(table.shape, jnp.bfloat16),
             pltpu.VMEM(col_table.shape, jnp.bfloat16),
             pltpu.VMEM(out_table.shape[1:], jnp.float32),
             pltpu.VMEM((portion, columns), jnp.float32),
             pltpu.SMEM((2 * own_lines.shape[0], LANES), jnp.float32),
             pltpu.SMEM((2 * own_lines.shape[0] + GROUPS[-1],), jnp.int32),
-            pltpu.SemaphoreType.DMA((5,)),
+            pltpu.SemaphoreType.DMA((2,)),
             pltpu.SemaphoreType.DMA((PARTS,)),
             band,
             band,

time: 17.6 us -> 17.4 us (0.989); the launches traced: 17.7 us -> 17.1 us
  Pallas kernels: 7.52 us -> 6.96 us
    pallas_call x1, Pallas kernels: 3.41 us -> 2.85 us  [adjoint(): pl.pallas_call(functools.partial(adjoint_kernel, n_src), out_shape=jax.Sh...]
where the time goes in v17:
time: 17.4 us; the launch traced here: 17.1 us
  starting transfers between devices  7.72 us (44%)
  Pallas kernels  6.96 us (40%)
  waiting for transfers between devices  1.37 us (8%)
  between operations  0.75 us (4%)
  other arithmetic  0.27 us (2%)
    ppermute x5, starting transfers between devices, swapped(): return lax.ppermute(array, axes, turn)  7.72 us
    pallas_call x1, Pallas kernels, forward(): pl.pallas_call(forward_kernel, out_shape=(jax.ShapeDtypeStruct((HALF + ZE...  3.65 us
    pallas_call x1, Pallas kernels, adjoint(): pl.pallas_call(functools.partial(adjoint_kernel, n_src), out_shape=jax.Sh...  2.85 us
    ppermute x5, waiting for transfers between devices, swapped(): return lax.ppermute(array, axes, turn)  1.37 us
    pallas_call x1, Pallas kernels, slot_lines(): pl.pallas_call(lines_kernel, out_shape=jax.ShapeDtypeStruct((count, LANES...  0.46 us
  transfers between devices with their start and end apart: 5, of which 1 were waited for; matrix products, arithmetic and copies ran while one was open for 2% of the time, Pallas kernels for 3%

profile of v17, /device:TPU:0, one launch (start us, length us, event | category | flops | bytes accessed | tf_op | source)
XLA Modules:
  0.0 17.1 jit_solution(1737774189998826496)
XLA Ops:
  0.0 0.0 copy-start.4
  0.0 0.0 copy-start
  0.0 0.0 copy-start.5
  0.0 0.0 copy-start.1
  0.0 0.0 copy-start.2
  0.0 0.0 copy-start.3
  0.0 3.7 %forward.1 = (f32[200,128]{1,0:T(8,128)S(1)}, f32[200,128]{1,0:T(8,128)S(1)}, s32[1,9]{1,0:T(1,128)S(1)}) custom-call(bf16[512,2048]{1,0:T(8,128)(2,1)} %mask.1, bf16[512,2048]{1,0:T(8,128)(2,1)} %cotangent.1, bf16[2048,384]{1,0:T(8,128)(2,1)} %constant.16.clone.col_table, bf16[4,384,512]{2,1,0:T(8,128)(2,1)} %constant.17.clone.row_table), custom_call_target="tpu_custom_call" | custom-call | flops 805306368 | bytes 6291456 | tf_op jit(solution)/shard_map/forward/pallas_call | solution.py:143
  3.7 0.5 %collective-permute-start = (f32[200,128]{1,0:T(8,128)S(1)}, f32[200,128]{1,0:T(8,128)S(1)}, u32[]{:S(2)}, u32[]{:S(2)}) collective-permute-start(f32[200,128]{1,0:T(8,128)S(1)} %get-tuple-element.9), channel_id=1, source_target_pairs={{0,1},{1,0},{2,3},{3,2},{4,5},{5,4},{6,7},{7,6},{8,9},{9,8},{10,11... | collective-permute-start | bytes 307208 | tf_op jit(solution)/shard_map/ppermute | solution.py:407
  4.9 0.0 copy-done.5
  4.9 0.1 add_add_fusion.1
  5.0 2.6 %collective-permute-start.3 = (s32[1,9]{1,0:T(1,128)S(1)}, s32[1,9]{1,0:T(1,128)S(1)}, u32[]{:S(2)}, u32[]{:S(2)}) collective-permute-start(s32[1,9]{1,0:T(1,128)S(1)} %add_add_fusion.1), channel_id=1, source_target_pairs={{0,4},{1,5},{2,6},{3,7},{4,0},{5,1},{6,2},{7,3},{8,12},{9,13},{10,... | collective-permute-start | bytes 116 | tf_op jit(solution)/shard_map/ppermute | solution.py:407
  7.5 0.0 collective-permute-done
  7.6 1.6 %collective-permute-start.1 = (f32[200,128]{1,0:T(8,128)S(1)}, f32[200,128]{1,0:T(8,128)S(1)}, u32[]{:S(2)}, u32[]{:S(2)}) collective-permute-start(f32[200,128]{1,0:T(8,128)S(1)} %add.31), channel_id=1, source_target_pairs={{0,2},{1,3},{2,0},{3,1},{4,6},{5,7},{6,4},{7,5},{8,10},{9,11},{10,... | collective-permute-start | bytes 307208 | tf_op jit(solution)/shard_map/ppermute | solution.py:407
  9.1 0.0 collective-permute-done.3
  9.2 0.0 copy-done.1
  9.2 0.0 copy-done.2
  9.2 0.5 %slot_lines.1.own_lines = f32[16,128]{1,0:T(8,128)S(1)} custom-call(s32[2,9]{1,0:T(2,128)S(1)} %add_add_fusion.ids, s32[192,128]{1,0:T(8,128)S(1)} %bitcast.14, f32[96,128]{1,0:T(8,128)S(1)} %bitcast.15), custom_call_target="tpu_custom_call" | custom-call | flops 1 | bytes 1 | tf_op jit(solution)/shard_map/slot_lines/pallas_call | solution.py:204
  9.6 3.0 %collective-permute-start.4 = (f32[16,128]{1,0:T(8,128)S(1)}, f32[16,128]{1,0:T(8,128)S(1)}, u32[]{:S(2)}, u32[]{:S(2)}) collective-permute-start(f32[16,128]{1,0:T(8,128)S(1)} %slot_lines.1.own_lines), channel_id=1, source_target_pairs={{0,8},{1,9},{2,10},{3,11},{4,12},{5,13},{6,14},{7,15},{8,0},{9,1},... | collective-permute-start | bytes 24584 | tf_op jit(solution)/shard_map/ppermute | solution.py:407
  12.6 0.0 copy-done.4
  12.6 0.0 copy-done.3
  12.6 0.1 cosine_select_fusion
  12.8 0.0 collective-permute-done.1
  12.8 0.1 collective-permute-start.2
  12.9 1.4 %collective-permute-done.4.other_lines = f32[16,128]{1,0:T(8,128)S(1)} collective-permute-done((f32[16,128]{1,0:T(8,128)S(1)}, f32[16,128]{1,0:T(8,128)S(1)}, u32[]{:S(2)}, u32[]{:S(2)}) %collective-permute-start.4) | collective-permute-done | bytes 8224 | tf_op jit(solution)/shard_map/ppermute | solution.py:407
  14.2 0.0 collective-permute-done.2.other
  14.2 0.0 copy-done
  14.2 2.9 %adjoint.1 = f32[1,128,2048]{2,1,0:T(8,128)} custom-call(f32[200,128]{1,0:T(8,128)S(1)} %add.32.own, f32[200,128]{1,0:T(8,128)S(1)} %collective-permute-done.2.other, f32[16,128]{1,0:T(8,128)S(1)} %slot_lines.1.own_lines, f32[16,128]{1,0:T(8,128)S(1)} %collective-permute-done.4.other_lines, f32[128,128]{1,0:T(8,128)S(1)} %select_maximum_fusion.pupil, ...), custom_call_target="tpu_custom_call" | custom-call | flops 268435456 | bytes 4194304 | tf_op jit(solution)/shard_map/adjoint/pallas_call | solution.py:362
  (6 shorter events, 0.1 us)
Async XLA Ops:
  0.0 12.6 %copy-start.4 = (pred[64,64]{1,0:T(32,128)(4,1)S(1)}, pred[64,64]{1,0:T(32,128)(4,1)}, u32[]{:S(2)}) copy-start(pred[64,64]{1,0:T(32,128)(4,1)} %constant.18.clone) | copy-start | bytes 12292
  0.0 14.2 %copy-start = (bf16[768,256]{1,0:T(8,128)(2,1)S(1)}, bf16[768,256]{1,0:T(8,128)(2,1)}, u32[]{:S(2)}) copy-start(bf16[768,256]{1,0:T(8,128)(2,1)} %constant.19.clone.table) | copy-start | bytes 1179652
  0.0 4.9 %copy-start.5 = (s32[1,8]{1,0:T(1,128)S(1)}, s32[1,8]{1,0:T(1,128)}, u32[]{:S(2)}) copy-start(s32[1,8]{1,0:T(1,128)} %param.18) | copy-start | bytes 100
  0.0 9.1 %copy-start.1 = (s32[12288,2]{0,1:T(2,128)S(1)}, s32[12288,2]{0,1:T(2,128)}, u32[]{:S(2)}) copy-start(s32[12288,2]{0,1:T(2,128)} %param.17) | copy-start | bytes 294916
  0.0 9.2 %copy-start.2 = (f32[12288]{0:T(1024)S(1)}, f32[12288]{0:T(1024)}, u32[]{:S(2)}) copy-start(f32[12288]{0:T(1024)} %param.16) | copy-start | bytes 147460
  0.0 12.6 %copy-start.3 = (f32[64,64]{1,0:T(8,128)S(1)}, f32[64,64]{1,0:T(8,128)}, u32[]{:S(2)}) copy-start(f32[64,64]{1,0:T(8,128)} %param.15) | copy-start | bytes 49156
  3.7 3.9 %collective-permute-start = (f32[200,128]{1,0:T(8,128)S(1)}, f32[200,128]{1,0:T(8,128)S(1)}, u32[]{:S(2)}, u32[]{:S(2)}) collective-permute-start(f32[200,128]{1,0:T(8,128)S(1)} %get-tuple-element.9), channel_id=1, source_target_pairs={{0,1},{1,0},{2,3},{3,2},{4,5},{5,4},{6,7},{7,6},{8,9},{9,8},{10,11... | collective-permute-start | bytes 307208 | tf_op jit(solution)/shard_map/ppermute | solution.py:407
  5.0 4.2 %collective-permute-start.3 = (s32[1,9]{1,0:T(1,128)S(1)}, s32[1,9]{1,0:T(1,128)S(1)}, u32[]{:S(2)}, u32[]{:S(2)}) collective-permute-start(s32[1,9]{1,0:T(1,128)S(1)} %add_add_fusion.1), channel_id=1, source_target_pairs={{0,4},{1,5},{2,6},{3,7},{4,0},{5,1},{6,2},{7,3},{8,12},{9,13},{10,... | collective-permute-start | bytes 116 | tf_op jit(solution)/shard_map/ppermute | solution.py:407
  7.6 5.2 %collective-permute-start.1 = (f32[200,128]{1,0:T(8,128)S(1)}, f32[200,128]{1,0:T(8,128)S(1)}, u32[]{:S(2)}, u32[]{:S(2)}) collective-permute-start(f32[200,128]{1,0:T(8,128)S(1)} %add.31), channel_id=1, source_target_pairs={{0,2},{1,3},{2,0},{3,1},{4,6},{5,7},{6,4},{7,5},{8,10},{9,11},{10,... | collective-permute-start | bytes 307208 | tf_op jit(solution)/shard_map/ppermute | solution.py:407
  9.6 4.6 %collective-permute-start.4 = (f32[16,128]{1,0:T(8,128)S(1)}, f32[16,128]{1,0:T(8,128)S(1)}, u32[]{:S(2)}, u32[]{:S(2)}) collective-permute-start(f32[16,128]{1,0:T(8,128)S(1)} %slot_lines.1.own_lines), channel_id=1, source_target_pairs={{0,8},{1,9},{2,10},{3,11},{4,12},{5,13},{6,14},{7,15},{8,0},{9,1},... | collective-permute-start | bytes 24584 | tf_op jit(solution)/shard_map/ppermute | solution.py:407
  12.8 1.5 %collective-permute-start.2 = (f32[200,128]{1,0:T(8,128)S(1)}, f32[200,128]{1,0:T(8,128)S(1)}, u32[]{:S(2)}, u32[]{:S(2)}) collective-permute-start(f32[200,128]{1,0:T(8,128)S(1)} %add.32.own), channel_id=1, source_target_pairs={{0,1},{1,0},{2,3},{3,2},{4,5},{5,4},{6,7},{7,6},{8,9},{9,8},{10,11... | collective-permute-start | bytes 307208 | tf_op jit(solution)/shard_map/ppermute | solution.py:407

commit v18 on v17

--- a/solution.py
+++ b/solution.py
@@ -19,7 +19,7 @@
 CHUNKS = (1,) * 8
 GROUPS = (16, 20, 24, 32)
 OX, OY, FACTOR, COUNT = range(4)
-PARTS = 4
+PARTS = 2
 LANES = 128
 SUMS = 2 * BAND + GRID
 HALF = SUMS // 2

time: 17.4 us -> 17.4 us (level); the launches traced: 17.1 us -> 17.5 us
  Pallas kernels: 6.96 us -> 7.35 us
    pallas_call x1, Pallas kernels: 2.85 us -> 3.24 us  [adjoint(): pl.pallas_call(functools.partial(adjoint_kernel, n_src), out_shape=jax.Sh...]
where the time goes in v18:
time: 17.4 us; the launch traced here: 17.5 us
  starting transfers between devices  7.72 us (44%)
  Pallas kernels  7.35 us (42%)
  waiting for transfers between devices  1.37 us (8%)
  between operations  0.75 us (4%)
  other arithmetic  0.27 us (2%)
    ppermute x5, starting transfers between devices, swapped(): return lax.ppermute(array, axes, turn)  7.72 us
    pallas_call x1, Pallas kernels, forward(): pl.pallas_call(forward_kernel, out_shape=(jax.ShapeDtypeStruct((HALF + ZE...  3.65 us
    pallas_call x1, Pallas kernels, adjoint(): pl.pallas_call(functools.partial(adjoint_kernel, n_src), out_shape=jax.Sh...  3.24 us
    ppermute x5, waiting for transfers between devices, swapped(): return lax.ppermute(array, axes, turn)  1.37 us
    pallas_call x1, Pallas kernels, slot_lines(): pl.pallas_call(lines_kernel, out_shape=jax.ShapeDtypeStruct((count, LANES...  0.46 us
  transfers between devices with their start and end apart: 5, of which 1 were waited for; matrix products, arithmetic and copies ran while one was open for 2% of the time, Pallas kernels for 3%

profile of v18, /device:TPU:0, one launch (start us, length us, event | category | flops | bytes accessed | tf_op | source)
XLA Modules:
  0.0 17.5 jit_solution(2749388924088253822)
XLA Ops:
  0.0 0.0 copy-start.4
  0.0 0.0 copy-start
  0.0 0.0 copy-start.5
  0.0 0.0 copy-start.1
  0.0 0.0 copy-start.2
  0.0 0.0 copy-start.3
  0.0 3.7 %forward.1 = (f32[200,128]{1,0:T(8,128)S(1)}, f32[200,128]{1,0:T(8,128)S(1)}, s32[1,9]{1,0:T(1,128)S(1)}) custom-call(bf16[512,2048]{1,0:T(8,128)(2,1)} %mask.1, bf16[512,2048]{1,0:T(8,128)(2,1)} %cotangent.1, bf16[2048,384]{1,0:T(8,128)(2,1)} %constant.16.clone.col_table, bf16[4,384,512]{2,1,0:T(8,128)(2,1)} %constant.17.clone.row_table), custom_call_target="tpu_custom_call" | custom-call | flops 805306368 | bytes 6291456 | tf_op jit(solution)/shard_map/forward/pallas_call | solution.py:143
  3.7 0.5 %collective-permute-start = (f32[200,128]{1,0:T(8,128)S(1)}, f32[200,128]{1,0:T(8,128)S(1)}, u32[]{:S(2)}, u32[]{:S(2)}) collective-permute-start(f32[200,128]{1,0:T(8,128)S(1)} %get-tuple-element.9), channel_id=1, source_target_pairs={{0,1},{1,0},{2,3},{3,2},{4,5},{5,4},{6,7},{7,6},{8,9},{9,8},{10,11... | collective-permute-start | bytes 307208 | tf_op jit(solution)/shard_map/ppermute | solution.py:407
  4.9 0.0 copy-done.5
  4.9 0.1 add_add_fusion.1
  5.0 2.6 %collective-permute-start.3 = (s32[1,9]{1,0:T(1,128)S(1)}, s32[1,9]{1,0:T(1,128)S(1)}, u32[]{:S(2)}, u32[]{:S(2)}) collective-permute-start(s32[1,9]{1,0:T(1,128)S(1)} %add_add_fusion.1), channel_id=1, source_target_pairs={{0,4},{1,5},{2,6},{3,7},{4,0},{5,1},{6,2},{7,3},{8,12},{9,13},{10,... | collective-permute-start | bytes 116 | tf_op jit(solution)/shard_map/ppermute | solution.py:407
  7.5 0.0 collective-permute-done
  7.6 1.6 %collective-permute-start.1 = (f32[200,128]{1,0:T(8,128)S(1)}, f32[200,128]{1,0:T(8,128)S(1)}, u32[]{:S(2)}, u32[]{:S(2)}) collective-permute-start(f32[200,128]{1,0:T(8,128)S(1)} %add.31), channel_id=1, source_target_pairs={{0,2},{1,3},{2,0},{3,1},{4,6},{5,7},{6,4},{7,5},{8,10},{9,11},{10,... | collective-permute-start | bytes 307208 | tf_op jit(solution)/shard_map/ppermute | solution.py:407
  9.1 0.0 collective-permute-done.3
  9.2 0.0 copy-done.1
  9.2 0.0 copy-done.2
  9.2 0.5 %slot_lines.1.own_lines = f32[16,128]{1,0:T(8,128)S(1)} custom-call(s32[2,9]{1,0:T(2,128)S(1)} %add_add_fusion.ids, s32[192,128]{1,0:T(8,128)S(1)} %bitcast.14, f32[96,128]{1,0:T(8,128)S(1)} %bitcast.15), custom_call_target="tpu_custom_call" | custom-call | flops 1 | bytes 1 | tf_op jit(solution)/shard_map/slot_lines/pallas_call | solution.py:204
  9.6 3.0 %collective-permute-start.4 = (f32[16,128]{1,0:T(8,128)S(1)}, f32[16,128]{1,0:T(8,128)S(1)}, u32[]{:S(2)}, u32[]{:S(2)}) collective-permute-start(f32[16,128]{1,0:T(8,128)S(1)} %slot_lines.1.own_lines), channel_id=1, source_target_pairs={{0,8},{1,9},{2,10},{3,11},{4,12},{5,13},{6,14},{7,15},{8,0},{9,1},... | collective-permute-start | bytes 24584 | tf_op jit(solution)/shard_map/ppermute | solution.py:407
  12.6 0.0 copy-done.4
  12.6 0.0 copy-done.3
  12.6 0.1 cosine_select_fusion
  12.8 0.0 collective-permute-done.1
  12.8 0.1 collective-permute-start.2
  12.9 1.4 %collective-permute-done.4.other_lines = f32[16,128]{1,0:T(8,128)S(1)} collective-permute-done((f32[16,128]{1,0:T(8,128)S(1)}, f32[16,128]{1,0:T(8,128)S(1)}, u32[]{:S(2)}, u32[]{:S(2)}) %collective-permute-start.4) | collective-permute-done | bytes 8224 | tf_op jit(solution)/shard_map/ppermute | solution.py:407
  14.2 0.0 collective-permute-done.2.other
  14.2 0.0 copy-done
  14.2 3.2 %adjoint.1 = f32[1,128,2048]{2,1,0:T(8,128)} custom-call(f32[200,128]{1,0:T(8,128)S(1)} %add.32.own, f32[200,128]{1,0:T(8,128)S(1)} %collective-permute-done.2.other, f32[16,128]{1,0:T(8,128)S(1)} %slot_lines.1.own_lines, f32[16,128]{1,0:T(8,128)S(1)} %collective-permute-done.4.other_lines, f32[128,128]{1,0:T(8,128)S(1)} %select_maximum_fusion.pupil, ...), custom_call_target="tpu_custom_call" | custom-call | flops 268435456 | bytes 4194304 | tf_op jit(solution)/shard_map/adjoint/pallas_call | solution.py:362
  (6 shorter events, 0.1 us)
Async XLA Ops:
  0.0 12.6 %copy-start.4 = (pred[64,64]{1,0:T(32,128)(4,1)S(1)}, pred[64,64]{1,0:T(32,128)(4,1)}, u32[]{:S(2)}) copy-start(pred[64,64]{1,0:T(32,128)(4,1)} %constant.18.clone) | copy-start | bytes 12292
  0.0 14.2 %copy-start = (bf16[768,256]{1,0:T(8,128)(2,1)S(1)}, bf16[768,256]{1,0:T(8,128)(2,1)}, u32[]{:S(2)}) copy-start(bf16[768,256]{1,0:T(8,128)(2,1)} %constant.19.clone.table) | copy-start | bytes 1179652
  0.0 4.9 %copy-start.5 = (s32[1,8]{1,0:T(1,128)S(1)}, s32[1,8]{1,0:T(1,128)}, u32[]{:S(2)}) copy-start(s32[1,8]{1,0:T(1,128)} %param.18) | copy-start | bytes 100
  0.0 9.1 %copy-start.1 = (s32[12288,2]{0,1:T(2,128)S(1)}, s32[12288,2]{0,1:T(2,128)}, u32[]{:S(2)}) copy-start(s32[12288,2]{0,1:T(2,128)} %param.17) | copy-start | bytes 294916
  0.0 9.2 %copy-start.2 = (f32[12288]{0:T(1024)S(1)}, f32[12288]{0:T(1024)}, u32[]{:S(2)}) copy-start(f32[12288]{0:T(1024)} %param.16) | copy-start | bytes 147460
  0.0 12.6 %copy-start.3 = (f32[64,64]{1,0:T(8,128)S(1)}, f32[64,64]{1,0:T(8,128)}, u32[]{:S(2)}) copy-start(f32[64,64]{1,0:T(8,128)} %param.15) | copy-start | bytes 49156
  3.7 3.9 %collective-permute-start = (f32[200,128]{1,0:T(8,128)S(1)}, f32[200,128]{1,0:T(8,128)S(1)}, u32[]{:S(2)}, u32[]{:S(2)}) collective-permute-start(f32[200,128]{1,0:T(8,128)S(1)} %get-tuple-element.9), channel_id=1, source_target_pairs={{0,1},{1,0},{2,3},{3,2},{4,5},{5,4},{6,7},{7,6},{8,9},{9,8},{10,11... | collective-permute-start | bytes 307208 | tf_op jit(solution)/shard_map/ppermute | solution.py:407
  5.0 4.2 %collective-permute-start.3 = (s32[1,9]{1,0:T(1,128)S(1)}, s32[1,9]{1,0:T(1,128)S(1)}, u32[]{:S(2)}, u32[]{:S(2)}) collective-permute-start(s32[1,9]{1,0:T(1,128)S(1)} %add_add_fusion.1), channel_id=1, source_target_pairs={{0,4},{1,5},{2,6},{3,7},{4,0},{5,1},{6,2},{7,3},{8,12},{9,13},{10,... | collective-permute-start | bytes 116 | tf_op jit(solution)/shard_map/ppermute | solution.py:407
  7.6 5.2 %collective-permute-start.1 = (f32[200,128]{1,0:T(8,128)S(1)}, f32[200,128]{1,0:T(8,128)S(1)}, u32[]{:S(2)}, u32[]{:S(2)}) collective-permute-start(f32[200,128]{1,0:T(8,128)S(1)} %add.31), channel_id=1, source_target_pairs={{0,2},{1,3},{2,0},{3,1},{4,6},{5,7},{6,4},{7,5},{8,10},{9,11},{10,... | collective-permute-start | bytes 307208 | tf_op jit(solution)/shard_map/ppermute | solution.py:407
  9.6 4.6 %collective-permute-start.4 = (f32[16,128]{1,0:T(8,128)S(1)}, f32[16,128]{1,0:T(8,128)S(1)}, u32[]{:S(2)}, u32[]{:S(2)}) collective-permute-start(f32[16,128]{1,0:T(8,128)S(1)} %slot_lines.1.own_lines), channel_id=1, source_target_pairs={{0,8},{1,9},{2,10},{3,11},{4,12},{5,13},{6,14},{7,15},{8,0},{9,1},... | collective-permute-start | bytes 24584 | tf_op jit(solution)/shard_map/ppermute | solution.py:407
  12.8 1.5 %collective-permute-start.2 = (f32[200,128]{1,0:T(8,128)S(1)}, f32[200,128]{1,0:T(8,128)S(1)}, u32[]{:S(2)}, u32[]{:S(2)}) collective-permute-start(f32[200,128]{1,0:T(8,128)S(1)} %add.32.own), channel_id=1, source_target_pairs={{0,1},{1,0},{2,3},{3,2},{4,5},{5,4},{6,7},{7,6},{8,9},{9,8},{10,11... | collective-permute-start | bytes 307208 | tf_op jit(solution)/shard_map/ppermute | solution.py:407

commit v19 on v17

--- a/solution.py
+++ b/solution.py
@@ -17,7 +17,7 @@
 SLOTS = 8
 GRID = 128
 CHUNKS = (1,) * 8
-GROUPS = (16, 20, 24, 32)
+GROUPS = (16, 18, 20, 22, 24, 32)
 OX, OY, FACTOR, COUNT = range(4)
 PARTS = 4
 LANES = 128

time: 17.4 us -> 17.3 us (level)
  no operation moved by 1% of the time
where the time goes in v19:
time: 17.3 us; the launch traced here: 17.1 us
  starting transfers between devices  7.72 us (45%)
  Pallas kernels  6.97 us (40%)
  waiting for transfers between devices  1.37 us (8%)
  between operations  0.75 us (4%)
  other arithmetic  0.27 us (2%)
    ppermute x5, starting transfers between devices, swapped(): return lax.ppermute(array, axes, turn)  7.72 us
    pallas_call x1, Pallas kernels, forward(): pl.pallas_call(forward_kernel, out_shape=(jax.ShapeDtypeStruct((HALF + ZE...  3.65 us
    pallas_call x1, Pallas kernels, adjoint(): pl.pallas_call(functools.partial(adjoint_kernel, n_src), out_shape=jax.Sh...  2.86 us
    ppermute x5, waiting for transfers between devices, swapped(): return lax.ppermute(array, axes, turn)  1.37 us
    pallas_call x1, Pallas kernels, slot_lines(): pl.pallas_call(lines_kernel, out_shape=jax.ShapeDtypeStruct((count, LANES...  0.46 us
  transfers between devices with their start and end apart: 5, of which 1 were waited for; matrix products, arithmetic and copies ran while one was open for 2% of the time, Pallas kernels for 3%

profile of v19, /device:TPU:0, one launch (start us, length us, event | category | flops | bytes accessed | tf_op | source)
XLA Modules:
  0.0 17.1 jit_solution(3944404178602785904)
XLA Ops:
  0.0 0.0 copy-start.4
  0.0 0.0 copy-start
  0.0 0.0 copy-start.5
  0.0 0.0 copy-start.1
  0.0 0.0 copy-start.2
  0.0 0.0 copy-start.3
  0.0 3.7 %forward.1 = (f32[200,128]{1,0:T(8,128)S(1)}, f32[200,128]{1,0:T(8,128)S(1)}, s32[1,9]{1,0:T(1,128)S(1)}) custom-call(bf16[512,2048]{1,0:T(8,128)(2,1)} %mask.1, bf16[512,2048]{1,0:T(8,128)(2,1)} %cotangent.1, bf16[2048,384]{1,0:T(8,128)(2,1)} %constant.16.clone.col_table, bf16[4,384,512]{2,1,0:T(8,128)(2,1)} %constant.17.clone.row_table), custom_call_target="tpu_custom_call" | custom-call | flops 805306368 | bytes 6291456 | tf_op jit(solution)/shard_map/forward/pallas_call | solution.py:143
  3.7 0.5 %collective-permute-start = (f32[200,128]{1,0:T(8,128)S(1)}, f32[200,128]{1,0:T(8,128)S(1)}, u32[]{:S(2)}, u32[]{:S(2)}) collective-permute-start(f32[200,128]{1,0:T(8,128)S(1)} %get-tuple-element.9), channel_id=1, source_target_pairs={{0,1},{1,0},{2,3},{3,2},{4,5},{5,4},{6,7},{7,6},{8,9},{9,8},{10,11... | collective-permute-start | bytes 307208 | tf_op jit(solution)/shard_map/ppermute | solution.py:407
  4.9 0.0 copy-done.5
  4.9 0.1 add_add_fusion.1
  5.0 2.6 %collective-permute-start.3 = (s32[1,9]{1,0:T(1,128)S(1)}, s32[1,9]{1,0:T(1,128)S(1)}, u32[]{:S(2)}, u32[]{:S(2)}) collective-permute-start(s32[1,9]{1,0:T(1,128)S(1)} %add_add_fusion.1), channel_id=1, source_target_pairs={{0,4},{1,5},{2,6},{3,7},{4,0},{5,1},{6,2},{7,3},{8,12},{9,13},{10,... | collective-permute-start | bytes 116 | tf_op jit(solution)/shard_map/ppermute | solution.py:407
  7.5 0.0 collective-permute-done
  7.6 1.6 %collective-permute-start.1 = (f32[200,128]{1,0:T(8,128)S(1)}, f32[200,128]{1,0:T(8,128)S(1)}, u32[]{:S(2)}, u32[]{:S(2)}) collective-permute-start(f32[200,128]{1,0:T(8,128)S(1)} %add.31), channel_id=1, source_target_pairs={{0,2},{1,3},{2,0},{3,1},{4,6},{5,7},{6,4},{7,5},{8,10},{9,11},{10,... | collective-permute-start | bytes 307208 | tf_op jit(solution)/shard_map/ppermute | solution.py:407
  9.1 0.0 collective-permute-done.3
  9.2 0.0 copy-done.1
  9.2 0.0 copy-done.2
  9.2 0.5 %slot_lines.1.own_lines = f32[16,128]{1,0:T(8,128)S(1)} custom-call(s32[2,9]{1,0:T(2,128)S(1)} %add_add_fusion.ids, s32[192,128]{1,0:T(8,128)S(1)} %bitcast.14, f32[96,128]{1,0:T(8,128)S(1)} %bitcast.15), custom_call_target="tpu_custom_call" | custom-call | flops 1 | bytes 1 | tf_op jit(solution)/shard_map/slot_lines/pallas_call | solution.py:204
  9.6 3.0 %collective-permute-start.4 = (f32[16,128]{1,0:T(8,128)S(1)}, f32[16,128]{1,0:T(8,128)S(1)}, u32[]{:S(2)}, u32[]{:S(2)}) collective-permute-start(f32[16,128]{1,0:T(8,128)S(1)} %slot_lines.1.own_lines), channel_id=1, source_target_pairs={{0,8},{1,9},{2,10},{3,11},{4,12},{5,13},{6,14},{7,15},{8,0},{9,1},... | collective-permute-start | bytes 24584 | tf_op jit(solution)/shard_map/ppermute | solution.py:407
  12.6 0.0 copy-done.4
  12.6 0.0 copy-done.3
  12.6 0.1 cosine_select_fusion
  12.8 0.0 collective-permute-done.1
  12.8 0.1 collective-permute-start.2
  12.9 1.4 %collective-permute-done.4.other_lines = f32[16,128]{1,0:T(8,128)S(1)} collective-permute-done((f32[16,128]{1,0:T(8,128)S(1)}, f32[16,128]{1,0:T(8,128)S(1)}, u32[]{:S(2)}, u32[]{:S(2)}) %collective-permute-start.4) | collective-permute-done | bytes 8224 | tf_op jit(solution)/shard_map/ppermute | solution.py:407
  14.2 0.0 collective-permute-done.2.other
  14.2 0.0 copy-done
  14.2 2.9 %adjoint.1 = f32[1,128,2048]{2,1,0:T(8,128)} custom-call(f32[200,128]{1,0:T(8,128)S(1)} %add.32.own, f32[200,128]{1,0:T(8,128)S(1)} %collective-permute-done.2.other, f32[16,128]{1,0:T(8,128)S(1)} %slot_lines.1.own_lines, f32[16,128]{1,0:T(8,128)S(1)} %collective-permute-done.4.other_lines, f32[128,128]{1,0:T(8,128)S(1)} %select_maximum_fusion.pupil, ...), custom_call_target="tpu_custom_call" | custom-call | flops 268435456 | bytes 4194304 | tf_op jit(solution)/shard_map/adjoint/pallas_call | solution.py:362
  (6 shorter events, 0.1 us)
Async XLA Ops:
  0.0 12.6 %copy-start.4 = (pred[64,64]{1,0:T(32,128)(4,1)S(1)}, pred[64,64]{1,0:T(32,128)(4,1)}, u32[]{:S(2)}) copy-start(pred[64,64]{1,0:T(32,128)(4,1)} %constant.18.clone) | copy-start | bytes 12292
  0.0 14.2 %copy-start = (bf16[768,256]{1,0:T(8,128)(2,1)S(1)}, bf16[768,256]{1,0:T(8,128)(2,1)}, u32[]{:S(2)}) copy-start(bf16[768,256]{1,0:T(8,128)(2,1)} %constant.19.clone.table) | copy-start | bytes 1179652
  0.0 4.9 %copy-start.5 = (s32[1,8]{1,0:T(1,128)S(1)}, s32[1,8]{1,0:T(1,128)}, u32[]{:S(2)}) copy-start(s32[1,8]{1,0:T(1,128)} %param.18) | copy-start | bytes 100
  0.0 9.1 %copy-start.1 = (s32[12288,2]{0,1:T(2,128)S(1)}, s32[12288,2]{0,1:T(2,128)}, u32[]{:S(2)}) copy-start(s32[12288,2]{0,1:T(2,128)} %param.17) | copy-start | bytes 294916
  0.0 9.2 %copy-start.2 = (f32[12288]{0:T(1024)S(1)}, f32[12288]{0:T(1024)}, u32[]{:S(2)}) copy-start(f32[12288]{0:T(1024)} %param.16) | copy-start | bytes 147460
  0.0 12.6 %copy-start.3 = (f32[64,64]{1,0:T(8,128)S(1)}, f32[64,64]{1,0:T(8,128)}, u32[]{:S(2)}) copy-start(f32[64,64]{1,0:T(8,128)} %param.15) | copy-start | bytes 49156
  3.7 3.9 %collective-permute-start = (f32[200,128]{1,0:T(8,128)S(1)}, f32[200,128]{1,0:T(8,128)S(1)}, u32[]{:S(2)}, u32[]{:S(2)}) collective-permute-start(f32[200,128]{1,0:T(8,128)S(1)} %get-tuple-element.9), channel_id=1, source_target_pairs={{0,1},{1,0},{2,3},{3,2},{4,5},{5,4},{6,7},{7,6},{8,9},{9,8},{10,11... | collective-permute-start | bytes 307208 | tf_op jit(solution)/shard_map/ppermute | solution.py:407
  5.0 4.2 %collective-permute-start.3 = (s32[1,9]{1,0:T(1,128)S(1)}, s32[1,9]{1,0:T(1,128)S(1)}, u32[]{:S(2)}, u32[]{:S(2)}) collective-permute-start(s32[1,9]{1,0:T(1,128)S(1)} %add_add_fusion.1), channel_id=1, source_target_pairs={{0,4},{1,5},{2,6},{3,7},{4,0},{5,1},{6,2},{7,3},{8,12},{9,13},{10,... | collective-permute-start | bytes 116 | tf_op jit(solution)/shard_map/ppermute | solution.py:407
  7.6 5.2 %collective-permute-start.1 = (f32[200,128]{1,0:T(8,128)S(1)}, f32[200,128]{1,0:T(8,128)S(1)}, u32[]{:S(2)}, u32[]{:S(2)}) collective-permute-start(f32[200,128]{1,0:T(8,128)S(1)} %add.31), channel_id=1, source_target_pairs={{0,2},{1,3},{2,0},{3,1},{4,6},{5,7},{6,4},{7,5},{8,10},{9,11},{10,... | collective-permute-start | bytes 307208 | tf_op jit(solution)/shard_map/ppermute | solution.py:407
  9.6 4.6 %collective-permute-start.4 = (f32[16,128]{1,0:T(8,128)S(1)}, f32[16,128]{1,0:T(8,128)S(1)}, u32[]{:S(2)}, u32[]{:S(2)}) collective-permute-start(f32[16,128]{1,0:T(8,128)S(1)} %slot_lines.1.own_lines), channel_id=1, source_target_pairs={{0,8},{1,9},{2,10},{3,11},{4,12},{5,13},{6,14},{7,15},{8,0},{9,1},... | collective-permute-start | bytes 24584 | tf_op jit(solution)/shard_map/ppermute | solution.py:407
  12.8 1.5 %collective-permute-start.2 = (f32[200,128]{1,0:T(8,128)S(1)}, f32[200,128]{1,0:T(8,128)S(1)}, u32[]{:S(2)}, u32[]{:S(2)}) collective-permute-start(f32[200,128]{1,0:T(8,128)S(1)} %add.32.own), channel_id=1, source_target_pairs={{0,1},{1,0},{2,3},{3,2},{4,5},{5,4},{6,7},{7,6},{8,9},{9,8},{10,11... | collective-permute-start | bytes 307208 | tf_op jit(solution)/shard_map/ppermute | solution.py:407
